TPU v7x, 128 devices: a whole 4x4x4 slice. The times are simulated.
128 devices in a mesh: prow: 16 (over x, z), pcol: 8 (over y, core).
Axes of the slice: x: 4, y: 4, z: 4, core: 2. Of those that a mesh axis runs over, the one named last changes fastest.
Arguments:
- matrix: float32 [20480, 20480], P('prow', 'pcol'), may hold values from -56 to 56
Outputs:
- reduced: float32 [20480, 20480], P('prow', 'pcol')
All inputs are finite; a program needn't handle non-finite values.
Results may differ from a plain program's by a relative error of at most 0.000096.
Values sent between devices are 32-bit elements; how exact they have to be, the bound alone decides.
No kernel may reach another device: no remote copies, remote signals or barrier semaphores. Data moves between devices by JAX's collectives and lax.ppermute only.
A program may use at most 128 MiB of HBM per device.

v0:
```python
import jax
import jax.numpy as jnp
from jax import lax
from jax.sharding import PartitionSpec as P

PANEL = 128


def broadcast(value, axis, root):
    mine = lax.axis_index(axis) == root
    return lax.psum(jnp.where(mine, value, jnp.zeros_like(value)), axis)


def to_columns(values, col_index, col_count):
    whole = lax.all_gather(values, "prow", axis=0, tiled=True)
    return lax.dynamic_slice_in_dim(whole, col_index * col_count, col_count, 0)


def on_device(matrix):
    high = lax.Precision.HIGHEST
    row_count = matrix.shape[0]
    col_count = matrix.shape[1]
    row_index = lax.axis_index("prow")
    col_index = lax.axis_index("pcol")
    row_ids = row_index * row_count + jnp.arange(row_count)
    panel = broadcast(matrix[:, :PANEL], "pcol", 0)
    panel = jnp.where(row_ids[:, None] >= PANEL, panel, 0.0)
    top_part = jnp.where(row_index == 0, panel[PANEL : 2 * PANEL], 0.0)
    gram, top_block = lax.psum((jnp.dot(panel.T, panel, precision=high), top_part), "prow")
    lower = jnp.linalg.cholesky(gram)
    basis = jax.scipy.linalg.solve_triangular(lower, panel.T, lower=True).T
    top_basis = jax.scipy.linalg.solve_triangular(lower, top_block.T, lower=True).T
    ident = (row_ids[:, None] - PANEL == jnp.arange(PANEL)[None, :]).astype(jnp.float32)
    vectors = basis - ident
    shifted = jnp.eye(PANEL, dtype=jnp.float32) - top_basis.T
    factor = jnp.linalg.cholesky(jnp.dot(shifted.T, shifted, precision=high))
    coupling = jax.scipy.linalg.cho_solve((factor, True), shifted.T)
    vec_cols = to_columns(vectors, col_index, col_count)
    partial_image = jnp.dot(matrix, vec_cols, precision=high)
    image = lax.psum(partial_image, "pcol")
    inner = lax.psum(jnp.dot(vectors.T, image, precision=high), "prow")
    middle = jnp.dot(jnp.dot(coupling, inner, precision=high), coupling.T, precision=high)
    correction = jnp.dot(image, coupling.T, precision=high) - 0.5 * jnp.dot(
        vectors, middle, precision=high
    )
    corr_cols = to_columns(correction, col_index, col_count)
    left_side = jnp.concatenate([vectors, correction], axis=1)
    right_side = jnp.concatenate([corr_cols, vec_cols], axis=1)
    update = lax.dot_general(left_side, right_side, (((1,), (1,)), ((), ())), precision=high)
    return matrix - update


def solution(mesh):
    return jax.shard_map(
        on_device,
        mesh=mesh,
        in_specs=(P("prow", "pcol"),),
        out_specs=P("prow", "pcol"),
        check_vma=False,
    )
```

profile of v0, /device:TPU:1, one launch (start us, length us, event | category | flops | bytes accessed | tf_op | source)
XLA Modules:
  0.0 561.3 jit_solution(13094698444745556264)
XLA Ops:
  6.5 2.0 slice_select_fusion
  8.6 63.6 %all-reduce.6.cloned.1.call-done = f32[1280,128]{1,0:T(8,128)} async-done(((f32[1280,128]{1,0:T(8,128)}), f32[1280,128]{1,0:T(8,128)}) %all-reduce.6.cloned.1.call-update) | async-done | bytes 655376 | tf_op jit(solution)/shard_map/psum | solution.py:11
  72.2 1.3 broadcast_select_fusion
  73.5 1.8 fusion.23
  75.4 80.8 %all-reduce.8.cloned.1.call-done = f32[128,128]{0,1:T(8,128)} async-done(((f32[128,128]{0,1:T(8,128)}), f32[128,128]{0,1:T(8,128)}) %all-reduce.8.cloned.1.call-update) | async-done | bytes 65552 | tf_op jit(solution)/shard_map/psum | solution.py:29
  156.2 0.9 copy.3
  157.1 0.9 fusion.18
  158.0 11.7 %cholesky.44 = f32[128,128]{1,0:T(8,128)S(1)} custom-call(f32[128,128]{1,0:T(8,128)S(1)} %fusion.18), custom_call_target="Cholesky" | custom-call | tf_op jit(solution)/shard_map/jit(cholesky)/cholesky | solution.py:30
  169.7 0.6 compare_reduce_fusion.1
  170.4 0.7 fusion.7
  171.0 9.8 %custom-call.13 = f32[1,128,128]{1,2,0:T(8,128)S(1)} custom-call(f32[1,128,128]{2,1,0:T(8,128)S(1)} %fusion.7), custom_call_target="InvertDiagBlocksLowerTriangular" | custom-call | tf_op jit(solution)/shard_map/jit(_solve_triangular)/triangular_solve | solution.py:31
  180.8 1.6 convolution_subtract_fusion.1
  182.7 81.3 %all-gather.3.cloned.1.call-done = f32[20480,128]{0,1:T(8,128)} async-done(((f32[1280,128]{0,1:T(8,128)}), f32[20480,128]{0,1:T(8,128)}) %all-gather.3.cloned.1.call-update) | async-done | bytes 10485776 | tf_op jit(solution)/shard_map/all_gather | solution.py:15
  264.0 1.4 constant_dynamic-slice_fusion.1
  265.4 17.3 %convolution_bitcast_fusion = f32[1280,128]{0,1:T(8,128)} fusion(f32[2560,128]{0,1:T(8,128)S(1)} %constant_dynamic-slice_fusion.1, f32[1280,2560]{1,0:T(8,128)} %param.4), kind=kOutput, calls=%fused_computation.7 | convolution fusion | flops 5033164800 | bytes 15073280 | tf_op jit(solution)/shard_map/dot_general | solution.py:39
  282.7 0.6 fusion.9
  283.4 58.3 %all-reduce.10.cloned.1.call-done = f32[1280,128]{0,1:T(8,128)} async-done(((f32[1280,128]{0,1:T(8,128)}), f32[1280,128]{0,1:T(8,128)}) %all-reduce.10.cloned.1.call-update) | async-done | bytes 655376 | tf_op jit(solution)/shard_map/psum | solution.py:40
  341.7 2.5 fusion.26
  344.5 83.2 %all-reduce.12.cloned.1.call-done = (f32[128,128]{0,1:T(8,128)}, f32[128,128]{1,0:T(8,128)}) async-done(((f32[128,128]{0,1:T(8,128)}, f32[128,128]{1,0:T(8,128)}), (f32[128,128]{0,1:T(8,128)}, f32[128,128]{1,0:T(8,128)})) %all-reduce.12.cloned.1.call-update) | async-done | bytes 131088 | tf_op jit(solution)/shard_map/psum | solution.py:29
  427.7 1.1 convolution_subtract_fusion.2
  428.8 0.3 fusion.24
  429.2 11.7 %cholesky.55 = f32[128,128]{1,0:T(8,128)S(1)} custom-call(f32[128,128]{1,0:T(8,128)S(1)} %fusion.15), custom_call_target="Cholesky" | custom-call | tf_op jit(solution)/shard_map/jit(cholesky)/cholesky | solution.py:36
  441.0 0.6 compare_reduce_fusion
  441.6 0.7 fusion.8
  442.3 9.8 %custom-call.14 = f32[1,128,128]{1,2,0:T(8,128)S(1)} custom-call(f32[1,128,128]{2,1,0:T(8,128)S(1)} %fusion.8), custom_call_target="InvertDiagBlocksLowerTriangular" | custom-call | tf_op jit(solution)/shard_map/jit(_cho_solve)/triangular_solve | solution.py:37
  452.1 0.3 fusion.10
  452.6 1.0 fusion.27
  453.9 0.7 fusion.25
  454.6 1.6 fusion.3
  456.2 81.3 %all-gather.5.cloned.1.call-done = f32[20480,128]{0,1:T(8,128)} async-done(((f32[1280,128]{0,1:T(8,128)}), f32[20480,128]{0,1:T(8,128)}) %all-gather.5.cloned.1.call-update) | async-done | bytes 10485776 | tf_op jit(solution)/shard_map/all_gather | solution.py:15
  537.5 1.4 constant_dynamic-slice_fusion
  538.9 15.5 %convolution_subtract_fusion = f32[1280,2560]{1,0:T(8,128)} fusion(f32[1280,2560]{1,0:T(8,128)} %param.4, f32[2560,128]{0,1:T(8,128)S(1)} %constant_dynamic-slice_fusion.1, f32[2560,128]{0,1:T(8,128)S(1)} %constant_dynamic-slice_fusion, f32[1280,128]{0,1:T(8,128)S(1)} %copy-done.1, f32[1280,128]{0,1:T(8,128)S(1)} %copy-done), kind=kOutput, calls=%fused_computation | convolution fusion | flops 10070589440 | bytes 30146560 | tf_op jit(solution)/shard_map/dot_general | solution.py:49
  (26 shorter events, 1.4 us)
Async XLA Ops:
  6.5 65.6 %all-reduce.6.cloned.1.call-start = ((), (), s32[]{:S(2)}) async-start(), calls=%async_computation | async-start | bytes 1310720 | tf_op jit(solution)/shard_map/psum | solution.py:11
  8.5 147.7 %all-reduce.8.cloned.1.call-start = ((), (), s32[]{:S(2)}) async-start(), calls=%async_computation.1 | async-start | bytes 131072 | tf_op jit(solution)/shard_map/psum | solution.py:29
  75.4 188.6 %all-gather.3.cloned.1.call-start = ((), (), s32[]{:S(2)}) async-start(), calls=%async_computation.2 | async-start | bytes 11141120 | tf_op jit(solution)/shard_map/all_gather | solution.py:15
  182.4 159.3 %all-reduce.10.cloned.1.call-start = ((), (), s32[]{:S(2)}) async-start(), calls=%async_computation.3 | async-start | bytes 1310720 | tf_op jit(solution)/shard_map/psum | solution.py:40
  265.4 76.3 %copy-start = (f32[1280,128]{0,1:T(8,128)S(1)}, f32[1280,128]{0,1:T(8,128)}, u32[]{:S(2)}) copy-start(f32[1280,128]{0,1:T(8,128)} %convolution_subtract_fusion.1) | copy-start | bytes 1966084
  282.7 145.0 %all-reduce.12.cloned.1.call-start = ((), (), s32[]{:S(2)}) async-start(), calls=%async_computation.5 | async-start | bytes 262144 | tf_op jit(solution)/shard_map/psum | solution.py:29
  341.7 112.2 %copy-start.2 = (f32[1280,128]{0,1:T(8,128)S(1)}, f32[1280,128]{0,1:T(8,128)}, u32[]{:S(2)}) copy-start(f32[1280,128]{0,1:T(8,128)} %all-reduce.10.cloned.1.call-done) | copy-start | bytes 1966084
  344.2 193.3 %all-gather.5.cloned.1.call-start = ((), (), s32[]{:S(2)}) async-start(), calls=%async_computation.4 | async-start | bytes 11141120 | tf_op jit(solution)/shard_map/all_gather | solution.py:15
  456.2 82.7 %copy-start.1 = (f32[1280,128]{0,1:T(8,128)S(1)}, f32[1280,128]{0,1:T(8,128)}, u32[]{:S(2)}) copy-start(f32[1280,128]{0,1:T(8,128)} %fusion.3) | copy-start | bytes 1966084
Sparse Core Ops, SparseCore 0:
  9.7 62.4 all-reduce.5
  75.5 80.6 all-reduce.7
  182.6 81.3 all-gather.2
  282.8 58.8 all-reduce.9
  345.2 82.4 all-reduce.11
  456.4 81.1 all-gather.4
where the time goes:
time: 562 us; the launch traced here: 561 us
  waiting for transfers between devices  449 us (80%)
  other arithmetic  50.5 us (9%)
  matrix products  44.2 us (8%)
  between operations  13.7 us (2%)
    psum x2, waiting for transfers between devices, on_device(): lax.psum((jnp.dot(panel.T, panel, precision=high), top_part), 'prow')  164 us
    all_gather x2, waiting for transfers between devices, to_columns(): whole = lax.all_gather(values, 'prow', axis=0, tiled=True)  163 us
    psum x1, waiting for transfers between devices, broadcast(): return lax.psum(jnp.where(mine, value, jnp.zeros_like(value)), axis)  63.6 us
    psum x1, waiting for transfers between devices, on_device(): image = lax.psum(partial_image, 'pcol')  58.3 us
    dot_general x1, matrix products, on_device(): partial_image = jnp.dot(matrix, vec_cols, precision=high)  17.3 us
    dot_general x1, matrix products, on_device(): lax.dot_general(left_side, right_side, (((1,), (1,)), ((), ())), precisio...  15.5 us
    another operation x3, other arithmetic, on_device(): factor = jnp.linalg.cholesky(jnp.dot(shifted.T, shifted, precision=high))  12.4 us
    another operation x3, other arithmetic, on_device(): lower = jnp.linalg.cholesky(gram)  12.4 us
  transfers between devices with their start and end apart: 6, of which 6 were waited for; matrix products, arithmetic and copies ran while one was open for 0% of the time, Pallas kernels for 0%

commit v1 on v0

v1 whole, which is shorter than its diff:
```python
import jax
import jax.numpy as jnp
from jax import lax
from jax.experimental import pallas as pl
from jax.experimental.pallas import tpu as pltpu
from jax.sharding import PartitionSpec as P

W = 128
NR = 16
NC = 8
STEP = 256
WIDE = 512
F32 = jnp.float32
BF16 = jnp.bfloat16
SM = pl.BlockSpec(memory_space=pltpu.SMEM)
HB = pl.BlockSpec(memory_space=pltpu.HBM)


def shape(*dims, dtype=F32):
    return jax.ShapeDtypeStruct(dims, dtype)


def exact(a, b, ca, cb):
    return lax.dot_general(
        a, b, (((ca,), (cb,)), ((), ())), precision=lax.Precision.HIGHEST, preferred_element_type=F32
    )


def split(x):
    hi = x.astype(BF16)
    return hi, (x - hi.astype(F32)).astype(BF16)


def bdot(a, b, ca, cb):
    return lax.dot_general(a, b, (((ca,), (cb,)), ((), ())), preferred_element_type=F32)


def three(a, b, ca, cb):
    (ah, al), (bh, bl) = a, b
    return bdot(ah, bh, ca, cb) + (bdot(ah, bl, ca, cb) + bdot(al, bh, ca, cb))


def dot3(a, b, ca, cb):
    return three(split(a), split(b), ca, cb)


def iota2(dims, dim):
    return lax.broadcasted_iota(jnp.int32, dims, dim)


def run(copies):
    for copy in copies:
        copy.start()
    return copies


def wait(copies):
    for copy in copies:
        copy.wait()


def call(kernel, name, flops, args, outs, scratch, sems):
    single = not isinstance(outs, list)
    out_list = [outs] if single else outs
    size = sum(4 * a.size for a in args[1:]) + sum(4 * o.size for o in out_list)

    def body(*refs):
        n = len(args)
        m = n + len(out_list)
        sem = refs[-1]
        used = []

        def copy(src, dst):
            used.append(None)
            return pltpu.make_async_copy(src, dst, sem.at[len(used) - 1])

        kernel(refs[0], refs[1:n], refs[n:m], refs[m:-1], copy)

    result = pl.pallas_call(
        body,
        in_specs=[SM] + [HB] * (len(args) - 1),
        out_specs=[HB] * len(out_list),
        out_shape=out_list,
        scratch_shapes=[pltpu.VMEM(s.shape, s.dtype) for s in scratch] + [pltpu.SemaphoreType.DMA((sems,))],
        compiler_params=pltpu.CompilerParams(vmem_limit_bytes=60 * 1024 * 1024),
        cost_estimate=pl.CostEstimate(flops=int(flops), bytes_accessed=int(size), transcendentals=0),
        name=name,
    )(*args)
    return result[0] if single else result


def load_panel(rc, held, other, buf, copy):
    half = held.shape[0]
    at = pl.multiple_of(rc[2], half)
    return run([copy(held, buf.at[pl.ds(at, half)]), copy(other, buf.at[pl.ds(half - at, half)])])


def clear_top(rc, buf):
    @pl.when(rc[0] == 0)
    def _():
        buf[:W] = jnp.zeros((W, W), F32)


def gram_kernel(rc, ins, outs, bufs, copy):
    buf, out = bufs
    wait(load_panel(rc, ins[0], ins[1], buf, copy))
    clear_top(rc, buf)
    p = split(buf[...])
    g = three(p, p, 0, 0).reshape(NR, 8, W)
    t = jnp.where(rc[0] == 0, buf[W : 2 * W], 0.0).reshape(NR, 8, W)
    out[...] = jnp.concatenate([g, t], 1)
    wait(run([copy(out, outs[0])]))


def lane(x, k):
    return jnp.broadcast_to(x[:, k : k + 1], (8, W))


def row(x, k):
    return jnp.broadcast_to(x[k : k + 1], (8, W))


def eliminate(g, tiles_out):
    lanes = iota2((8, W), 1)
    subs = iota2((8, W), 0)
    tiles = [g[8 * t : 8 * t + 8] for t in range(W // 8)]
    for k in range(0, W, 2):
        t0, o = k // 8, k % 8
        top = tiles[t0]
        at0, at1 = lanes == k, lanes == k + 1
        both = at0 | at1
        c0, c1 = lane(top, k), lane(top, k + 1)
        a, b, d = row(c0, o), row(c1, o), row(c1, o + 1)
        r0 = jnp.where(at1, 0.0, jnp.where(at0, 1.0, row(top, o)))
        r1 = jnp.where(at0, 0.0, jnp.where(at1, 1.0, row(top, o + 1)))
        ia = 1.0 / a
        ba = b * ia
        n1 = r1 - ba * r0
        s = d - b * ba
        q1 = n1 * (1.0 / s)
        q0 = r0 * ia - ba * q1
        for t in range(t0, W // 8):
            m = tiles[t]
            if t > t0:
                tiles[t] = jnp.where(both, 0.0, m) - lane(m, k) * q0 - lane(m, k + 1) * q1
            elif o < 6:
                tiles[t] = jnp.where(subs > o + 1, jnp.where(both, 0.0, m) - c0 * q0 - c1 * q1, m)
        if o == 0:
            final = jnp.zeros((8, W), F32)
        final = jnp.where(subs == o, r0 * lax.rsqrt(a), jnp.where(subs == o + 1, n1 * lax.rsqrt(s), final))
        if o == 6:
            tiles_out.append(final)
        yield


def lower_part(tiles):
    i, j = iota2((W, W), 0), iota2((W, W), 1)
    return jnp.where(i >= j, jnp.concatenate(tiles, 0), 0.0)


def inverse_factor(g):
    tiles = []
    for _ in eliminate(g, tiles):
        pass
    return lower_part(tiles)


def first_kernel(rc, ins, outs, bufs, copy):
    a_ref, held, other, small = ins
    buf, panel, acc, rows_out, msg, linv = bufs
    rows, cols = buf.shape
    n = rows // STEP
    get = run([copy(small, msg)])
    first = load_panel(rc, held, other, panel, copy)
    copies = run([copy(a_ref.at[pl.ds(k * STEP, STEP)], buf.at[pl.ds(k * STEP, STEP)]) for k in range(n)])
    wait(get)
    gram = msg[:, :8].reshape(W, W)
    tiles = []
    steps = eliminate(gram, tiles)
    wait(first)
    clear_top(rc, panel)
    ph, plow = split(panel[...])
    both = jnp.concatenate([ph, plow], 1)
    blocks = cols // WIDE
    each = -(-W // (2 * n * blocks))
    for k in range(n):
        copies[k].wait()
        lo, up = k * STEP, (k + 1) * STEP
        for b in range(blocks):
            for _ in range(each):
                next(steps, None)
            sl = slice(b * WIDE, (b + 1) * WIDE)
            ah, al = split(buf[lo:up, sl])
            x = bdot(both[lo:up], ah, 0, 0)
            x = x[:W] + (x[W:] + bdot(ph[lo:up], al, 0, 0))
            if k == 0:
                acc[:, sl] = x
            else:
                acc[:, sl] += x
    for _ in steps:
        pass
    inverse = lower_part(tiles)
    linv[...] = inverse
    sent = run([copy(linv, outs[1])])

    @pl.when(rc[0] == 0)
    def _():
        ls = split(exact(gram, inverse, 1, 1))
        for b in range(blocks):
            sl = slice(b * WIDE, (b + 1) * WIDE)
            acc[:, sl] -= three(ls, split(buf[W : 2 * W, sl]), 1, 0)

    for b in range(blocks):
        sl = slice(b * WIDE, (b + 1) * WIDE)
        rows_out[sl] = acc[:, sl].T
    piece = outs[0].shape[1]
    wait(sent + run([copy(rows_out.at[pl.ds(k * piece, piece)], outs[0].at[k]) for k in range(NR)]))


def coupling_kernel(rc, ins, outs, bufs, copy):
    msg, linv, out = bufs
    wait(run([copy(ins[0], msg), copy(ins[1], linv)]))
    i, j = iota2((W, W), 0), iota2((W, W), 1)
    shifted = jnp.where(i == j, 1.0, 0.0) - exact(linv[...], msg[:, 8:].reshape(W, W), 1, 1)
    finv = inverse_factor(exact(shifted, shifted, 0, 0))
    out[...] = exact(finv, exact(finv, shifted, 1, 1), 0, 0)
    wait(run([copy(out, outs[0])]))


def piece_kernel(rc, ins, outs, bufs, copy):
    msg, linv, out = bufs
    wait(run([copy(ins[0], msg), copy(ins[1], linv)]))
    out[...] = dot3(jnp.sum(msg[...], 0), linv[...], 1, 1)
    wait(run([copy(out, outs[0].at[k]) for k in range(NR)] + [copy(out, outs[1])]))


def vectors_kernel(rc, ins, outs, bufs, copy):
    p, linv, v = bufs
    cols = p.shape[0]
    wait(run([copy(ins[0], p), copy(ins[1], linv)]))
    ls = split(linv[...])
    for b in range(cols // WIDE):
        sl = slice(b * WIDE, (b + 1) * WIDE)
        at = iota2((W, WIDE), 1) + (rc[1] * cols + b * WIDE - W)
        x = three(ls, split(p[sl]), 1, 1)
        x = jnp.where(at < 0, 0.0, x) - jnp.where(at == iota2((W, WIDE), 0), 1.0, 0.0)
        v[0, :, sl], v[1, :, sl] = split(x)
    wait(run([copy(v, outs[0])]))


def inner_kernel(rc, ins, outs, bufs, copy):
    v, y, out = bufs
    wait(run([copy(ins[0], v), copy(ins[1], y)]))
    out[...] = three((v[0], v[1]), split(y[...].reshape(v.shape[2], W)), 1, 0)
    wait(run([copy(out, outs[0].at[k]) for k in range(NC)]))


def sides_kernel(rc, ins, outs, bufs, copy):
    held, other, y_r, y_c, linv_ref, coup_ref = ins
    panel, yr, yc, linv, coup, left, wide = bufs
    rows, cols = panel.shape[0], wide.shape[1]
    small = run([copy(linv_ref, linv), copy(coup_ref, coup), copy(y_c, yc)])
    more = load_panel(rc, held, other, panel, copy) + run([copy(y_r, yr)])
    wait(small)
    ls, cs = split(linv[...]), split(coup[...])
    flat = yc.reshape(cols, W)
    for b in range(cols // WIDE):
        sl = slice(b * WIDE, (b + 1) * WIDE)
        wide[:, sl] = three(cs, split(flat[sl]), 1, 1)
    last = run([copy(wide, outs[1])])
    wait(more)
    clear_top(rc, panel)
    for k in range(rows // STEP):
        sl = slice(k * STEP, (k + 1) * STEP)
        ids = rc[0] * rows + k * STEP + iota2((STEP, W), 0)
        v = three(split(panel[sl]), ls, 1, 1) - jnp.where(ids - W == iota2((STEP, W), 1), 1.0, 0.0)
        left[0, sl, :W], left[1, sl, :W] = split(v)
        left[0, sl, W:], left[1, sl, W:] = split(three(split(yr[sl]), cs, 1, 1))
    wait(last + run([copy(left, outs[0])]))


def last_kernel(rc, ins, outs, bufs, copy):
    a_ref, s_ref, coup_ref, left_ref, wide_ref, v_ref = ins
    buf, s, coup, left, wide, right = bufs
    rows, cols = buf.shape
    n = rows // STEP
    small = run([copy(s_ref, s), copy(coup_ref, coup)])
    mid = run([copy(v_ref, right.at[:, pl.ds(W, W)]), copy(wide_ref, wide)])
    copies = run([copy(a_ref.at[pl.ds(0, STEP)], buf.at[pl.ds(0, STEP)])])
    lefts = run([copy(left_ref, left)])
    copies += run([copy(a_ref.at[pl.ds(k * STEP, STEP)], buf.at[pl.ds(k * STEP, STEP)]) for k in range(1, n)])
    wait(small)
    c = coup[...]
    middle = exact(exact(c, jnp.sum(s[...], 0), 1, 0), c, 1, 1)
    ms = split(0.5 * (middle + middle.T))
    wait(mid)
    for b in range(cols // WIDE):
        sl = slice(b * WIDE, (b + 1) * WIDE)
        w = wide[:, sl] - three(ms, (right[0, W:, sl], right[1, W:, sl]), 1, 0)
        right[0, :W, sl], right[1, :W, sl] = split(w)
    wait(lefts)
    ends = []
    for k in range(n):
        copies[k].wait()
        lo = k * STEP
        lh = (left[0, lo : lo + STEP], left[1, lo : lo + STEP])
        for b in range(cols // WIDE):
            sl = slice(b * WIDE, (b + 1) * WIDE)
            buf[lo : lo + STEP, sl] -= three(lh, (right[0, :, sl], right[1, :, sl]), 1, 0)
        ends += run([copy(buf.at[pl.ds(lo, STEP)], outs[0].at[pl.ds(lo, STEP)])])
    wait(ends)


def spread(x, n):
    return jnp.broadcast_to(x[None], (n,) + x.shape)


def on_device(matrix):
    rows, cols = matrix.shape
    piece = cols // NR
    half = rows // 2
    r = lax.axis_index("prow")
    c = lax.axis_index("pcol")
    axes = ("prow", "pcol")
    holds_top = (c == 0) | (c == 2) | (c == 4) | (c == 7)
    rc = jnp.stack([r, c, jnp.where(holds_top, 0, half)])
    big = 6 * rows * cols * W

    top, bot = matrix[:half, :W], matrix[half:, :W]
    to1 = lax.ppermute(bot, "pcol", [(0, 1)])
    to2 = lax.ppermute(top, "pcol", [(0, 2)])
    to6 = lax.ppermute(bot, "pcol", [(0, 6)])
    send = jnp.where(c == 0, top, jnp.where(c == 1, to1, jnp.where(c == 2, to2, to6)))
    got = lax.ppermute(send, "pcol", [(0, 7), (1, 3), (2, 4), (6, 5)])
    held = jnp.where((c == 0) | (c == 1) | (c == 2) | (c == 6), send, got)
    other = lax.ppermute(held, "pcol", [(i, i ^ 1) for i in range(NC)])
    owner = [(8 * ((g // NC) % 2) + g % NC) * NC + (g // NC) // 2 for g in range(NR * NC)]
    at = (c % (NC // 2)) * piece
    mine = jnp.where(
        (c < NC // 2) == holds_top,
        lax.dynamic_slice_in_dim(held, at, piece, 0),
        lax.dynamic_slice_in_dim(other, at, piece, 0),
    )
    panel_q = lax.ppermute(mine, axes, list(enumerate(owner)))
    panel_c = lax.all_gather(panel_q, "prow", axis=0, tiled=True)

    half_bufs = [shape(rows, W)]
    small = call(gram_kernel, "gram", 6 * rows * W * W, (rc, held, other), shape(NR, 16, W), half_bufs + [shape(NR, 16, W)], 3)
    small = lax.all_to_all(small, "prow", 0, 0, tiled=True)
    small = spread(jnp.sum(small, 0), NR)
    small = lax.all_to_all(small, "prow", 0, 0, tiled=True)
    msg, linv = call(
        first_kernel,
        "first_pass",
        big,
        (rc, matrix, held, other, small),
        [shape(NR, piece, W), shape(W, W)],
        [shape(rows, cols), shape(rows, W), shape(W, cols), shape(cols, W), shape(NR, 16, W), shape(W, W)],
        4 + rows // STEP + NR,
    )
    msg = lax.all_to_all(msg, "prow", 0, 0, tiled=True)
    coup = call(
        coupling_kernel, "coupling", 8e9, (rc, small, linv), shape(W, W), [shape(NR, 16, W), shape(W, W), shape(W, W)], 3
    )
    msg, coup, panel_c = lax.optimization_barrier((msg, coup, panel_c))
    msg, y_q = call(
        piece_kernel,
        "piece_image",
        msg.size,
        (rc, msg, linv),
        [shape(NR, piece, W), shape(piece, W)],
        [shape(NR, piece, W), shape(W, W), shape(piece, W)],
        2 + NR + 1,
    )
    y_p = lax.ppermute(y_q, axes, [(b, a) for a, b in enumerate(owner)])
    msg = lax.all_to_all(msg, "prow", 0, 0, tiled=True)
    vt = call(
        vectors_kernel,
        "vectors",
        6 * cols * W * W,
        (rc, panel_c, linv),
        shape(2, W, cols, dtype=BF16),
        [shape(cols, W), shape(W, W), shape(2, W, cols, dtype=BF16)],
        3,
    )
    y_r = lax.all_to_all(spread(y_p, NC), "pcol", 0, 0, tiled=True).reshape(rows, W)
    s = call(
        inner_kernel,
        "inner",
        6 * cols * W * W,
        (rc, vt, msg),
        shape(NC, W, W),
        [shape(2, W, cols, dtype=BF16), shape(NR, piece, W), shape(W, W)],
        2 + NC,
    )
    s = lax.all_to_all(s, "pcol", 0, 0, tiled=True)
    left, wide = call(
        sides_kernel,
        "sides",
        12 * (rows + cols) * W * W,
        (rc, held, other, y_r, msg, linv, coup),
        [shape(2, rows, 2 * W, dtype=BF16), shape(W, cols)],
        [
            shape(rows, W),
            shape(rows, W),
            shape(NR, piece, W),
            shape(W, W),
            shape(W, W),
            shape(2, rows, 2 * W, dtype=BF16),
            shape(W, cols),
        ],
        8,
    )
    return call(
        last_kernel,
        "last_pass",
        2 * big,
        (rc, matrix, s, coup, left, wide, vt),
        shape(rows, cols),
        [
            shape(rows, cols),
            shape(NC, W, W),
            shape(W, W),
            shape(2, rows, 2 * W, dtype=BF16),
            shape(W, cols),
            shape(2, 2 * W, cols, dtype=BF16),
        ],
        5 + 2 * (rows // STEP),
    )


def solution(mesh):
    return jax.shard_map(
        on_device, mesh=mesh, in_specs=(P("prow", "pcol"),), out_specs=P("prow", "pcol"), check_vma=False
    )
```

time: 562 us -> 188 us (0.33)
  waiting for transfers between devices: 449 us -> 32.5 us
  Pallas kernels: 0 us -> 59.8 us
  other arithmetic: 50.5 us -> 1.68 us
  matrix products: 44.2 us -> 0 us
  starting transfers between devices: 0.61 us -> 44.3 us
  blocking collectives: 0 us -> 29 us
    psum x4 -> x0, waiting for transfers between devices: 286 us -> none  [the longest x2 164 us: on_device(): lax.psum((jnp.dot(panel.T, panel, precision=high), top_part), 'prow')]
    all_gather x2 -> x1, waiting for transfers between devices: 163 us -> 0.01 us  [on_device(): panel_c = lax.all_gather(panel_q, 'prow', axis=0, tiled=True)]
    pallas_call x0 -> x8, Pallas kernels: none -> 59.8 us  [call(): pl.pallas_call(body, in_specs=[SM] + [HB] * (len(args) - 1), out_specs=[H...]
    another operation x10 -> x1, other arithmetic: 45.7 us -> 0.58 us  [on_device(): rc = jnp.stack([r, c, jnp.where(holds_top, 0, half)])]
    dot_general x9 -> x0, matrix products: 41 us -> none  [the longest x1 17.3 us: on_device(): partial_image = jnp.dot(matrix, vec_cols, precision=high)]
    all_to_all x0 -> x2, blocking collectives: none -> 29 us  [on_device(): small = lax.all_to_all(small, 'prow', 0, 0, tiled=True)]
    all_to_all x0 -> x4, starting transfers between devices: none -> 23.4 us  [the longest x1 11.4 us: on_device(): lax.all_to_all(spread(y_p, NC), 'pcol', 0, 0, tiled=True).reshape(rows, W)]
    ppermute x0 -> x7, waiting for transfers between devices: none -> 21.9 us  [the longest x1 6.83 us: on_device(): to1 = lax.ppermute(bot, 'pcol', [(0, 1)])]
  transfers between devices with their start and end apart: 6 -> 12, of which waited for: 6 -> 8; matrix products, arithmetic and copies ran while one was open for 0% -> 0% of each run, Pallas kernels for 0% -> 24%
where the time goes in v1:
time: 188 us; the launch traced here: 186 us
  Pallas kernels  59.8 us (32%)
  starting transfers between devices  44.3 us (24%)
  waiting for transfers between devices  32.5 us (17%)
  blocking collectives  29 us (15%)
  between operations  13.7 us (7%)
  local copies, waits for them, and re-layouts  4.61 us (2%)
    pallas_call x8, Pallas kernels, call(): pl.pallas_call(body, in_specs=[SM] + [HB] * (len(args) - 1), out_specs=[H...  59.8 us
    all_to_all x2, blocking collectives, on_device(): small = lax.all_to_all(small, 'prow', 0, 0, tiled=True)  29 us
    all_to_all x1, starting transfers between devices, on_device(): lax.all_to_all(spread(y_p, NC), 'pcol', 0, 0, tiled=True).reshape(rows, W)  11.4 us
    ppermute x1, starting transfers between devices, on_device(): y_p = lax.ppermute(y_q, axes, [(b, a) for a, b in enumerate(owner)])  10.4 us
    all_to_all x2, starting transfers between devices, on_device(): msg = lax.all_to_all(msg, 'prow', 0, 0, tiled=True)  7.74 us
    ppermute x1, waiting for transfers between devices, on_device(): to1 = lax.ppermute(bot, 'pcol', [(0, 1)])  6.83 us
    ppermute x1, waiting for transfers between devices, on_device(): y_p = lax.ppermute(y_q, axes, [(b, a) for a, b in enumerate(owner)])  5.78 us
    all_to_all x1, waiting for transfers between devices, on_device(): s = lax.all_to_all(s, 'pcol', 0, 0, tiled=True)  4.67 us
  transfers between devices with their start and end apart: 12, of which 8 were waited for; matrix products, arithmetic and copies ran while one was open for 0% of the time, Pallas kernels for 24%

profile of v1, /device:TPU:1, one launch (start us, length us, event | category | flops | bytes accessed | tf_op | source)
XLA Modules:
  0.0 185.5 jit_solution(15562957217346619437)
XLA Ops:
  6.5 1.1 fusion
  9.0 1.3 collective-permute-start
  10.4 6.8 %collective-permute-done = f32[640,128]{1,0:T(8,128)S(1)} collective-permute-done((f32[640,128]{1,0:T(8,128)S(1)}, f32[640,128]{1,0:T(8,128)S(1)}, u32[]{:S(2)}, u32[]{:S(2)}) %collective-permute-start) | collective-permute-done | bytes 327712 | tf_op jit(solution)/shard_map/ppermute | solution.py:330
  17.2 1.0 select_select_fusion
  18.2 1.3 collective-permute-start.3
  19.6 4.0 %collective-permute-done.3 = f32[640,128]{1,0:T(8,128)S(1)} collective-permute-done((f32[640,128]{1,0:T(8,128)S(1)}, f32[640,128]{1,0:T(8,128)S(1)}, u32[]{:S(2)}, u32[]{:S(2)}) %collective-permute-start.3) | collective-permute-done | bytes 327712 | tf_op jit(solution)/shard_map/ppermute | solution.py:334
  23.6 2.8 %collective-permute-start.4 = (f32[640,128]{1,0:T(8,128)S(1)}, f32[640,128]{1,0:T(8,128)S(1)}, u32[]{:S(2)}, u32[]{:S(2)}) collective-permute-start(f32[640,128]{1,0:T(8,128)S(1)} %broadcast_select_fusion.refs_1_.refs_2_), channel_id=1, source_target_pairs={{0,1},{1,0},{2,3},{3,2},{4,5},{5,4},{6,7},{7,6},{8,9},{9,8},{10,11... | collective-permute-start | bytes 983048 | tf_op jit(solution)/shard_map/ppermute | solution.py:336
  26.4 1.3 collective-permute-done.4.refs_2_.refs_3_
  27.7 3.8 %collective-permute-start.5 = (f32[160,128]{1,0:T(8,128)S(1)}, f32[160,128]{1,0:T(8,128)S(1)}, u32[]{:S(2)}, u32[]{:S(2)}) collective-permute-start(f32[160,128]{1,0:T(8,128)S(1)} %dynamic-slice_select_fusion), channel_id=1, source_target_pairs={{0,0},{1,8},{2,16},{3,24},{4,32},{5,40},{6,48},{7,56},{8,64},{9,72... | collective-permute-start | bytes 245768 | tf_op jit(solution)/shard_map/ppermute | solution.py:344
  31.5 4.1 %collective-permute-done.5 = f32[160,128]{1,0:T(8,128)S(1)} collective-permute-done((f32[160,128]{1,0:T(8,128)S(1)}, f32[160,128]{1,0:T(8,128)S(1)}, u32[]{:S(2)}, u32[]{:S(2)}) %collective-permute-start.5) | collective-permute-done | bytes 81952 | tf_op jit(solution)/shard_map/ppermute | solution.py:344
  36.8 2.9 %gram.1 = f32[16,16,128]{2,1,0:T(8,128)} custom-call(s32[3]{0:T(128)} %pad_add_fusion.refs_0_, f32[640,128]{1,0:T(8,128)} %copy-done.2, f32[640,128]{1,0:T(8,128)} %copy-done.4), custom_call_target="tpu_custom_call" | custom-call | flops 125829120 | bytes 786432 | tf_op jit(solution)/shard_map/gram/pallas_call | solution.py:79
  39.7 18.8 %all_to_all.30 = f32[16,16,128]{2,1,0:T(8,128)S(1)} all-to-all(f32[16,16,128]{2,1,0:T(8,128)} %gram.1), channel_id=1, replica_groups=mesh['prow'=16,'pcol'=8] {'prow'}, dimensions={0} | all-to-all | bytes 262144 | tf_op jit(solution)/shard_map/all_to_all | solution.py:349
  58.5 10.2 %all_to_all.31.refs_4_.refs_1_ = f32[16,16,128]{2,1,0:T(8,128)} all-to-all(f32[16,16,128]{2,1,0:T(8,128)S(1)} %broadcast_in_dim.4), channel_id=1, replica_groups=mesh['prow'=16,'pcol'=8] {'prow'}, dimensions={0} | all-to-all | bytes 262144 | tf_op jit(solution)/shard_map/all_to_all | solution.py:351
  68.7 15.5 %first_pass.1 = (f32[16,160,128]{2,1,0:T(8,128)}, f32[128,128]{1,0:T(8,128)}) custom-call(s32[3]{0:T(128)} %pad_add_fusion.refs_0_, f32[1280,2560]{1,0:T(8,128)} %refs_1_.3, f32[640,128]{1,0:T(8,128)} %copy-done.2, f32[640,128]{1,0:T(8,128)} %copy-done.4, f32[16,16,128]{2,1,0:T(8,128)} %all_to_all.31.refs_4_.refs_1_), custom_call_target="tpu_custom_call" | custom-call | flops 2516582400 | bytes 15269888 | tf_op jit(solution)/shard_map/first_pass/pallas_call | solution.py:79
  84.3 3.9 %all-to-all-start.2 = ((f32[16,160,128]{2,1,0:T(8,128)}), f32[16,160,128]{2,1,0:T(8,128)S(1)}, u32[]{:S(2)}, u32[]{:S(2)}) async-start(f32[16,160,128]{2,1,0:T(8,128)} %get-tuple-element.14), calls=%async_computation.2 | async-start | bytes 2621440 | tf_op jit(solution)/shard_map/all_to_all | solution.py:361
  88.2 13.2 %coupling.1.refs_6_.refs_3_ = f32[128,128]{1,0:T(8,128)} custom-call(s32[3]{0:T(128)} %pad_add_fusion.refs_0_, f32[16,16,128]{2,1,0:T(8,128)} %all_to_all.31.refs_4_.refs_1_, f32[128,128]{1,0:T(8,128)} %get-tuple-element.15.refs_2_.refs_5_), custom_call_target="tpu_custom_call" | custom-call | flops 8000000000 | bytes 262144 | tf_op jit(solution)/shard_map/coupling/pallas_call | solution.py:79
  101.4 2.8 %all-to-all-done.2.refs_1_ = f32[16,160,128]{2,1,0:T(8,128)S(1)} async-done(((f32[16,160,128]{2,1,0:T(8,128)}), f32[16,160,128]{2,1,0:T(8,128)S(1)}, u32[]{:S(2)}, u32[]{:S(2)}) %all-to-all-start.2) | async-done | bytes 1310752 | tf_op jit(solution)/shard_map/all_to_all | solution.py:361
  104.2 1.1 copy-done.1
  105.2 3.5 %piece_image.1 = (f32[16,160,128]{2,1,0:T(8,128)}, f32[160,128]{1,0:T(8,128)}) custom-call(s32[3]{0:T(128)} %pad_add_fusion.refs_0_, f32[16,160,128]{2,1,0:T(8,128)} %copy-done.1, f32[128,128]{1,0:T(8,128)} %get-tuple-element.15.refs_2_.refs_5_), custom_call_target="tpu_custom_call" | custom-call | flops 327680 | bytes 2768896 | tf_op jit(solution)/shard_map/piece_image/pallas_call | solution.py:79
  108.7 3.8 %all-to-all-start.3 = ((f32[16,160,128]{2,1,0:T(8,128)}), f32[16,160,128]{2,1,0:T(8,128)S(1)}, u32[]{:S(2)}, u32[]{:S(2)}) async-start(f32[16,160,128]{2,1,0:T(8,128)} %get-tuple-element.18), calls=%async_computation.3 | async-start | bytes 2621440 | tf_op jit(solution)/shard_map/all_to_all | solution.py:376
  112.6 10.4 %collective-permute-start.6 = (f32[160,128]{1,0:T(8,128)S(1)}, f32[160,128]{1,0:T(8,128)S(1)}, u32[]{:S(2)}, u32[]{:S(2)}) collective-permute-start(f32[160,128]{1,0:T(8,128)S(1)} %copy-done.7), channel_id=1, source_target_pairs={{0,0},{8,1},{16,2},{24,3},{32,4},{40,5},{48,6},{56,7},{64,8},{72,9... | collective-permute-start | bytes 245768 | tf_op jit(solution)/shard_map/ppermute | solution.py:375
  122.9 5.8 %collective-permute-done.6 = f32[160,128]{1,0:T(8,128)S(1)} collective-permute-done((f32[160,128]{1,0:T(8,128)S(1)}, f32[160,128]{1,0:T(8,128)S(1)}, u32[]{:S(2)}, u32[]{:S(2)}) %collective-permute-start.6) | collective-permute-done | bytes 81952 | tf_op jit(solution)/shard_map/ppermute | solution.py:375
  128.7 1.0 broadcast_in_dim.5
  129.7 11.4 %all-to-all-start.5 = ((f32[8,160,128]{2,1,0:T(8,128)}), f32[8,160,128]{2,1,0:T(8,128)S(1)}, u32[]{:S(2)}, u32[]{:S(2)}) async-start(f32[8,160,128]{2,1,0:T(8,128)} %broadcast_in_dim.5), calls=%async_computation.5 | async-start | bytes 1310720 | tf_op jit(solution)/shard_map/all_to_all | solution.py:386
  141.1 3.8 %vectors.1.refs_1_.refs_6_ = bf16[2,128,2560]{2,1,0:T(8,128)(2,1)} custom-call(s32[3]{0:T(128)} %pad_add_fusion.refs_0_, f32[2560,128]{1,0:T(8,128)} %all-gather.2.cloned.1.call-done.refs_1_, f32[128,128]{1,0:T(8,128)} %get-tuple-element.15.refs_2_.refs_5_), custom_call_target="tpu_custom_call" | custom-call | flops 251658240 | bytes 3997696 | tf_op jit(solution)/shard_map/vectors/pallas_call | solution.py:79
  144.9 3.9 %inner.1 = f32[8,128,128]{2,1,0:T(8,128)} custom-call(s32[3]{0:T(128)} %pad_add_fusion.refs_0_, bf16[2,128,2560]{2,1,0:T(8,128)(2,1)} %vectors.1.refs_1_.refs_6_, f32[16,160,128]{2,1,0:T(8,128)} %copy-done), custom_call_target="tpu_custom_call" | custom-call | flops 251658240 | bytes 4456448 | tf_op jit(solution)/shard_map/inner/pallas_call | solution.py:79
  148.8 3.1 %all-to-all-done.5 = f32[8,160,128]{2,1,0:T(8,128)S(1)} async-done(((f32[8,160,128]{2,1,0:T(8,128)}), f32[8,160,128]{2,1,0:T(8,128)S(1)}, u32[]{:S(2)}, u32[]{:S(2)}) %all-to-all-start.5) | async-done | bytes 655392 | tf_op jit(solution)/shard_map/all_to_all | solution.py:386
  152.0 4.3 %all-to-all-start.4 = ((f32[8,128,128]{2,1,0:T(8,128)}), f32[8,128,128]{2,1,0:T(8,128)S(1)}, u32[]{:S(2)}, u32[]{:S(2)}) async-start(f32[8,128,128]{2,1,0:T(8,128)} %inner.1), calls=%async_computation.4 | async-start | bytes 1048576 | tf_op jit(solution)/shard_map/all_to_all | solution.py:396
  156.2 4.8 %sides.1 = (bf16[2,1280,256]{2,1,0:T(8,128)(2,1)}, f32[128,2560]{1,0:T(8,128)}) custom-call(s32[3]{0:T(128)} %pad_add_fusion.refs_0_, f32[640,128]{1,0:T(8,128)} %copy-done.2, f32[640,128]{1,0:T(8,128)} %copy-done.4, f32[1280,128]{1,0:T(8,128)} %bitcast.4, f32[16,160,128]{2,1,0:T(8,128)} %copy-done, f32[128,128]{1,0:T(8,128)} %get-tuple-element.15.refs_2_.refs_5_, ...), custom_call_target="tpu_custom_call" | custom-call | flops 754974720 | bytes 6684672 | tf_op jit(solution)/shard_map/sides/pallas_call | solution.py:79
  161.1 4.7 %all-to-all-done.4.refs_2_ = f32[8,128,128]{2,1,0:T(8,128)S(1)} async-done(((f32[8,128,128]{2,1,0:T(8,128)}), f32[8,128,128]{2,1,0:T(8,128)S(1)}, u32[]{:S(2)}, u32[]{:S(2)}) %all-to-all-start.4) | async-done | bytes 524320 | tf_op jit(solution)/shard_map/all_to_all | solution.py:396
  165.7 0.8 copy-done.3
  166.5 12.1 %last_pass.1 = f32[1280,2560]{1,0:T(8,128)} custom-call(s32[3]{0:T(128)} %pad_add_fusion.refs_0_, f32[1280,2560]{1,0:T(8,128)} %refs_1_.3, f32[8,128,128]{2,1,0:T(8,128)} %copy-done.3, f32[128,128]{1,0:T(8,128)} %coupling.1.refs_6_.refs_3_, bf16[2,1280,256]{2,1,0:T(8,128)(2,1)} %get-tuple-element.21.refs_4_, f32[128,2560]{1,0:T(8,128)} %get-tuple-element.22.refs_5_, ...), custom_call_target="tpu_custom_call" | custom-call | flops 5033164800 | bytes 33357824 | tf_op jit(solution)/shard_map/last_pass/pallas_call | solution.py:79
  (27 shorter events, 2.7 us)
Async XLA Ops:
  6.5 97.6 %all-gather.2.cloned.1.call-start = ((), (), s32[]{:S(2)}) async-start(), calls=%async_computation.6 | async-start | bytes 1392640 | tf_op jit(solution)/shard_map/all_gather | solution.py:345
  7.7 2.7 %collective-permute-start.1 = (f32[640,128]{1,0:T(8,128)S(1)}, f32[640,128]{1,0:T(8,128)S(1)}, u32[]{:S(2)}, u32[]{:S(2)}) collective-permute-start(f32[640,128]{1,0:T(8,128)S(1)} %get-tuple-element.23), channel_id=1, source_target_pairs={{0,2},{8,10},{16,18},{24,26},{32,34},{40,42},{48,50},{56,58},{64,6... | collective-permute-start | bytes 983048 | tf_op jit(solution)/shard_map/ppermute | solution.py:331
  8.3 2.0 %collective-permute-start.2 = (f32[640,128]{1,0:T(8,128)S(1)}, f32[640,128]{1,0:T(8,128)S(1)}, u32[]{:S(2)}, u32[]{:S(2)}) collective-permute-start(f32[640,128]{1,0:T(8,128)S(1)} %get-tuple-element.24), channel_id=1, source_target_pairs={{0,6},{8,14},{16,22},{24,30},{32,38},{40,46},{48,54},{56,62},{64,7... | collective-permute-start | bytes 983048 | tf_op jit(solution)/shard_map/ppermute | solution.py:332
  9.0 8.2 %collective-permute-start = (f32[640,128]{1,0:T(8,128)S(1)}, f32[640,128]{1,0:T(8,128)S(1)}, u32[]{:S(2)}, u32[]{:S(2)}) collective-permute-start(f32[640,128]{1,0:T(8,128)S(1)} %get-tuple-element.24), channel_id=1, source_target_pairs={{0,1},{8,9},{16,17},{24,25},{32,33},{40,41},{48,49},{56,57},{64,65... | collective-permute-start | bytes 983048 | tf_op jit(solution)/shard_map/ppermute | solution.py:330
  18.2 5.3 %collective-permute-start.3 = (f32[640,128]{1,0:T(8,128)S(1)}, f32[640,128]{1,0:T(8,128)S(1)}, u32[]{:S(2)}, u32[]{:S(2)}) collective-permute-start(f32[640,128]{1,0:T(8,128)S(1)} %select_select_fusion), channel_id=1, source_target_pairs={{0,7},{1,3},{2,4},{6,5},{8,15},{9,11},{10,12},{14,13},{16,23},{17,... | collective-permute-start | bytes 983048 | tf_op jit(solution)/shard_map/ppermute | solution.py:334
  23.6 13.2 %copy-start.2 = (f32[640,128]{1,0:T(8,128)}, f32[640,128]{1,0:T(8,128)S(1)}, u32[]{:S(2)}) copy-start(f32[640,128]{1,0:T(8,128)S(1)} %broadcast_select_fusion.refs_1_.refs_2_) | copy-start | bytes 983044
  23.6 4.1 %collective-permute-start.4 = (f32[640,128]{1,0:T(8,128)S(1)}, f32[640,128]{1,0:T(8,128)S(1)}, u32[]{:S(2)}, u32[]{:S(2)}) collective-permute-start(f32[640,128]{1,0:T(8,128)S(1)} %broadcast_select_fusion.refs_1_.refs_2_), channel_id=1, source_target_pairs={{0,1},{1,0},{2,3},{3,2},{4,5},{5,4},{6,7},{7,6},{8,9},{9,8},{10,11... | collective-permute-start | bytes 983048 | tf_op jit(solution)/shard_map/ppermute | solution.py:336
  27.7 9.2 %copy-start.4 = (f32[640,128]{1,0:T(8,128)}, f32[640,128]{1,0:T(8,128)S(1)}, u32[]{:S(2)}) copy-start(f32[640,128]{1,0:T(8,128)S(1)} %collective-permute-done.4.refs_2_.refs_3_) | copy-start | bytes 983044
  27.7 7.9 %collective-permute-start.5 = (f32[160,128]{1,0:T(8,128)S(1)}, f32[160,128]{1,0:T(8,128)S(1)}, u32[]{:S(2)}, u32[]{:S(2)}) collective-permute-start(f32[160,128]{1,0:T(8,128)S(1)} %dynamic-slice_select_fusion), channel_id=1, source_target_pairs={{0,0},{1,8},{2,16},{3,24},{4,32},{5,40},{6,48},{7,56},{8,64},{9,72... | collective-permute-start | bytes 245768 | tf_op jit(solution)/shard_map/ppermute | solution.py:344
  35.6 0.6 copy-start.6
  84.3 19.9 %all-to-all-start.2 = ((f32[16,160,128]{2,1,0:T(8,128)}), f32[16,160,128]{2,1,0:T(8,128)S(1)}, u32[]{:S(2)}, u32[]{:S(2)}) async-start(f32[16,160,128]{2,1,0:T(8,128)} %get-tuple-element.14), calls=%async_computation.2 | async-start | bytes 2621440 | tf_op jit(solution)/shard_map/all_to_all | solution.py:361
  104.2 1.1 copy-start.1
  108.7 3.9 %copy-start.7 = (f32[160,128]{1,0:T(8,128)S(1)}, f32[160,128]{1,0:T(8,128)}, u32[]{:S(2)}) copy-start(f32[160,128]{1,0:T(8,128)} %get-tuple-element.20) | copy-start | bytes 245764
  108.7 20.0 %all-to-all-start.3 = ((f32[16,160,128]{2,1,0:T(8,128)}), f32[16,160,128]{2,1,0:T(8,128)S(1)}, u32[]{:S(2)}, u32[]{:S(2)}) async-start(f32[16,160,128]{2,1,0:T(8,128)} %get-tuple-element.18), calls=%async_computation.3 | async-start | bytes 2621440 | tf_op jit(solution)/shard_map/all_to_all | solution.py:376
  112.6 16.2 %collective-permute-start.6 = (f32[160,128]{1,0:T(8,128)S(1)}, f32[160,128]{1,0:T(8,128)S(1)}, u32[]{:S(2)}, u32[]{:S(2)}) collective-permute-start(f32[160,128]{1,0:T(8,128)S(1)} %copy-done.7), channel_id=1, source_target_pairs={{0,0},{8,1},{16,2},{24,3},{32,4},{40,5},{48,6},{56,7},{64,8},{72,9... | collective-permute-start | bytes 245768 | tf_op jit(solution)/shard_map/ppermute | solution.py:375
  128.7 16.2 %copy-start = (f32[16,160,128]{2,1,0:T(8,128)}, f32[16,160,128]{2,1,0:T(8,128)S(1)}, u32[]{:S(2)}) copy-start(f32[16,160,128]{2,1,0:T(8,128)S(1)} %all-to-all-done.3.refs_2_.refs_4_) | copy-start | bytes 3932164
  129.7 22.3 %all-to-all-start.5 = ((f32[8,160,128]{2,1,0:T(8,128)}), f32[8,160,128]{2,1,0:T(8,128)S(1)}, u32[]{:S(2)}, u32[]{:S(2)}) async-start(f32[8,160,128]{2,1,0:T(8,128)} %broadcast_in_dim.5), calls=%async_computation.5 | async-start | bytes 1310720 | tf_op jit(solution)/shard_map/all_to_all | solution.py:386
  152.0 4.3 %copy-start.5 = (f32[8,160,128]{2,1,0:T(8,128)}, f32[8,160,128]{2,1,0:T(8,128)S(1)}, u32[]{:S(2)}) copy-start(f32[8,160,128]{2,1,0:T(8,128)S(1)} %all-to-all-done.5) | copy-start | bytes 1966084
  152.0 13.8 %all-to-all-start.4 = ((f32[8,128,128]{2,1,0:T(8,128)}), f32[8,128,128]{2,1,0:T(8,128)S(1)}, u32[]{:S(2)}, u32[]{:S(2)}) async-start(f32[8,128,128]{2,1,0:T(8,128)} %inner.1), calls=%async_computation.4 | async-start | bytes 1048576 | tf_op jit(solution)/shard_map/all_to_all | solution.py:396
  165.7 0.8 copy-start.3
Sparse Core Ops, SparseCore 0:
  36.3 49.4 all-gather.1

commit v2 on v1

v2 whole, which is shorter than its diff:
```python
import jax
import jax.numpy as jnp
from jax import lax
from jax.experimental import pallas as pl
from jax.experimental.pallas import tpu as pltpu
from jax.sharding import PartitionSpec as P

W = 128
NR = 16
NC = 8
STEP = 256
WIDE = 512
F32 = jnp.float32
BF16 = jnp.bfloat16
SM = pl.BlockSpec(memory_space=pltpu.SMEM)
HB = pl.BlockSpec(memory_space=pltpu.HBM)


def shape(*dims, dtype=F32):
    return jax.ShapeDtypeStruct(dims, dtype)


def exact(a, b, ca, cb):
    return lax.dot_general(
        a, b, (((ca,), (cb,)), ((), ())), precision=lax.Precision.HIGHEST, preferred_element_type=F32
    )


def split(x):
    hi = x.astype(BF16)
    return hi, (x - hi.astype(F32)).astype(BF16)


def bdot(a, b, ca, cb):
    return lax.dot_general(a, b, (((ca,), (cb,)), ((), ())), preferred_element_type=F32)


def three(a, b, ca, cb):
    (ah, al), (bh, bl) = a, b
    return bdot(ah, bh, ca, cb) + (bdot(ah, bl, ca, cb) + bdot(al, bh, ca, cb))


def dot3(a, b, ca, cb):
    return three(split(a), split(b), ca, cb)


def iota2(dims, dim):
    return lax.broadcasted_iota(jnp.int32, dims, dim)


def run(copies):
    for copy in copies:
        copy.start()
    return copies


def wait(copies):
    for copy in copies:
        copy.wait()


def call(kernel, name, flops, args, outs, scratch, sems):
    single = not isinstance(outs, list)
    out_list = [outs] if single else outs
    size = sum(4 * a.size for a in args[1:]) + sum(4 * o.size for o in out_list)

    def body(*refs):
        n = len(args)
        m = n + len(out_list)
        sem = refs[-1]
        used = []

        def copy(src, dst):
            used.append(None)
            return pltpu.make_async_copy(src, dst, sem.at[len(used) - 1])

        kernel(refs[0], refs[1:n], refs[n:m], refs[m:-1], copy)

    result = pl.pallas_call(
        body,
        in_specs=[SM] + [HB] * (len(args) - 1),
        out_specs=[HB] * len(out_list),
        out_shape=out_list,
        scratch_shapes=[pltpu.VMEM(s.shape, s.dtype) for s in scratch] + [pltpu.SemaphoreType.DMA((sems,))],
        compiler_params=pltpu.CompilerParams(vmem_limit_bytes=60 * 1024 * 1024),
        cost_estimate=pl.CostEstimate(flops=int(flops), bytes_accessed=int(size), transcendentals=0),
        name=name,
    )(*args)
    return result[0] if single else result


def load_panel(rc, held, other, buf, copy):
    half = held.shape[0]
    at = pl.multiple_of(rc[2], half)
    return run([copy(held, buf.at[pl.ds(at, half)]), copy(other, buf.at[pl.ds(half - at, half)])])


def clear_top(rc, buf):
    @pl.when(rc[0] == 0)
    def _():
        buf[:W] = jnp.zeros((W, W), F32)


def gram_kernel(rc, ins, outs, bufs, copy):
    buf, out = bufs
    wait(load_panel(rc, ins[0], ins[1], buf, copy))
    clear_top(rc, buf)
    p = split(buf[...])
    g = three(p, p, 0, 0).reshape(NR, 8, W)
    t = jnp.where(rc[0] == 0, buf[W : 2 * W], 0.0).reshape(NR, 8, W)
    out[...] = jnp.concatenate([g, t], 1)
    wait(run([copy(out, outs[0])]))


def second_kernel(rc, ins, outs, bufs, copy):
    buf, out = bufs
    cols = buf.shape[1]
    wait(run([copy(ins[0].at[pl.ds(W, W)], buf)]))
    for b in range(cols // WIDE):
        sl = slice(b * WIDE, (b + 1) * WIDE)
        out[sl] = buf[:, sl].T
    piece = outs[0].shape[1]
    wait(run([copy(out.at[pl.ds(k * piece, piece)], outs[0].at[k]) for k in range(NR)]))


def first_kernel(rc, ins, outs, bufs, copy):
    a_ref, held, other = ins
    buf, panel, acc, rows_out = bufs
    rows, cols = buf.shape
    n = rows // STEP
    first = load_panel(rc, held, other, panel, copy)
    copies = run([copy(a_ref.at[pl.ds(k * STEP, STEP)], buf.at[pl.ds(k * STEP, STEP)]) for k in range(n)])
    wait(first)
    clear_top(rc, panel)
    ph, plow = split(panel[...])
    both = jnp.concatenate([ph, plow], 1)
    for k in range(n):
        copies[k].wait()
        lo, up = k * STEP, (k + 1) * STEP
        for b in range(cols // WIDE):
            sl = slice(b * WIDE, (b + 1) * WIDE)
            ah, al = split(buf[lo:up, sl])
            x = bdot(both[lo:up], ah, 0, 0)
            x = x[:W] + (x[W:] + bdot(ph[lo:up], al, 0, 0))
            if k == 0:
                acc[:, sl] = x
            elif k < n - 1:
                acc[:, sl] += x
            else:
                rows_out[sl] = (acc[:, sl] + x).T
    piece = outs[0].shape[1]
    wait(run([copy(rows_out.at[pl.ds(k * piece, piece)], outs[0].at[k]) for k in range(NR)]))


def lane(x, k):
    return jnp.broadcast_to(x[:, k : k + 1], (8, W))


def row(x, k):
    return jnp.broadcast_to(x[k : k + 1], (8, W))


def inverse_factor(g):
    lanes = iota2((8, W), 1)
    subs = iota2((8, W), 0)
    tiles = [g[8 * t : 8 * t + 8] for t in range(W // 8)]
    done = []
    for k in range(0, W, 2):
        t0, o = k // 8, k % 8
        top = tiles[t0]
        at0, at1 = lanes == k, lanes == k + 1
        both = at0 | at1
        c0, c1 = lane(top, k), lane(top, k + 1)
        a, b, d = row(c0, o), row(c1, o), row(c1, o + 1)
        r0 = jnp.where(at1, 0.0, jnp.where(at0, 1.0, row(top, o)))
        r1 = jnp.where(at0, 0.0, jnp.where(at1, 1.0, row(top, o + 1)))
        ia = 1.0 / a
        ba = b * ia
        n1 = r1 - ba * r0
        s = d - b * ba
        q1 = n1 * (1.0 / s)
        q0 = r0 * ia - ba * q1
        for t in range(t0, W // 8):
            m = tiles[t]
            if t > t0:
                tiles[t] = jnp.where(both, 0.0, m) - lane(m, k) * q0 - lane(m, k + 1) * q1
            elif o < 6:
                tiles[t] = jnp.where(subs > o + 1, jnp.where(both, 0.0, m) - c0 * q0 - c1 * q1, m)
        if o == 0:
            final = jnp.zeros((8, W), F32)
        final = jnp.where(subs == o, r0 * lax.rsqrt(a), jnp.where(subs == o + 1, n1 * lax.rsqrt(s), final))
        if o == 6:
            done.append(final)
    i, j = iota2((W, W), 0), iota2((W, W), 1)
    return jnp.where(i >= j, jnp.concatenate(done, 0), 0.0)


def factor_kernel(rc, ins, outs, bufs, copy):
    msg, out = bufs
    wait(run([copy(ins[0], msg)]))
    out[...] = inverse_factor(msg[:, :8].reshape(W, W))
    wait(run([copy(out, outs[0])]))


def coupling_kernel(rc, ins, outs, bufs, copy):
    msg, linv, out = bufs
    wait(run([copy(ins[0], msg), copy(ins[1], linv)]))
    i, j = iota2((W, W), 0), iota2((W, W), 1)
    shifted = jnp.where(i == j, 1.0, 0.0) - exact(linv[...], msg[:, 8:].reshape(W, W), 1, 1)
    finv = inverse_factor(exact(shifted, shifted, 0, 0))
    out[...] = exact(finv, exact(finv, shifted, 1, 1), 0, 0)
    wait(run([copy(out, outs[0])]))


def piece_kernel(rc, ins, outs, bufs, copy):
    msg, linv, f, out = bufs
    wait(run([copy(ins[0], msg), copy(ins[1], linv), copy(ins[2].at[0], f)]))
    out[...] = dot3(jnp.sum(msg[...], 0), linv[...], 1, 1) - f[...]
    wait(run([copy(out, outs[0].at[k]) for k in range(NR)] + [copy(out, outs[1])]))


def vectors_kernel(rc, ins, outs, bufs, copy):
    msg, linv, v = bufs
    cols = v.shape[2]
    p = msg.reshape(cols, W)
    wait(run([copy(ins[0], msg), copy(ins[1], linv)]))
    ls = split(linv[...])
    for b in range(cols // WIDE):
        sl = slice(b * WIDE, (b + 1) * WIDE)
        at = iota2((W, WIDE), 1) + (rc[1] * cols + b * WIDE - W)
        x = three(ls, split(p[sl]), 1, 1)
        x = jnp.where(at < 0, 0.0, x) - jnp.where(at == iota2((W, WIDE), 0), 1.0, 0.0)
        v[0, :, sl], v[1, :, sl] = split(x)
    wait(run([copy(v, outs[0])]))


def inner_kernel(rc, ins, outs, bufs, copy):
    v, y, out = bufs
    piece = y.shape[1]
    first = run([copy(ins[0], v), copy(ins[1], y)])
    more = run([copy(ins[2], outs[0].at[k, pl.ds(0, piece)]) for k in range(NC)])
    wait(first)
    out[...] = three((v[0], v[1]), split(y[...].reshape(v.shape[2], W)), 1, 0)
    wait(more + run([copy(out, outs[0].at[k, pl.ds(piece, W)]) for k in range(NC)]))


def sides_kernel(rc, ins, outs, bufs, copy):
    held, other, y_c, linv_ref, coup_ref = ins
    panel, yc, linv, coup, left, wide = bufs
    rows, cols = panel.shape[0], wide.shape[1]
    small = run([copy(linv_ref, linv), copy(coup_ref, coup), copy(y_c, yc)])
    more = load_panel(rc, held, other, panel, copy)
    wait(small)
    ls, cs = split(linv[...]), split(coup[...])
    flat = yc.reshape(cols, W)
    for b in range(cols // WIDE):
        sl = slice(b * WIDE, (b + 1) * WIDE)
        wide[:, sl] = three(cs, split(flat[sl]), 1, 1)
    last = run([copy(wide, outs[1])])
    wait(more)
    clear_top(rc, panel)
    for k in range(rows // STEP):
        sl = slice(k * STEP, (k + 1) * STEP)
        ids = rc[0] * rows + k * STEP + iota2((STEP, W), 0)
        v = three(split(panel[sl]), ls, 1, 1) - jnp.where(ids - W == iota2((STEP, W), 1), 1.0, 0.0)
        left[0, sl], left[1, sl] = split(v)
    wait(last + run([copy(left, outs[0])]))


def last_kernel(rc, ins, outs, bufs, copy):
    a_ref, msg_ref, coup_ref, left_ref, wide_ref, v_ref = ins
    buf, s, coup, yr, left, wide, right = bufs
    rows, cols = buf.shape
    piece = yr.shape[1]
    n = cols // WIDE
    small = run([copy(msg_ref.at[:, pl.ds(piece, W)], s), copy(coup_ref, coup)])
    lefts = run([copy(msg_ref.at[:, pl.ds(0, piece)], yr), copy(left_ref, left.at[:, :, pl.ds(0, W)])])
    mid = run([copy(v_ref, right.at[:, pl.ds(W, W)]), copy(wide_ref, wide)])
    cut = [pl.ds(k * WIDE, WIDE) for k in range(n)]
    copies = run([copy(a_ref.at[:, cut[k]], buf.at[:, cut[k]]) for k in range(n)])
    wait(small)
    cs = split(coup[...])
    middle = three(split(three(cs, split(jnp.sum(s[...], 0)), 1, 0)), cs, 1, 1)
    ms = split(0.5 * (middle + middle.T))
    wait(lefts)
    left[0, :, W:], left[1, :, W:] = split(three(split(yr[...].reshape(rows, W)), cs, 1, 1))
    wait(mid)
    lh, ll = left[0], left[1]
    ends = []
    for k in range(n):
        sl = slice(k * WIDE, (k + 1) * WIDE)
        vh, vl = right[0, W:, sl], right[1, W:, sl]
        wh, wl = split(wide[:, sl] - three(ms, (vh, vl), 1, 0))
        rh = jnp.concatenate([wh, vh], 0)
        rl = jnp.concatenate([wl, vl], 0)
        copies[k].wait()
        buf[:, sl] -= bdot(lh, rh, 1, 0) + (bdot(ll, rh, 1, 0) + bdot(lh, rl, 1, 0))
        ends += run([copy(buf.at[:, cut[k]], outs[0].at[:, cut[k]])])
    wait(ends)


def spread(x, n):
    return jnp.broadcast_to(x[None], (n,) + x.shape)


def on_device(matrix):
    rows, cols = matrix.shape
    piece = cols // NR
    half = rows // 2
    r = lax.axis_index("prow")
    c = lax.axis_index("pcol")
    axes = ("prow", "pcol")
    holds_top = (c == 0) | (c == 2) | (c == 4) | (c == 7)
    rc = jnp.stack([r, c, jnp.where(holds_top, 0, half)])
    big = 6 * rows * cols * W

    top, bot = matrix[:half, :W], matrix[half:, :W]
    to1 = lax.ppermute(bot, "pcol", [(0, 1)])
    to2 = lax.ppermute(top, "pcol", [(0, 2)])
    to6 = lax.ppermute(bot, "pcol", [(0, 6)])
    f_msg = call(
        second_kernel, "second", W, (rc, matrix), shape(NR, piece, W), [shape(W, cols), shape(cols, W)], 1 + NR
    )
    f_msg = lax.all_to_all(f_msg, "prow", 0, 0, tiled=True)
    send = jnp.where(c == 0, top, jnp.where(c == 1, to1, jnp.where(c == 2, to2, to6)))
    got = lax.ppermute(send, "pcol", [(0, 7), (1, 3), (2, 4), (6, 5)])
    held = jnp.where((c == 0) | (c == 1) | (c == 2) | (c == 6), send, got)
    other = lax.ppermute(held, "pcol", [(i, i ^ 1) for i in range(NC)])
    owner = [(8 * ((g // NC) % 2) + g % NC) * NC + (g // NC) // 2 for g in range(NR * NC)]
    at = (c % (NC // 2)) * piece
    mine = jnp.where(
        (c < NC // 2) == holds_top,
        lax.dynamic_slice_in_dim(held, at, piece, 0),
        lax.dynamic_slice_in_dim(other, at, piece, 0),
    )
    panel_q = lax.ppermute(mine, axes, list(enumerate(owner)))
    half_bufs = [shape(rows, W)]
    small = call(gram_kernel, "gram", 6 * rows * W * W, (rc, held, other), shape(NR, 16, W), half_bufs + [shape(NR, 16, W)], 3)
    small, f_msg, panel_q = lax.optimization_barrier((small, f_msg, panel_q))
    small = lax.all_to_all(small, "prow", 0, 0, tiled=True)
    panel_c = lax.all_to_all(spread(panel_q, NR), "prow", 0, 0, tiled=True)
    msg = call(
        first_kernel,
        "first_pass",
        big,
        (rc, matrix, held, other),
        shape(NR, piece, W),
        [shape(rows, cols), shape(rows, W), shape(W, cols), shape(cols, W)],
        2 + rows // STEP + NR,
    )
    small = spread(jnp.sum(small, 0), NR)
    small, msg = lax.optimization_barrier((small, msg))
    small = lax.all_to_all(small, "prow", 0, 0, tiled=True)
    msg, panel_c = lax.optimization_barrier((msg, panel_c))
    msg = lax.all_to_all(msg, "prow", 0, 0, tiled=True)
    linv = call(factor_kernel, "factor", 8e9, (rc, small), shape(W, W), [shape(NR, 16, W), shape(W, W)], 2)
    msg, y_q = call(
        piece_kernel,
        "piece_image",
        msg.size,
        (rc, msg, linv, f_msg),
        [shape(NR, piece, W), shape(piece, W)],
        [shape(NR, piece, W), shape(W, W), shape(piece, W), shape(piece, W)],
        3 + NR + 1,
    )
    y_q, small = lax.optimization_barrier((y_q, small))
    y_p = lax.ppermute(y_q, axes, [(b, a) for a, b in enumerate(owner)])
    msg = lax.all_to_all(msg, "prow", 0, 0, tiled=True)
    coup = call(
        coupling_kernel, "coupling", 8e9, (rc, small, linv), shape(W, W), [shape(NR, 16, W), shape(W, W), shape(W, W)], 3
    )
    vt = call(
        vectors_kernel,
        "vectors",
        6 * cols * W * W,
        (rc, panel_c, linv),
        shape(2, W, cols, dtype=BF16),
        [shape(NR, piece, W), shape(W, W), shape(2, W, cols, dtype=BF16)],
        3,
    )
    end = call(
        inner_kernel,
        "inner",
        6 * cols * W * W,
        (rc, vt, msg, y_p),
        shape(NC, piece + W, W),
        [shape(2, W, cols, dtype=BF16), shape(NR, piece, W), shape(W, W)],
        2 + 2 * NC,
    )
    end = lax.all_to_all(end, "pcol", 0, 0, tiled=True)
    left, wide = call(
        sides_kernel,
        "sides",
        12 * (rows + cols) * W * W,
        (rc, held, other, msg, linv, coup),
        [shape(2, rows, W, dtype=BF16), shape(W, cols)],
        [
            shape(rows, W),
            shape(NR, piece, W),
            shape(W, W),
            shape(W, W),
            shape(2, rows, W, dtype=BF16),
            shape(W, cols),
        ],
        7,
    )
    return call(
        last_kernel,
        "last_pass",
        2 * big,
        (rc, matrix, end, coup, left, wide, vt),
        shape(rows, cols),
        [
            shape(rows, cols),
            shape(NC, W, W),
            shape(W, W),
            shape(NC, piece, W),
            shape(2, rows, 2 * W, dtype=BF16),
            shape(W, cols),
            shape(2, 2 * W, cols, dtype=BF16),
        ],
        6 + 2 * (cols // WIDE),
    )


def solution(mesh):
    return jax.shard_map(
        on_device, mesh=mesh, in_specs=(P("prow", "pcol"),), out_specs=P("prow", "pcol"), check_vma=False
    )
```

time: 188 us -> 203 us (1.080)
  Pallas kernels: 59.8 us -> 84.9 us
  between operations: 13.7 us -> 0.48 us
  blocking collectives: 29 us -> 18.2 us
  starting transfers between devices: 44.3 us -> 54.9 us
  local copies, waits for them, and re-layouts: 4.61 us -> 7.38 us
    pallas_call x8 -> x10, Pallas kernels: 59.8 us -> 84.9 us  [call(): pl.pallas_call(body, in_specs=[SM] + [HB] * (len(args) - 1), out_specs=[H...]
    all_to_all x2 -> x1, blocking collectives: 29 us -> 18.2 us  [on_device(): small = lax.all_to_all(small, 'prow', 0, 0, tiled=True)]
    all_to_all x2 -> x4, waiting for transfers between devices: 7.8 us -> 16 us  [the longest x1 9.31 us: on_device(): panel_c = lax.all_to_all(spread(panel_q, NR), 'prow', 0, 0, tiled=True)]
    all_to_all x2 -> x4, starting transfers between devices: 15.6 us -> 23.4 us  [the longest x1 8.44 us: on_device(): f_msg = lax.all_to_all(f_msg, 'prow', 0, 0, tiled=True)]
    ppermute x1, waiting for transfers between devices: 6.83 us -> 0.01 us  [on_device(): to1 = lax.ppermute(bot, 'pcol', [(0, 1)])]
    ppermute x1, waiting for transfers between devices: 4.07 us -> 1.13 us  [on_device(): panel_q = lax.ppermute(mine, axes, list(enumerate(owner)))]
    ppermute x1, starting transfers between devices: 10.4 us -> 8.21 us  [on_device(): y_p = lax.ppermute(y_q, axes, [(b, a) for a, b in enumerate(owner)])]
    unnamed x16 -> x20, local copies, waits for them, and re-layouts: 2.5 us -> 4.42 us
  transfers between devices with their start and end apart: 12 -> 13, of which waited for: 8 -> 7; matrix products, arithmetic and copies ran while one was open for 0% -> 1% of each run, Pallas kernels for 24% -> 24%
where the time goes in v2:
time: 203 us; the launch traced here: 202 us
  Pallas kernels  84.9 us (42%)
  starting transfers between devices  54.9 us (27%)
  waiting for transfers between devices  34.2 us (17%)
  blocking collectives  18.2 us (9%)
  local copies, waits for them, and re-layouts  7.38 us (4%)
    pallas_call x10, Pallas kernels, call(): pl.pallas_call(body, in_specs=[SM] + [HB] * (len(args) - 1), out_specs=[H...  84.9 us
    all_to_all x1, blocking collectives, on_device(): small = lax.all_to_all(small, 'prow', 0, 0, tiled=True)  18.2 us
    all_to_all x2, starting transfers between devices, on_device(): msg = lax.all_to_all(msg, 'prow', 0, 0, tiled=True)  9.62 us
    all_to_all x1, waiting for transfers between devices, on_device(): panel_c = lax.all_to_all(spread(panel_q, NR), 'prow', 0, 0, tiled=True)  9.31 us
    all_to_all x1, starting transfers between devices, on_device(): f_msg = lax.all_to_all(f_msg, 'prow', 0, 0, tiled=True)  8.44 us
    ppermute x1, starting transfers between devices, on_device(): y_p = lax.ppermute(y_q, axes, [(b, a) for a, b in enumerate(owner)])  8.21 us
    ppermute x1, waiting for transfers between devices, on_device(): y_p = lax.ppermute(y_q, axes, [(b, a) for a, b in enumerate(owner)])  7.64 us
    all_to_all x1, starting transfers between devices, on_device(): end = lax.all_to_all(end, 'pcol', 0, 0, tiled=True)  6.93 us
  transfers between devices with their start and end apart: 13, of which 7 were waited for; matrix products, arithmetic and copies ran while one was open for 1% of the time, Pallas kernels for 24%

profile of v2, /device:TPU:1, one launch (start us, length us, event | category | flops | bytes accessed | tf_op | source)
XLA Modules:
  0.0 201.6 jit_solution(5092860401322617361)
XLA Ops:
  0.0 1.1 fusion
  2.5 1.3 collective-permute-start
  4.4 3.6 %second.1 = f32[16,160,128]{2,1,0:T(8,128)} custom-call(s32[3]{0:T(128)} %pad_add_fusion.refs_0_, f32[1280,2560]{1,0:T(8,128)} %refs_1_.5), custom_call_target="tpu_custom_call" | custom-call | flops 128 | bytes 14417920 | tf_op jit(solution)/shard_map/second/pallas_call | solution.py:79
  8.0 8.4 %all-to-all-start = ((f32[16,160,128]{2,1,0:T(8,128)}), f32[16,160,128]{2,1,0:T(8,128)S(1)}, u32[]{:S(2)}, u32[]{:S(2)}) async-start(f32[16,160,128]{2,1,0:T(8,128)} %second.1), calls=%async_computation | async-start | bytes 2621440 | tf_op jit(solution)/shard_map/all_to_all | solution.py:324
  17.5 2.6 %collective-permute-start.3 = (f32[640,128]{1,0:T(8,128)S(1)}, f32[640,128]{1,0:T(8,128)S(1)}, u32[]{:S(2)}, u32[]{:S(2)}) collective-permute-start(f32[640,128]{1,0:T(8,128)S(1)} %select_select_fusion), channel_id=1, source_target_pairs={{0,7},{1,3},{2,4},{6,5},{8,15},{9,11},{10,12},{14,13},{16,23},{17,... | collective-permute-start | bytes 983048 | tf_op jit(solution)/shard_map/ppermute | solution.py:326
  20.2 4.0 %collective-permute-done.3 = f32[640,128]{1,0:T(8,128)S(1)} collective-permute-done((f32[640,128]{1,0:T(8,128)S(1)}, f32[640,128]{1,0:T(8,128)S(1)}, u32[]{:S(2)}, u32[]{:S(2)}) %collective-permute-start.3) | collective-permute-done | bytes 327712 | tf_op jit(solution)/shard_map/ppermute | solution.py:326
  24.2 4.6 %collective-permute-start.4 = (f32[640,128]{1,0:T(8,128)S(1)}, f32[640,128]{1,0:T(8,128)S(1)}, u32[]{:S(2)}, u32[]{:S(2)}) collective-permute-start(f32[640,128]{1,0:T(8,128)S(1)} %broadcast_select_fusion.refs_1_.refs_2_), channel_id=1, source_target_pairs={{0,1},{1,0},{2,3},{3,2},{4,5},{5,4},{6,7},{7,6},{8,9},{9,8},{10,11... | collective-permute-start | bytes 983048 | tf_op jit(solution)/shard_map/ppermute | solution.py:328
  28.8 1.3 collective-permute-done.4.refs_2_.refs_3_
  30.0 3.8 %collective-permute-start.5 = (f32[160,128]{1,0:T(8,128)S(1)}, f32[160,128]{1,0:T(8,128)S(1)}, u32[]{:S(2)}, u32[]{:S(2)}) collective-permute-start(f32[160,128]{1,0:T(8,128)S(1)} %dynamic-slice_select_fusion), channel_id=1, source_target_pairs={{0,0},{1,8},{2,16},{3,24},{4,32},{5,40},{6,48},{7,56},{8,64},{9,72... | collective-permute-start | bytes 245768 | tf_op jit(solution)/shard_map/ppermute | solution.py:336
  33.9 2.9 %gram.1 = f32[16,16,128]{2,1,0:T(8,128)} custom-call(s32[3]{0:T(128)} %pad_add_fusion.refs_0_, f32[640,128]{1,0:T(8,128)} %copy-done.5, f32[640,128]{1,0:T(8,128)} %copy-done.6), custom_call_target="tpu_custom_call" | custom-call | flops 125829120 | bytes 786432 | tf_op jit(solution)/shard_map/gram/pallas_call | solution.py:79
  36.7 1.1 collective-permute-done.5
  37.9 18.2 %all_to_all.35 = f32[16,16,128]{2,1,0:T(8,128)S(1)} all-to-all(f32[16,16,128]{2,1,0:T(8,128)} %gram.1), channel_id=1, replica_groups=mesh['prow'=16,'pcol'=8] {'prow'}, dimensions={0} | all-to-all | bytes 262144 | tf_op jit(solution)/shard_map/all_to_all | solution.py:340
  56.1 1.2 broadcast_in_dim.5
  57.2 3.7 %all-to-all-start.2 = ((f32[16,160,128]{2,1,0:T(8,128)}), f32[16,160,128]{2,1,0:T(8,128)S(1)}, u32[]{:S(2)}, u32[]{:S(2)}) async-start(f32[16,160,128]{2,1,0:T(8,128)} %broadcast_in_dim.5), calls=%async_computation.2 | async-start | bytes 2621440 | tf_op jit(solution)/shard_map/all_to_all | solution.py:341
  61.0 7.8 %first_pass.1 = f32[16,160,128]{2,1,0:T(8,128)} custom-call(s32[3]{0:T(128)} %pad_add_fusion.refs_0_, f32[1280,2560]{1,0:T(8,128)} %refs_1_.5, f32[640,128]{1,0:T(8,128)} %copy-done.5, f32[640,128]{1,0:T(8,128)} %copy-done.6), custom_call_target="tpu_custom_call" | custom-call | flops 2516582400 | bytes 15073280 | tf_op jit(solution)/shard_map/first_pass/pallas_call | solution.py:79
  69.4 9.3 %all-to-all-done.2.refs_1_ = f32[16,160,128]{2,1,0:T(8,128)S(1)} async-done(((f32[16,160,128]{2,1,0:T(8,128)}), f32[16,160,128]{2,1,0:T(8,128)S(1)}, u32[]{:S(2)}, u32[]{:S(2)}) %all-to-all-start.2) | async-done | bytes 1310752 | tf_op jit(solution)/shard_map/all_to_all | solution.py:341
  78.7 4.3 %all-to-all-start.3 = ((f32[16,16,128]{2,1,0:T(8,128)}), f32[16,16,128]{2,1,0:T(8,128)S(1)}, u32[]{:S(2)}, u32[]{:S(2)}) async-start(f32[16,16,128]{2,1,0:T(8,128)} %broadcast_in_dim.4), calls=%async_computation.3 | async-start | bytes 262144 | tf_op jit(solution)/shard_map/all_to_all | solution.py:353
  83.1 6.7 %all-to-all-done.3.refs_1_ = f32[16,16,128]{2,1,0:T(8,128)S(1)} async-done(((f32[16,16,128]{2,1,0:T(8,128)}), f32[16,16,128]{2,1,0:T(8,128)S(1)}, u32[]{:S(2)}, u32[]{:S(2)}) %all-to-all-start.3) | async-done | bytes 131104 | tf_op jit(solution)/shard_map/all_to_all | solution.py:353
  90.4 3.7 %all-to-all-start.4 = ((f32[16,160,128]{2,1,0:T(8,128)}), f32[16,160,128]{2,1,0:T(8,128)S(1)}, u32[]{:S(2)}, u32[]{:S(2)}) async-start(f32[16,160,128]{2,1,0:T(8,128)} %first_pass.1), calls=%async_computation.4 | async-start | bytes 2621440 | tf_op jit(solution)/shard_map/all_to_all | solution.py:355
  94.1 12.1 %factor.1.refs_2_.refs_4_ = f32[128,128]{1,0:T(8,128)} custom-call(s32[3]{0:T(128)} %pad_add_fusion.refs_0_, f32[16,16,128]{2,1,0:T(8,128)} %copy-done.7), custom_call_target="tpu_custom_call" | custom-call | flops 8000000000 | bytes 196608 | tf_op jit(solution)/shard_map/factor/pallas_call | solution.py:79
  106.2 4.2 %all-to-all-done.4.refs_1_ = f32[16,160,128]{2,1,0:T(8,128)S(1)} async-done(((f32[16,160,128]{2,1,0:T(8,128)}), f32[16,160,128]{2,1,0:T(8,128)S(1)}, u32[]{:S(2)}, u32[]{:S(2)}) %all-to-all-start.4) | async-done | bytes 1310752 | tf_op jit(solution)/shard_map/all_to_all | solution.py:355
  110.4 1.1 copy-done.3
  111.4 3.5 %piece_image.1 = (f32[16,160,128]{2,1,0:T(8,128)}, f32[160,128]{1,0:T(8,128)}) custom-call(s32[3]{0:T(128)} %pad_add_fusion.refs_0_, f32[16,160,128]{2,1,0:T(8,128)} %copy-done.3, f32[128,128]{1,0:T(8,128)} %factor.1.refs_2_.refs_4_, f32[16,160,128]{2,1,0:T(8,128)} %copy-done), custom_call_target="tpu_custom_call" | custom-call | flops 327680 | bytes 4079616 | tf_op jit(solution)/shard_map/piece_image/pallas_call | solution.py:79
  114.9 5.9 %all-to-all-start.5 = ((f32[16,160,128]{2,1,0:T(8,128)}), f32[16,160,128]{2,1,0:T(8,128)S(1)}, u32[]{:S(2)}, u32[]{:S(2)}) async-start(f32[16,160,128]{2,1,0:T(8,128)} %get-tuple-element.25), calls=%async_computation.5 | async-start | bytes 2621440 | tf_op jit(solution)/shard_map/all_to_all | solution.py:368
  120.9 8.2 %collective-permute-start.6 = (f32[160,128]{1,0:T(8,128)S(1)}, f32[160,128]{1,0:T(8,128)S(1)}, u32[]{:S(2)}, u32[]{:S(2)}) collective-permute-start(f32[160,128]{1,0:T(8,128)S(1)} %copy-done.9), channel_id=1, source_target_pairs={{0,0},{8,1},{16,2},{24,3},{32,4},{40,5},{48,6},{56,7},{64,8},{72,9... | collective-permute-start | bytes 245768 | tf_op jit(solution)/shard_map/ppermute | solution.py:367
  129.1 3.8 %vectors.1.refs_1_.refs_6_ = bf16[2,128,2560]{2,1,0:T(8,128)(2,1)} custom-call(s32[3]{0:T(128)} %pad_add_fusion.refs_0_, f32[16,160,128]{2,1,0:T(8,128)} %copy-done.1, f32[128,128]{1,0:T(8,128)} %factor.1.refs_2_.refs_4_), custom_call_target="tpu_custom_call" | custom-call | flops 251658240 | bytes 3997696 | tf_op jit(solution)/shard_map/vectors/pallas_call | solution.py:79
  132.9 7.6 %collective-permute-done.6.refs_3_ = f32[160,128]{1,0:T(8,128)S(1)} collective-permute-done((f32[160,128]{1,0:T(8,128)S(1)}, f32[160,128]{1,0:T(8,128)S(1)}, u32[]{:S(2)}, u32[]{:S(2)}) %collective-permute-start.6) | collective-permute-done | bytes 81952 | tf_op jit(solution)/shard_map/ppermute | solution.py:367
  142.2 21.8 %inner.1 = f32[8,288,128]{2,1,0:T(8,128)} custom-call(s32[3]{0:T(128)} %pad_add_fusion.refs_0_, bf16[2,128,2560]{2,1,0:T(8,128)(2,1)} %vectors.1.refs_1_.refs_6_, f32[16,160,128]{2,1,0:T(8,128)} %copy-done.2, f32[160,128]{1,0:T(8,128)} %copy-done.8), custom_call_target="tpu_custom_call" | custom-call | flops 251658240 | bytes 5193728 | tf_op jit(solution)/shard_map/inner/pallas_call | solution.py:79
  164.0 6.9 %all-to-all-start.6 = ((f32[8,288,128]{2,1,0:T(8,128)}), f32[8,288,128]{2,1,0:T(8,128)S(1)}, u32[]{:S(2)}, u32[]{:S(2)}) async-start(f32[8,288,128]{2,1,0:T(8,128)} %inner.1), calls=%async_computation.6 | async-start | bytes 2359296 | tf_op jit(solution)/shard_map/all_to_all | solution.py:390
  170.9 13.2 %coupling.1.refs_5_.refs_3_ = f32[128,128]{1,0:T(8,128)} custom-call(s32[3]{0:T(128)} %pad_add_fusion.refs_0_, f32[16,16,128]{2,1,0:T(8,128)} %copy-done.7, f32[128,128]{1,0:T(8,128)} %factor.1.refs_2_.refs_4_), custom_call_target="tpu_custom_call" | custom-call | flops 8000000000 | bytes 262144 | tf_op jit(solution)/shard_map/coupling/pallas_call | solution.py:79
  184.2 4.1 %sides.1 = (bf16[2,1280,128]{2,1,0:T(8,128)(2,1)}, f32[128,2560]{1,0:T(8,128)}) custom-call(s32[3]{0:T(128)} %pad_add_fusion.refs_0_, f32[640,128]{1,0:T(8,128)} %copy-done.5, f32[640,128]{1,0:T(8,128)} %copy-done.6, f32[16,160,128]{2,1,0:T(8,128)} %copy-done.2, f32[128,128]{1,0:T(8,128)} %factor.1.refs_2_.refs_4_, f32[128,128]{1,0:T(8,128)} %coupling.1.refs_5_.refs_3_), custom_call_target="tpu_custom_call" | custom-call | flops 754974720 | bytes 4718592 | tf_op jit(solution)/shard_map/sides/pallas_call | solution.py:79
  189.3 12.1 %last_pass.1 = f32[1280,2560]{1,0:T(8,128)} custom-call(s32[3]{0:T(128)} %pad_add_fusion.refs_0_, f32[1280,2560]{1,0:T(8,128)} %refs_1_.5, f32[8,288,128]{2,1,0:T(8,128)} %copy-done.4, f32[128,128]{1,0:T(8,128)} %coupling.1.refs_5_.refs_3_, bf16[2,1280,128]{2,1,0:T(8,128)(2,1)} %get-tuple-element.29.refs_4_, f32[128,2560]{1,0:T(8,128)} %get-tuple-element.30.refs_5_, ...), custom_call_target="tpu_custom_call" | custom-call | flops 5033164800 | bytes 32702464 | tf_op jit(solution)/shard_map/last_pass/pallas_call | solution.py:79
  (33 shorter events, 7.1 us)
Async XLA Ops:
  1.1 15.3 %collective-permute-start.1 = (f32[640,128]{1,0:T(8,128)S(1)}, f32[640,128]{1,0:T(8,128)S(1)}, u32[]{:S(2)}, u32[]{:S(2)}) collective-permute-start(f32[640,128]{1,0:T(8,128)S(1)} %get-tuple-element.31), channel_id=1, source_target_pairs={{0,2},{8,10},{16,18},{24,26},{32,34},{40,42},{48,50},{56,58},{64,6... | collective-permute-start | bytes 983048 | tf_op jit(solution)/shard_map/ppermute | solution.py:319
  1.8 14.6 %collective-permute-start.2 = (f32[640,128]{1,0:T(8,128)S(1)}, f32[640,128]{1,0:T(8,128)S(1)}, u32[]{:S(2)}, u32[]{:S(2)}) collective-permute-start(f32[640,128]{1,0:T(8,128)S(1)} %get-tuple-element.32), channel_id=1, source_target_pairs={{0,6},{8,14},{16,22},{24,30},{32,38},{40,46},{48,54},{56,62},{64,7... | collective-permute-start | bytes 983048 | tf_op jit(solution)/shard_map/ppermute | solution.py:320
  2.5 14.0 %collective-permute-start = (f32[640,128]{1,0:T(8,128)S(1)}, f32[640,128]{1,0:T(8,128)S(1)}, u32[]{:S(2)}, u32[]{:S(2)}) collective-permute-start(f32[640,128]{1,0:T(8,128)S(1)} %get-tuple-element.32), channel_id=1, source_target_pairs={{0,1},{8,9},{16,17},{24,25},{32,33},{40,41},{48,49},{56,57},{64,65... | collective-permute-start | bytes 983048 | tf_op jit(solution)/shard_map/ppermute | solution.py:318
  8.0 29.9 %all-to-all-start = ((f32[16,160,128]{2,1,0:T(8,128)}), f32[16,160,128]{2,1,0:T(8,128)S(1)}, u32[]{:S(2)}, u32[]{:S(2)}) async-start(f32[16,160,128]{2,1,0:T(8,128)} %second.1), calls=%async_computation | async-start | bytes 2621440 | tf_op jit(solution)/shard_map/all_to_all | solution.py:324
  17.5 6.6 %collective-permute-start.3 = (f32[640,128]{1,0:T(8,128)S(1)}, f32[640,128]{1,0:T(8,128)S(1)}, u32[]{:S(2)}, u32[]{:S(2)}) collective-permute-start(f32[640,128]{1,0:T(8,128)S(1)} %select_select_fusion), channel_id=1, source_target_pairs={{0,7},{1,3},{2,4},{6,5},{8,15},{9,11},{10,12},{14,13},{16,23},{17,... | collective-permute-start | bytes 983048 | tf_op jit(solution)/shard_map/ppermute | solution.py:326
  24.2 9.7 %copy-start.5 = (f32[640,128]{1,0:T(8,128)}, f32[640,128]{1,0:T(8,128)S(1)}, u32[]{:S(2)}) copy-start(f32[640,128]{1,0:T(8,128)S(1)} %broadcast_select_fusion.refs_1_.refs_2_) | copy-start | bytes 983044
  24.2 5.8 %collective-permute-start.4 = (f32[640,128]{1,0:T(8,128)S(1)}, f32[640,128]{1,0:T(8,128)S(1)}, u32[]{:S(2)}, u32[]{:S(2)}) collective-permute-start(f32[640,128]{1,0:T(8,128)S(1)} %broadcast_select_fusion.refs_1_.refs_2_), channel_id=1, source_target_pairs={{0,1},{1,0},{2,3},{3,2},{4,5},{5,4},{6,7},{7,6},{8,9},{9,8},{10,11... | collective-permute-start | bytes 983048 | tf_op jit(solution)/shard_map/ppermute | solution.py:328
  30.0 3.8 %copy-start.6 = (f32[640,128]{1,0:T(8,128)}, f32[640,128]{1,0:T(8,128)S(1)}, u32[]{:S(2)}) copy-start(f32[640,128]{1,0:T(8,128)S(1)} %collective-permute-done.4.refs_2_.refs_3_) | copy-start | bytes 983044
  30.0 7.9 %collective-permute-start.5 = (f32[160,128]{1,0:T(8,128)S(1)}, f32[160,128]{1,0:T(8,128)S(1)}, u32[]{:S(2)}, u32[]{:S(2)}) collective-permute-start(f32[160,128]{1,0:T(8,128)S(1)} %dynamic-slice_select_fusion), channel_id=1, source_target_pairs={{0,0},{1,8},{2,16},{3,24},{4,32},{5,40},{6,48},{7,56},{8,64},{9,72... | collective-permute-start | bytes 245768 | tf_op jit(solution)/shard_map/ppermute | solution.py:336
  37.9 19.4 %copy-start = (f32[16,160,128]{2,1,0:T(8,128)}, f32[16,160,128]{2,1,0:T(8,128)S(1)}, u32[]{:S(2)}) copy-start(f32[16,160,128]{2,1,0:T(8,128)S(1)} %all-to-all-done.refs_3_) | copy-start | bytes 3932164
  57.2 21.5 %all-to-all-start.2 = ((f32[16,160,128]{2,1,0:T(8,128)}), f32[16,160,128]{2,1,0:T(8,128)S(1)}, u32[]{:S(2)}, u32[]{:S(2)}) async-start(f32[16,160,128]{2,1,0:T(8,128)} %broadcast_in_dim.5), calls=%async_computation.2 | async-start | bytes 2621440 | tf_op jit(solution)/shard_map/all_to_all | solution.py:341
  78.7 11.0 %copy-start.1 = (f32[16,160,128]{2,1,0:T(8,128)}, f32[16,160,128]{2,1,0:T(8,128)S(1)}, u32[]{:S(2)}) copy-start(f32[16,160,128]{2,1,0:T(8,128)S(1)} %all-to-all-done.2.refs_1_) | copy-start | bytes 3932164
  78.7 11.0 %all-to-all-start.3 = ((f32[16,16,128]{2,1,0:T(8,128)}), f32[16,16,128]{2,1,0:T(8,128)S(1)}, u32[]{:S(2)}, u32[]{:S(2)}) async-start(f32[16,16,128]{2,1,0:T(8,128)} %broadcast_in_dim.4), calls=%async_computation.3 | async-start | bytes 262144 | tf_op jit(solution)/shard_map/all_to_all | solution.py:353
  89.8 0.6 copy-start.7
  90.4 20.0 %all-to-all-start.4 = ((f32[16,160,128]{2,1,0:T(8,128)}), f32[16,160,128]{2,1,0:T(8,128)S(1)}, u32[]{:S(2)}, u32[]{:S(2)}) async-start(f32[16,160,128]{2,1,0:T(8,128)} %first_pass.1), calls=%async_computation.4 | async-start | bytes 2621440 | tf_op jit(solution)/shard_map/all_to_all | solution.py:355
  110.4 1.1 copy-start.3
  114.9 5.9 %copy-start.9 = (f32[160,128]{1,0:T(8,128)S(1)}, f32[160,128]{1,0:T(8,128)}, u32[]{:S(2)}) copy-start(f32[160,128]{1,0:T(8,128)} %get-tuple-element.27) | copy-start | bytes 245764
  114.9 25.6 %all-to-all-start.5 = ((f32[16,160,128]{2,1,0:T(8,128)}), f32[16,160,128]{2,1,0:T(8,128)S(1)}, u32[]{:S(2)}, u32[]{:S(2)}) async-start(f32[16,160,128]{2,1,0:T(8,128)} %get-tuple-element.25), calls=%async_computation.5 | async-start | bytes 2621440 | tf_op jit(solution)/shard_map/all_to_all | solution.py:368
  120.9 19.7 %collective-permute-start.6 = (f32[160,128]{1,0:T(8,128)S(1)}, f32[160,128]{1,0:T(8,128)S(1)}, u32[]{:S(2)}, u32[]{:S(2)}) collective-permute-start(f32[160,128]{1,0:T(8,128)S(1)} %copy-done.9), channel_id=1, source_target_pairs={{0,0},{8,1},{16,2},{24,3},{32,4},{40,5},{48,6},{56,7},{64,8},{72,9... | collective-permute-start | bytes 245768 | tf_op jit(solution)/shard_map/ppermute | solution.py:367
  140.5 0.6 copy-start.8
  141.2 1.1 copy-start.2
  164.0 24.3 %all-to-all-start.6 = ((f32[8,288,128]{2,1,0:T(8,128)}), f32[8,288,128]{2,1,0:T(8,128)S(1)}, u32[]{:S(2)}, u32[]{:S(2)}) async-start(f32[8,288,128]{2,1,0:T(8,128)} %inner.1), calls=%async_computation.6 | async-start | bytes 2359296 | tf_op jit(solution)/shard_map/all_to_all | solution.py:390
  188.3 1.0 copy-start.4

commit v3 on v2

--- a/solution.py
+++ b/solution.py
@@ -110,6 +110,17 @@
     t = jnp.where(rc[0] == 0, buf[W : 2 * W], 0.0).reshape(NR, 8, W)
     out[...] = jnp.concatenate([g, t], 1)
     wait(run([copy(out, outs[0])]))
+
+
+def mix_kernel(rc, ins, outs, bufs, copy):
+    msg, p, small = bufs
+    piece, n = p.shape[0], small.shape[0]
+    first = run([copy(ins[0], msg)])
+    wait(run([copy(ins[1], p)]))
+    more = run([copy(p, outs[0].at[k, pl.ds(0, piece)]) for k in range(NR)])
+    wait(first)
+    small[...] = jnp.sum(msg[...], 0)
+    wait(more + run([copy(small, outs[0].at[k, pl.ds(piece, n)]) for k in range(NR)]))
 
 
 def second_kernel(rc, ins, outs, bufs, copy):
@@ -197,16 +208,16 @@
 
 def factor_kernel(rc, ins, outs, bufs, copy):
     msg, out = bufs
-    wait(run([copy(ins[0], msg)]))
-    out[...] = inverse_factor(msg[:, :8].reshape(W, W))
+    wait(run([copy(ins[0].at[:, pl.ds(ins[0].shape[1] - 16, 8)], msg)]))
+    out[...] = inverse_factor(msg[...].reshape(W, W))
     wait(run([copy(out, outs[0])]))
 
 
 def coupling_kernel(rc, ins, outs, bufs, copy):
     msg, linv, out = bufs
-    wait(run([copy(ins[0], msg), copy(ins[1], linv)]))
+    wait(run([copy(ins[0].at[:, pl.ds(ins[0].shape[1] - 8, 8)], msg), copy(ins[1], linv)]))
     i, j = iota2((W, W), 0), iota2((W, W), 1)
-    shifted = jnp.where(i == j, 1.0, 0.0) - exact(linv[...], msg[:, 8:].reshape(W, W), 1, 1)
+    shifted = jnp.where(i == j, 1.0, 0.0) - exact(linv[...], msg[...].reshape(W, W), 1, 1)
     finv = inverse_factor(exact(shifted, shifted, 0, 0))
     out[...] = exact(finv, exact(finv, shifted, 1, 1), 0, 0)
     wait(run([copy(out, outs[0])]))
@@ -223,7 +234,7 @@
     msg, linv, v = bufs
     cols = v.shape[2]
     p = msg.reshape(cols, W)
-    wait(run([copy(ins[0], msg), copy(ins[1], linv)]))
+    wait(run([copy(ins[0].at[:, pl.ds(0, msg.shape[1])], msg), copy(ins[1], linv)]))
     ls = split(linv[...])
     for b in range(cols // WIDE):
         sl = slice(b * WIDE, (b + 1) * WIDE)
@@ -235,10 +246,11 @@
 
 
 def inner_kernel(rc, ins, outs, bufs, copy):
-    v, y, out = bufs
+    v, y, out, mine = bufs
     piece = y.shape[1]
     first = run([copy(ins[0], v), copy(ins[1], y)])
-    more = run([copy(ins[2], outs[0].at[k, pl.ds(0, piece)]) for k in range(NC)])
+    wait(run([copy(ins[2], mine)]))
+    more = run([copy(mine, outs[0].at[k, pl.ds(0, piece)]) for k in range(NC)])
     wait(first)
     out[...] = three((v[0], v[1]), split(y[...].reshape(v.shape[2], W)), 1, 0)
     wait(more + run([copy(out, outs[0].at[k, pl.ds(piece, W)]) for k in range(NC)]))
@@ -299,10 +311,6 @@
     wait(ends)
 
 
-def spread(x, n):
-    return jnp.broadcast_to(x[None], (n,) + x.shape)
-
-
 def on_device(matrix):
     rows, cols = matrix.shape
     piece = cols // NR
@@ -336,9 +344,19 @@
     panel_q = lax.ppermute(mine, axes, list(enumerate(owner)))
     half_bufs = [shape(rows, W)]
     small = call(gram_kernel, "gram", 6 * rows * W * W, (rc, held, other), shape(NR, 16, W), half_bufs + [shape(NR, 16, W)], 3)
-    small, f_msg, panel_q = lax.optimization_barrier((small, f_msg, panel_q))
+    small, f_msg = lax.optimization_barrier((small, f_msg))
     small = lax.all_to_all(small, "prow", 0, 0, tiled=True)
-    panel_c = lax.all_to_all(spread(panel_q, NR), "prow", 0, 0, tiled=True)
+    small = call(
+        mix_kernel,
+        "mix",
+        NR * 16 * W,
+        (rc, small, panel_q),
+        shape(NR, piece + 16, W),
+        [shape(NR, 16, W), shape(piece, W), shape(16, W)],
+        2 + 2 * NR,
+    )
+    small, held, other = lax.optimization_barrier((small, held, other))
+    small = lax.all_to_all(small, "prow", 0, 0, tiled=True)
     msg = call(
         first_kernel,
         "first_pass",
@@ -348,12 +366,8 @@
         [shape(rows, cols), shape(rows, W), shape(W, cols), shape(cols, W)],
         2 + rows // STEP + NR,
     )
-    small = spread(jnp.sum(small, 0), NR)
-    small, msg = lax.optimization_barrier((small, msg))
-    small = lax.all_to_all(small, "prow", 0, 0, tiled=True)
-    msg, panel_c = lax.optimization_barrier((msg, panel_c))
     msg = lax.all_to_all(msg, "prow", 0, 0, tiled=True)
-    linv = call(factor_kernel, "factor", 8e9, (rc, small), shape(W, W), [shape(NR, 16, W), shape(W, W)], 2)
+    linv = call(factor_kernel, "factor", 8e9, (rc, small), shape(W, W), [shape(NR, 8, W), shape(W, W)], 2)
     msg, y_q = call(
         piece_kernel,
         "piece_image",
@@ -367,13 +381,13 @@
     y_p = lax.ppermute(y_q, axes, [(b, a) for a, b in enumerate(owner)])
     msg = lax.all_to_all(msg, "prow", 0, 0, tiled=True)
     coup = call(
-        coupling_kernel, "coupling", 8e9, (rc, small, linv), shape(W, W), [shape(NR, 16, W), shape(W, W), shape(W, W)], 3
+        coupling_kernel, "coupling", 8e9, (rc, small, linv), shape(W, W), [shape(NR, 8, W), shape(W, W), shape(W, W)], 3
     )
     vt = call(
         vectors_kernel,
         "vectors",
         6 * cols * W * W,
-        (rc, panel_c, linv),
+        (rc, small, linv),
         shape(2, W, cols, dtype=BF16),
         [shape(NR, piece, W), shape(W, W), shape(2, W, cols, dtype=BF16)],
         3,
@@ -384,8 +398,8 @@
         6 * cols * W * W,
         (rc, vt, msg, y_p),
         shape(NC, piece + W, W),
-        [shape(2, W, cols, dtype=BF16), shape(NR, piece, W), shape(W, W)],
-        2 + 2 * NC,
+        [shape(2, W, cols, dtype=BF16), shape(NR, piece, W), shape(W, W), shape(piece, W)],
+        3 + 2 * NC,
     )
     end = lax.all_to_all(end, "pcol", 0, 0, tiled=True)
     left, wide = call(

time: 203 us -> 181 us (0.89)
  blocking collectives: 18.2 us -> 0 us
  Pallas kernels: 84.9 us -> 70 us
  starting transfers between devices: 54.9 us -> 67.1 us
  waiting for transfers between devices: 34.2 us -> 31.9 us
    all_to_all x1 -> x0, blocking collectives: 18.2 us -> none  [on_device(): small = lax.all_to_all(small, 'prow', 0, 0, tiled=True)]
    pallas_call x10 -> x11, Pallas kernels: 84.9 us -> 70 us  [call(): pl.pallas_call(body, in_specs=[SM] + [HB] * (len(args) - 1), out_specs=[H...]
    all_to_all x1 -> x2, starting transfers between devices: 4.31 us -> 17.8 us  [on_device(): small = lax.all_to_all(small, 'prow', 0, 0, tiled=True)]
    all_to_all x1 -> x0, waiting for transfers between devices: 9.31 us -> none  [on_device(): panel_c = lax.all_to_all(spread(panel_q, NR), 'prow', 0, 0, tiled=True)]
    all_to_all x1 -> x2, waiting for transfers between devices: 6.69 us -> 11 us  [on_device(): small = lax.all_to_all(small, 'prow', 0, 0, tiled=True)]
    all_to_all x1 -> x0, starting transfers between devices: 3.7 us -> none  [on_device(): panel_c = lax.all_to_all(spread(panel_q, NR), 'prow', 0, 0, tiled=True)]
    ppermute x1, waiting for transfers between devices: 1.13 us -> 4 us  [on_device(): panel_q = lax.ppermute(mine, axes, list(enumerate(owner)))]
    all_to_all x1, starting transfers between devices: 6.93 us -> 9.61 us  [on_device(): end = lax.all_to_all(end, 'pcol', 0, 0, tiled=True)]
  transfers between devices with their start and end apart: 13 -> 13, of which waited for: 7 -> 7; matrix products, arithmetic and copies ran while one was open for 1% -> 1% of each run, Pallas kernels for 24% -> 26%
where the time goes in v3:
time: 181 us; the launch traced here: 180 us
  Pallas kernels  70 us (39%)
  starting transfers between devices  67.1 us (37%)
  waiting for transfers between devices  31.9 us (18%)
  local copies, waits for them, and re-layouts  7.45 us (4%)
  other arithmetic  2.64 us (1%)
    pallas_call x11, Pallas kernels, call(): pl.pallas_call(body, in_specs=[SM] + [HB] * (len(args) - 1), out_specs=[H...  70 us
    all_to_all x2, starting transfers between devices, on_device(): small = lax.all_to_all(small, 'prow', 0, 0, tiled=True)  17.8 us
    all_to_all x2, waiting for transfers between devices, on_device(): small = lax.all_to_all(small, 'prow', 0, 0, tiled=True)  11 us
    all_to_all x2, starting transfers between devices, on_device(): msg = lax.all_to_all(msg, 'prow', 0, 0, tiled=True)  10.3 us
    all_to_all x1, starting transfers between devices, on_device(): end = lax.all_to_all(end, 'pcol', 0, 0, tiled=True)  9.61 us
    all_to_all x1, starting transfers between devices, on_device(): f_msg = lax.all_to_all(f_msg, 'prow', 0, 0, tiled=True)  8.44 us
    ppermute x1, starting transfers between devices, on_device(): y_p = lax.ppermute(y_q, axes, [(b, a) for a, b in enumerate(owner)])  7 us
    unnamed x22, local copies, waits for them, and re-layouts  6.33 us
  transfers between devices with their start and end apart: 13, of which 7 were waited for; matrix products, arithmetic and copies ran while one was open for 1% of the time, Pallas kernels for 26%

profile of v3, /device:TPU:1, one launch (start us, length us, event | category | flops | bytes accessed | tf_op | source)
XLA Modules:
  0.0 179.6 jit_solution(11634979910723695758)
XLA Ops:
  0.0 1.1 fusion
  2.5 1.3 collective-permute-start
  4.4 3.6 %second.1 = f32[16,160,128]{2,1,0:T(8,128)} custom-call(s32[3]{0:T(128)} %pad_add_fusion.refs_0_, f32[1280,2560]{1,0:T(8,128)} %refs_1_.5), custom_call_target="tpu_custom_call" | custom-call | flops 128 | bytes 14417920 | tf_op jit(solution)/shard_map/second/pallas_call | solution.py:79
  8.0 8.4 %all-to-all-start = ((f32[16,160,128]{2,1,0:T(8,128)}), f32[16,160,128]{2,1,0:T(8,128)S(1)}, u32[]{:S(2)}, u32[]{:S(2)}) async-start(f32[16,160,128]{2,1,0:T(8,128)} %second.1), calls=%async_computation | async-start | bytes 2621440 | tf_op jit(solution)/shard_map/all_to_all | solution.py:332
  17.5 2.6 %collective-permute-start.3 = (f32[640,128]{1,0:T(8,128)S(1)}, f32[640,128]{1,0:T(8,128)S(1)}, u32[]{:S(2)}, u32[]{:S(2)}) collective-permute-start(f32[640,128]{1,0:T(8,128)S(1)} %select_select_fusion), channel_id=1, source_target_pairs={{0,7},{1,3},{2,4},{6,5},{8,15},{9,11},{10,12},{14,13},{16,23},{17,... | collective-permute-start | bytes 983048 | tf_op jit(solution)/shard_map/ppermute | solution.py:334
  20.2 4.0 %collective-permute-done.3 = f32[640,128]{1,0:T(8,128)S(1)} collective-permute-done((f32[640,128]{1,0:T(8,128)S(1)}, f32[640,128]{1,0:T(8,128)S(1)}, u32[]{:S(2)}, u32[]{:S(2)}) %collective-permute-start.3) | collective-permute-done | bytes 327712 | tf_op jit(solution)/shard_map/ppermute | solution.py:334
  24.2 4.6 %collective-permute-start.4 = (f32[640,128]{1,0:T(8,128)S(1)}, f32[640,128]{1,0:T(8,128)S(1)}, u32[]{:S(2)}, u32[]{:S(2)}) collective-permute-start(f32[640,128]{1,0:T(8,128)S(1)} %broadcast_select_fusion.refs_1_.refs_2_), channel_id=1, source_target_pairs={{0,1},{1,0},{2,3},{3,2},{4,5},{5,4},{6,7},{7,6},{8,9},{9,8},{10,11... | collective-permute-start | bytes 983048 | tf_op jit(solution)/shard_map/ppermute | solution.py:336
  28.8 1.3 collective-permute-done.4.refs_2_.refs_3_
  30.8 2.9 %gram.1 = f32[16,16,128]{2,1,0:T(8,128)} custom-call(s32[3]{0:T(128)} %pad_add_fusion.refs_0_, f32[640,128]{1,0:T(8,128)} %copy-done.5, f32[640,128]{1,0:T(8,128)} %copy-done.6), custom_call_target="tpu_custom_call" | custom-call | flops 125829120 | bytes 786432 | tf_op jit(solution)/shard_map/gram/pallas_call | solution.py:79
  33.7 6.9 %all-to-all-start.1 = ((f32[16,16,128]{2,1,0:T(8,128)}), f32[16,16,128]{2,1,0:T(8,128)S(1)}, u32[]{:S(2)}, u32[]{:S(2)}) async-start(f32[16,16,128]{2,1,0:T(8,128)} %gram.1), calls=%async_computation.1 | async-start | bytes 262144 | tf_op jit(solution)/shard_map/all_to_all | solution.py:348
  41.6 4.1 %collective-permute-start.5 = (f32[160,128]{1,0:T(8,128)S(1)}, f32[160,128]{1,0:T(8,128)S(1)}, u32[]{:S(2)}, u32[]{:S(2)}) collective-permute-start(f32[160,128]{1,0:T(8,128)S(1)} %dynamic-slice_select_fusion), channel_id=1, source_target_pairs={{0,0},{1,8},{2,16},{3,24},{4,32},{5,40},{6,48},{7,56},{8,64},{9,72... | collective-permute-start | bytes 245768 | tf_op jit(solution)/shard_map/ppermute | solution.py:344
  45.7 4.0 %collective-permute-done.5.refs_2_ = f32[160,128]{1,0:T(8,128)S(1)} collective-permute-done((f32[160,128]{1,0:T(8,128)S(1)}, f32[160,128]{1,0:T(8,128)S(1)}, u32[]{:S(2)}, u32[]{:S(2)}) %collective-permute-start.5) | collective-permute-done | bytes 81952 | tf_op jit(solution)/shard_map/ppermute | solution.py:344
  51.0 3.0 %mix.1 = f32[16,176,128]{2,1,0:T(8,128)} custom-call(s32[3]{0:T(128)} %pad_add_fusion.refs_0_, f32[16,16,128]{2,1,0:T(8,128)} %copy-done.7, f32[160,128]{1,0:T(8,128)} %copy-done.8), custom_call_target="tpu_custom_call" | custom-call | flops 32768 | bytes 1654784 | tf_op jit(solution)/shard_map/mix/pallas_call | solution.py:79
  54.0 10.9 %all-to-all-start.3 = ((f32[16,176,128]{2,1,0:T(8,128)}), f32[16,176,128]{2,1,0:T(8,128)S(1)}, u32[]{:S(2)}, u32[]{:S(2)}) async-start(f32[16,176,128]{2,1,0:T(8,128)} %mix.1), calls=%async_computation.3 | async-start | bytes 2883584 | tf_op jit(solution)/shard_map/all_to_all | solution.py:359
  64.8 7.8 %first_pass.1 = f32[16,160,128]{2,1,0:T(8,128)} custom-call(s32[3]{0:T(128)} %pad_add_fusion.refs_0_, f32[1280,2560]{1,0:T(8,128)} %refs_1_.5, f32[640,128]{1,0:T(8,128)} %copy-done.5, f32[640,128]{1,0:T(8,128)} %copy-done.6), custom_call_target="tpu_custom_call" | custom-call | flops 2516582400 | bytes 15073280 | tf_op jit(solution)/shard_map/first_pass/pallas_call | solution.py:79
  72.6 11.0 %all-to-all-done.3.refs_1_ = f32[16,176,128]{2,1,0:T(8,128)S(1)} async-done(((f32[16,176,128]{2,1,0:T(8,128)}), f32[16,176,128]{2,1,0:T(8,128)S(1)}, u32[]{:S(2)}, u32[]{:S(2)}) %all-to-all-start.3) | async-done | bytes 1441824 | tf_op jit(solution)/shard_map/all_to_all | solution.py:359
  83.6 1.1 copy-done
  84.7 4.5 %all-to-all-start.2 = ((f32[16,160,128]{2,1,0:T(8,128)}), f32[16,160,128]{2,1,0:T(8,128)S(1)}, u32[]{:S(2)}, u32[]{:S(2)}) async-start(f32[16,160,128]{2,1,0:T(8,128)} %first_pass.1), calls=%async_computation.2 | async-start | bytes 2621440 | tf_op jit(solution)/shard_map/all_to_all | solution.py:369
  89.3 12.0 %factor.1.refs_2_.refs_4_ = f32[128,128]{1,0:T(8,128)} custom-call(s32[3]{0:T(128)} %pad_add_fusion.refs_0_, f32[16,176,128]{2,1,0:T(8,128)} %copy-done), custom_call_target="tpu_custom_call" | custom-call | flops 8000000000 | bytes 1507328 | tf_op jit(solution)/shard_map/factor/pallas_call | solution.py:79
  101.3 4.9 %all-to-all-done.2.refs_1_ = f32[16,160,128]{2,1,0:T(8,128)S(1)} async-done(((f32[16,160,128]{2,1,0:T(8,128)}), f32[16,160,128]{2,1,0:T(8,128)S(1)}, u32[]{:S(2)}, u32[]{:S(2)}) %all-to-all-start.2) | async-done | bytes 1310752 | tf_op jit(solution)/shard_map/all_to_all | solution.py:369
  107.3 3.5 %piece_image.1 = (f32[16,160,128]{2,1,0:T(8,128)}, f32[160,128]{1,0:T(8,128)}) custom-call(s32[3]{0:T(128)} %pad_add_fusion.refs_0_, f32[16,160,128]{2,1,0:T(8,128)} %copy-done.3, f32[128,128]{1,0:T(8,128)} %factor.1.refs_2_.refs_4_, f32[16,160,128]{2,1,0:T(8,128)} %copy-done.1), custom_call_target="tpu_custom_call" | custom-call | flops 327680 | bytes 4079616 | tf_op jit(solution)/shard_map/piece_image/pallas_call | solution.py:79
  110.8 5.8 %all-to-all-start.4 = ((f32[16,160,128]{2,1,0:T(8,128)}), f32[16,160,128]{2,1,0:T(8,128)S(1)}, u32[]{:S(2)}, u32[]{:S(2)}) async-start(f32[16,160,128]{2,1,0:T(8,128)} %get-tuple-element.23), calls=%async_computation.4 | async-start | bytes 2621440 | tf_op jit(solution)/shard_map/all_to_all | solution.py:382
  116.6 7.0 %collective-permute-start.6 = (f32[160,128]{1,0:T(8,128)S(1)}, f32[160,128]{1,0:T(8,128)S(1)}, u32[]{:S(2)}, u32[]{:S(2)}) collective-permute-start(f32[160,128]{1,0:T(8,128)S(1)} %copy-done.10), channel_id=1, source_target_pairs={{0,0},{8,1},{16,2},{24,3},{32,4},{40,5},{48,6},{56,7},{64,8},{72,9... | collective-permute-start | bytes 245768 | tf_op jit(solution)/shard_map/ppermute | solution.py:381
  123.6 3.8 %vectors.1.refs_1_.refs_6_ = bf16[2,128,2560]{2,1,0:T(8,128)(2,1)} custom-call(s32[3]{0:T(128)} %pad_add_fusion.refs_0_, f32[16,176,128]{2,1,0:T(8,128)} %copy-done, f32[128,128]{1,0:T(8,128)} %factor.1.refs_2_.refs_4_), custom_call_target="tpu_custom_call" | custom-call | flops 251658240 | bytes 4128768 | tf_op jit(solution)/shard_map/vectors/pallas_call | solution.py:79
  127.5 5.4 %collective-permute-done.6.refs_3_ = f32[160,128]{1,0:T(8,128)S(1)} collective-permute-done((f32[160,128]{1,0:T(8,128)S(1)}, f32[160,128]{1,0:T(8,128)S(1)}, u32[]{:S(2)}, u32[]{:S(2)}) %collective-permute-start.6) | collective-permute-done | bytes 81952 | tf_op jit(solution)/shard_map/ppermute | solution.py:381
  132.8 1.4 all-to-all-done.4.refs_2_.refs_3_
  134.2 1.1 copy-done.2
  135.3 4.0 %inner.1 = f32[8,288,128]{2,1,0:T(8,128)} custom-call(s32[3]{0:T(128)} %pad_add_fusion.refs_0_, bf16[2,128,2560]{2,1,0:T(8,128)(2,1)} %vectors.1.refs_1_.refs_6_, f32[16,160,128]{2,1,0:T(8,128)} %copy-done.2, f32[160,128]{1,0:T(8,128)} %copy-done.9), custom_call_target="tpu_custom_call" | custom-call | flops 251658240 | bytes 5193728 | tf_op jit(solution)/shard_map/inner/pallas_call | solution.py:79
  139.3 9.6 %all-to-all-start.5 = ((f32[8,288,128]{2,1,0:T(8,128)}), f32[8,288,128]{2,1,0:T(8,128)S(1)}, u32[]{:S(2)}, u32[]{:S(2)}) async-start(f32[8,288,128]{2,1,0:T(8,128)} %inner.1), calls=%async_computation.5 | async-start | bytes 2359296 | tf_op jit(solution)/shard_map/all_to_all | solution.py:404
  148.9 13.2 %coupling.1.refs_5_.refs_3_ = f32[128,128]{1,0:T(8,128)} custom-call(s32[3]{0:T(128)} %pad_add_fusion.refs_0_, f32[16,176,128]{2,1,0:T(8,128)} %copy-done, f32[128,128]{1,0:T(8,128)} %factor.1.refs_2_.refs_4_), custom_call_target="tpu_custom_call" | custom-call | flops 8000000000 | bytes 1572864 | tf_op jit(solution)/shard_map/coupling/pallas_call | solution.py:79
  162.1 4.2 %sides.1 = (bf16[2,1280,128]{2,1,0:T(8,128)(2,1)}, f32[128,2560]{1,0:T(8,128)}) custom-call(s32[3]{0:T(128)} %pad_add_fusion.refs_0_, f32[640,128]{1,0:T(8,128)} %copy-done.5, f32[640,128]{1,0:T(8,128)} %copy-done.6, f32[16,160,128]{2,1,0:T(8,128)} %copy-done.2, f32[128,128]{1,0:T(8,128)} %factor.1.refs_2_.refs_4_, f32[128,128]{1,0:T(8,128)} %coupling.1.refs_5_.refs_3_), custom_call_target="tpu_custom_call" | custom-call | flops 754974720 | bytes 4718592 | tf_op jit(solution)/shard_map/sides/pallas_call | solution.py:79
  167.3 12.1 %last_pass.1 = f32[1280,2560]{1,0:T(8,128)} custom-call(s32[3]{0:T(128)} %pad_add_fusion.refs_0_, f32[1280,2560]{1,0:T(8,128)} %refs_1_.5, f32[8,288,128]{2,1,0:T(8,128)} %copy-done.4, f32[128,128]{1,0:T(8,128)} %coupling.1.refs_5_.refs_3_, bf16[2,1280,128]{2,1,0:T(8,128)(2,1)} %get-tuple-element.25.refs_4_, f32[128,2560]{1,0:T(8,128)} %get-tuple-element.26.refs_5_, ...), custom_call_target="tpu_custom_call" | custom-call | flops 5033164800 | bytes 32702464 | tf_op jit(solution)/shard_map/last_pass/pallas_call | solution.py:79
  (32 shorter events, 8.2 us)
Async XLA Ops:
  1.1 15.4 %collective-permute-start.1 = (f32[640,128]{1,0:T(8,128)S(1)}, f32[640,128]{1,0:T(8,128)S(1)}, u32[]{:S(2)}, u32[]{:S(2)}) collective-permute-start(f32[640,128]{1,0:T(8,128)S(1)} %get-tuple-element.27), channel_id=1, source_target_pairs={{0,2},{8,10},{16,18},{24,26},{32,34},{40,42},{48,50},{56,58},{64,6... | collective-permute-start | bytes 983048 | tf_op jit(solution)/shard_map/ppermute | solution.py:327
  1.8 14.7 %collective-permute-start.2 = (f32[640,128]{1,0:T(8,128)S(1)}, f32[640,128]{1,0:T(8,128)S(1)}, u32[]{:S(2)}, u32[]{:S(2)}) collective-permute-start(f32[640,128]{1,0:T(8,128)S(1)} %get-tuple-element.28), channel_id=1, source_target_pairs={{0,6},{8,14},{16,22},{24,30},{32,38},{40,46},{48,54},{56,62},{64,7... | collective-permute-start | bytes 983048 | tf_op jit(solution)/shard_map/ppermute | solution.py:328
  2.5 14.0 %collective-permute-start = (f32[640,128]{1,0:T(8,128)S(1)}, f32[640,128]{1,0:T(8,128)S(1)}, u32[]{:S(2)}, u32[]{:S(2)}) collective-permute-start(f32[640,128]{1,0:T(8,128)S(1)} %get-tuple-element.28), channel_id=1, source_target_pairs={{0,1},{8,9},{16,17},{24,25},{32,33},{40,41},{48,49},{56,57},{64,65... | collective-permute-start | bytes 983048 | tf_op jit(solution)/shard_map/ppermute | solution.py:326
  8.0 25.6 %all-to-all-start = ((f32[16,160,128]{2,1,0:T(8,128)}), f32[16,160,128]{2,1,0:T(8,128)S(1)}, u32[]{:S(2)}, u32[]{:S(2)}) async-start(f32[16,160,128]{2,1,0:T(8,128)} %second.1), calls=%async_computation | async-start | bytes 2621440 | tf_op jit(solution)/shard_map/all_to_all | solution.py:332
  17.5 6.6 %collective-permute-start.3 = (f32[640,128]{1,0:T(8,128)S(1)}, f32[640,128]{1,0:T(8,128)S(1)}, u32[]{:S(2)}, u32[]{:S(2)}) collective-permute-start(f32[640,128]{1,0:T(8,128)S(1)} %select_select_fusion), channel_id=1, source_target_pairs={{0,7},{1,3},{2,4},{6,5},{8,15},{9,11},{10,12},{14,13},{16,23},{17,... | collective-permute-start | bytes 983048 | tf_op jit(solution)/shard_map/ppermute | solution.py:334
  24.2 5.9 %copy-start.5 = (f32[640,128]{1,0:T(8,128)}, f32[640,128]{1,0:T(8,128)S(1)}, u32[]{:S(2)}) copy-start(f32[640,128]{1,0:T(8,128)S(1)} %broadcast_select_fusion.refs_1_.refs_2_) | copy-start | bytes 983044
  24.2 5.8 %collective-permute-start.4 = (f32[640,128]{1,0:T(8,128)S(1)}, f32[640,128]{1,0:T(8,128)S(1)}, u32[]{:S(2)}, u32[]{:S(2)}) collective-permute-start(f32[640,128]{1,0:T(8,128)S(1)} %broadcast_select_fusion.refs_1_.refs_2_), channel_id=1, source_target_pairs={{0,1},{1,0},{2,3},{3,2},{4,5},{5,4},{6,7},{7,6},{8,9},{9,8},{10,11... | collective-permute-start | bytes 983048 | tf_op jit(solution)/shard_map/ppermute | solution.py:336
  30.0 0.7 copy-start.6
  33.7 20.3 %copy-start.1 = (f32[16,160,128]{2,1,0:T(8,128)}, f32[16,160,128]{2,1,0:T(8,128)S(1)}, u32[]{:S(2)}) copy-start(f32[16,160,128]{2,1,0:T(8,128)S(1)} %all-to-all-done.refs_3_) | copy-start | bytes 3932164
  33.7 16.0 %all-to-all-start.1 = ((f32[16,16,128]{2,1,0:T(8,128)}), f32[16,16,128]{2,1,0:T(8,128)S(1)}, u32[]{:S(2)}, u32[]{:S(2)}) async-start(f32[16,16,128]{2,1,0:T(8,128)} %gram.1), calls=%async_computation.1 | async-start | bytes 262144 | tf_op jit(solution)/shard_map/all_to_all | solution.py:348
  41.6 8.1 %collective-permute-start.5 = (f32[160,128]{1,0:T(8,128)S(1)}, f32[160,128]{1,0:T(8,128)S(1)}, u32[]{:S(2)}, u32[]{:S(2)}) collective-permute-start(f32[160,128]{1,0:T(8,128)S(1)} %dynamic-slice_select_fusion), channel_id=1, source_target_pairs={{0,0},{1,8},{2,16},{3,24},{4,32},{5,40},{6,48},{7,56},{8,64},{9,72... | collective-permute-start | bytes 245768 | tf_op jit(solution)/shard_map/ppermute | solution.py:344
  49.7 0.6 copy-start.8
  50.3 0.6 copy-start.7
  54.0 29.7 %all-to-all-start.3 = ((f32[16,176,128]{2,1,0:T(8,128)}), f32[16,176,128]{2,1,0:T(8,128)S(1)}, u32[]{:S(2)}, u32[]{:S(2)}) async-start(f32[16,176,128]{2,1,0:T(8,128)} %mix.1), calls=%async_computation.3 | async-start | bytes 2883584 | tf_op jit(solution)/shard_map/all_to_all | solution.py:359
  83.6 1.1 copy-start
  84.7 21.5 %all-to-all-start.2 = ((f32[16,160,128]{2,1,0:T(8,128)}), f32[16,160,128]{2,1,0:T(8,128)S(1)}, u32[]{:S(2)}, u32[]{:S(2)}) async-start(f32[16,160,128]{2,1,0:T(8,128)} %first_pass.1), calls=%async_computation.2 | async-start | bytes 2621440 | tf_op jit(solution)/shard_map/all_to_all | solution.py:369
  106.2 1.1 copy-start.3
  110.8 5.8 %copy-start.10 = (f32[160,128]{1,0:T(8,128)S(1)}, f32[160,128]{1,0:T(8,128)}, u32[]{:S(2)}) copy-start(f32[160,128]{1,0:T(8,128)} %get-tuple-element.24) | copy-start | bytes 245764
  110.8 23.4 %all-to-all-start.4 = ((f32[16,160,128]{2,1,0:T(8,128)}), f32[16,160,128]{2,1,0:T(8,128)S(1)}, u32[]{:S(2)}, u32[]{:S(2)}) async-start(f32[16,160,128]{2,1,0:T(8,128)} %get-tuple-element.23), calls=%async_computation.4 | async-start | bytes 2621440 | tf_op jit(solution)/shard_map/all_to_all | solution.py:382
  116.6 16.2 %collective-permute-start.6 = (f32[160,128]{1,0:T(8,128)S(1)}, f32[160,128]{1,0:T(8,128)S(1)}, u32[]{:S(2)}, u32[]{:S(2)}) collective-permute-start(f32[160,128]{1,0:T(8,128)S(1)} %copy-done.10), channel_id=1, source_target_pairs={{0,0},{8,1},{16,2},{24,3},{32,4},{40,5},{48,6},{56,7},{64,8},{72,9... | collective-permute-start | bytes 245768 | tf_op jit(solution)/shard_map/ppermute | solution.py:381
  132.8 1.4 copy-start.9
  134.2 1.1 copy-start.2
  139.3 27.0 %all-to-all-start.5 = ((f32[8,288,128]{2,1,0:T(8,128)}), f32[8,288,128]{2,1,0:T(8,128)S(1)}, u32[]{:S(2)}, u32[]{:S(2)}) async-start(f32[8,288,128]{2,1,0:T(8,128)} %inner.1), calls=%async_computation.5 | async-start | bytes 2359296 | tf_op jit(solution)/shard_map/all_to_all | solution.py:404
  166.3 1.0 copy-start.4

commit v4 on v3

--- a/solution.py
+++ b/solution.py
@@ -10,6 +10,7 @@
 NC = 8
 STEP = 256
 WIDE = 512
+LIMITS = {"gram": 20, "mix": 20, "factor": 20, "second": 52, "first_pass": 52}
 F32 = jnp.float32
 BF16 = jnp.bfloat16
 SM = pl.BlockSpec(memory_space=pltpu.SMEM)
@@ -60,6 +61,7 @@
 
 
 def call(kernel, name, flops, args, outs, scratch, sems):
+    limit = LIMITS.get(name, 60)
     single = not isinstance(outs, list)
     out_list = [outs] if single else outs
     size = sum(4 * a.size for a in args[1:]) + sum(4 * o.size for o in out_list)
@@ -78,11 +80,11 @@
 
     result = pl.pallas_call(
         body,
-        in_specs=[SM] + [HB] * (len(args) - 1),
+        in_specs=[SM] + [pl.BlockSpec(memory_space=pl.ANY)] * (len(args) - 1),
         out_specs=[HB] * len(out_list),
         out_shape=out_list,
         scratch_shapes=[pltpu.VMEM(s.shape, s.dtype) for s in scratch] + [pltpu.SemaphoreType.DMA((sems,))],
-        compiler_params=pltpu.CompilerParams(vmem_limit_bytes=60 * 1024 * 1024),
+        compiler_params=pltpu.CompilerParams(vmem_limit_bytes=limit * 1024 * 1024),
         cost_estimate=pl.CostEstimate(flops=int(flops), bytes_accessed=int(size), transcendentals=0),
         name=name,
     )(*args)
@@ -231,8 +233,9 @@
 
 
 def vectors_kernel(rc, ins, outs, bufs, copy):
-    msg, linv, v = bufs
-    cols = v.shape[2]
+    msg, linv, v, panel, left = bufs
+    cols, rows = v.shape[2], panel.shape[0]
+    more = load_panel(rc, ins[2], ins[3], panel, copy)
     p = msg.reshape(cols, W)
     wait(run([copy(ins[0].at[:, pl.ds(0, msg.shape[1])], msg), copy(ins[1], linv)]))
     ls = split(linv[...])
@@ -242,7 +245,15 @@
         x = three(ls, split(p[sl]), 1, 1)
         x = jnp.where(at < 0, 0.0, x) - jnp.where(at == iota2((W, WIDE), 0), 1.0, 0.0)
         v[0, :, sl], v[1, :, sl] = split(x)
-    wait(run([copy(v, outs[0])]))
+    last = run([copy(v, outs[0])])
+    wait(more)
+    clear_top(rc, panel)
+    for k in range(rows // STEP):
+        sl = slice(k * STEP, (k + 1) * STEP)
+        ids = rc[0] * rows + k * STEP + iota2((STEP, W), 0)
+        x = three(split(panel[sl]), ls, 1, 1) - jnp.where(ids - W == iota2((STEP, W), 1), 1.0, 0.0)
+        left[0, sl], left[1, sl] = split(x)
+    wait(last + run([copy(left, outs[1])]))
 
 
 def inner_kernel(rc, ins, outs, bufs, copy):
@@ -257,26 +268,15 @@
 
 
 def sides_kernel(rc, ins, outs, bufs, copy):
-    held, other, y_c, linv_ref, coup_ref = ins
-    panel, yc, linv, coup, left, wide = bufs
-    rows, cols = panel.shape[0], wide.shape[1]
-    small = run([copy(linv_ref, linv), copy(coup_ref, coup), copy(y_c, yc)])
-    more = load_panel(rc, held, other, panel, copy)
-    wait(small)
-    ls, cs = split(linv[...]), split(coup[...])
+    yc, coup, wide = bufs
+    cols = wide.shape[1]
+    wait(run([copy(ins[0], yc), copy(ins[1], coup)]))
+    cs = split(coup[...])
     flat = yc.reshape(cols, W)
     for b in range(cols // WIDE):
         sl = slice(b * WIDE, (b + 1) * WIDE)
         wide[:, sl] = three(cs, split(flat[sl]), 1, 1)
-    last = run([copy(wide, outs[1])])
-    wait(more)
-    clear_top(rc, panel)
-    for k in range(rows // STEP):
-        sl = slice(k * STEP, (k + 1) * STEP)
-        ids = rc[0] * rows + k * STEP + iota2((STEP, W), 0)
-        v = three(split(panel[sl]), ls, 1, 1) - jnp.where(ids - W == iota2((STEP, W), 1), 1.0, 0.0)
-        left[0, sl], left[1, sl] = split(v)
-    wait(last + run([copy(left, outs[0])]))
+    wait(run([copy(wide, outs[0])]))
 
 
 def last_kernel(rc, ins, outs, bufs, copy):
@@ -286,8 +286,10 @@
     piece = yr.shape[1]
     n = cols // WIDE
     small = run([copy(msg_ref.at[:, pl.ds(piece, W)], s), copy(coup_ref, coup)])
-    lefts = run([copy(msg_ref.at[:, pl.ds(0, piece)], yr), copy(left_ref, left.at[:, :, pl.ds(0, W)])])
-    mid = run([copy(v_ref, right.at[:, pl.ds(W, W)]), copy(wide_ref, wide)])
+    lefts = run([copy(msg_ref.at[:, pl.ds(0, piece)], yr)])
+    for i, part in enumerate((0, 1, 0)):
+        lefts += run([copy(left_ref.at[part], left.at[:, pl.ds(2 * i * W, W)])])
+    mid = run([copy(v_ref, right), copy(wide_ref, wide)])
     cut = [pl.ds(k * WIDE, WIDE) for k in range(n)]
     copies = run([copy(a_ref.at[:, cut[k]], buf.at[:, cut[k]]) for k in range(n)])
     wait(small)
@@ -295,18 +297,18 @@
     middle = three(split(three(cs, split(jnp.sum(s[...], 0)), 1, 0)), cs, 1, 1)
     ms = split(0.5 * (middle + middle.T))
     wait(lefts)
-    left[0, :, W:], left[1, :, W:] = split(three(split(yr[...].reshape(rows, W)), cs, 1, 1))
+    high, low = split(three(split(yr[...].reshape(rows, W)), cs, 1, 1))
+    for i, part in enumerate((high, low, high)):
+        left[:, (2 * i + 1) * W : (2 * i + 2) * W] = part
     wait(mid)
-    lh, ll = left[0], left[1]
     ends = []
     for k in range(n):
         sl = slice(k * WIDE, (k + 1) * WIDE)
-        vh, vl = right[0, W:, sl], right[1, W:, sl]
+        vh, vl = right[0, :, sl], right[1, :, sl]
         wh, wl = split(wide[:, sl] - three(ms, (vh, vl), 1, 0))
-        rh = jnp.concatenate([wh, vh], 0)
-        rl = jnp.concatenate([wl, vl], 0)
+        three_parts = jnp.concatenate([wh, vh, wh, vh, wl, vl], 0)
         copies[k].wait()
-        buf[:, sl] -= bdot(lh, rh, 1, 0) + (bdot(ll, rh, 1, 0) + bdot(lh, rl, 1, 0))
+        buf[:, sl] -= bdot(left[...], three_parts, 1, 0)
         ends += run([copy(buf.at[:, cut[k]], outs[0].at[:, cut[k]])])
     wait(ends)
 
@@ -329,12 +331,14 @@
     f_msg = call(
         second_kernel, "second", W, (rc, matrix), shape(NR, piece, W), [shape(W, cols), shape(cols, W)], 1 + NR
     )
+    send = jnp.where(c == 0, top, jnp.where(c == 1, to1, jnp.where(c == 2, to2, to6)))
+    f_msg, send = lax.optimization_barrier((f_msg, send))
     f_msg = lax.all_to_all(f_msg, "prow", 0, 0, tiled=True)
-    send = jnp.where(c == 0, top, jnp.where(c == 1, to1, jnp.where(c == 2, to2, to6)))
     got = lax.ppermute(send, "pcol", [(0, 7), (1, 3), (2, 4), (6, 5)])
     held = jnp.where((c == 0) | (c == 1) | (c == 2) | (c == 6), send, got)
     other = lax.ppermute(held, "pcol", [(i, i ^ 1) for i in range(NC)])
     owner = [(8 * ((g // NC) % 2) + g % NC) * NC + (g // NC) // 2 for g in range(NR * NC)]
+
     at = (c % (NC // 2)) * piece
     mine = jnp.where(
         (c < NC // 2) == holds_top,
@@ -383,14 +387,20 @@
     coup = call(
         coupling_kernel, "coupling", 8e9, (rc, small, linv), shape(W, W), [shape(NR, 8, W), shape(W, W), shape(W, W)], 3
     )
-    vt = call(
+    vt, left = call(
         vectors_kernel,
         "vectors",
-        6 * cols * W * W,
-        (rc, small, linv),
-        shape(2, W, cols, dtype=BF16),
-        [shape(NR, piece, W), shape(W, W), shape(2, W, cols, dtype=BF16)],
-        3,
+        6 * (rows + cols) * W * W,
+        (rc, small, linv, held, other),
+        [shape(2, W, cols, dtype=BF16), shape(2, rows, W, dtype=BF16)],
+        [
+            shape(NR, piece, W),
+            shape(W, W),
+            shape(2, W, cols, dtype=BF16),
+            shape(rows, W),
+            shape(2, rows, W, dtype=BF16),
+        ],
+        6,
     )
     end = call(
         inner_kernel,
@@ -402,21 +412,14 @@
         3 + 2 * NC,
     )
     end = lax.all_to_all(end, "pcol", 0, 0, tiled=True)
-    left, wide = call(
+    wide = call(
         sides_kernel,
         "sides",
-        12 * (rows + cols) * W * W,
-        (rc, held, other, msg, linv, coup),
-        [shape(2, rows, W, dtype=BF16), shape(W, cols)],
-        [
-            shape(rows, W),
-            shape(NR, piece, W),
-            shape(W, W),
-            shape(W, W),
-            shape(2, rows, W, dtype=BF16),
-            shape(W, cols),
-        ],
-        7,
+        6 * cols * W * W,
+        (rc, msg, coup),
+        shape(W, cols),
+        [shape(NR, piece, W), shape(W, W), shape(W, cols)],
+        3,
     )
     return call(
         last_kernel,
@@ -429,11 +432,11 @@
             shape(NC, W, W),
             shape(W, W),
             shape(NC, piece, W),
-            shape(2, rows, 2 * W, dtype=BF16),
+            shape(rows, 6 * W, dtype=BF16),
             shape(W, cols),
-            shape(2, 2 * W, cols, dtype=BF16),
+            shape(2, W, cols, dtype=BF16),
         ],
-        6 + 2 * (cols // WIDE),
+        8 + 2 * (cols // WIDE),
     )
 
 

time: 181 us -> 176 us (0.972)
  waiting for transfers between devices: 31.9 us -> 38.1 us
  starting transfers between devices: 67.1 us -> 63.2 us
  Pallas kernels: 70 us -> 66.7 us
  local copies, waits for them, and re-layouts: 7.45 us -> 4.96 us
    all_to_all x2, starting transfers between devices: 17.8 us -> 12.6 us  [on_device(): small = lax.all_to_all(small, 'prow', 0, 0, tiled=True)]
    all_to_all x1, waiting for transfers between devices: 0.01 us -> 4.89 us  [on_device(): f_msg = lax.all_to_all(f_msg, 'prow', 0, 0, tiled=True)]
    pallas_call x11, Pallas kernels: 70 us -> 66.7 us  [call(): pl.pallas_call(body, in_specs=[SM] + [pl.BlockSpec(memory_space=pl.ANY)]...]
    ppermute x1, waiting for transfers between devices: 0.01 us -> 3.28 us  [on_device(): to1 = lax.ppermute(bot, 'pcol', [(0, 1)])]
    all_to_all x2, starting transfers between devices: 10.3 us -> 13.1 us  [on_device(): msg = lax.all_to_all(msg, 'prow', 0, 0, tiled=True)]
    unnamed x22, local copies, waits for them, and re-layouts: 6.33 us -> 3.84 us
    all_to_all x2, waiting for transfers between devices: 11 us -> 8.7 us  [on_device(): small = lax.all_to_all(small, 'prow', 0, 0, tiled=True)]
    ppermute x1, starting transfers between devices: 4.08 us -> 6.1 us  [on_device(): panel_q = lax.ppermute(mine, axes, list(enumerate(owner)))]
  transfers between devices with their start and end apart: 13 -> 13, of which waited for: 7 -> 9; matrix products, arithmetic and copies ran while one was open for 1% -> 0% of each run, Pallas kernels for 26% -> 26%
where the time goes in v4:
time: 176 us; the launch traced here: 175 us
  Pallas kernels  66.7 us (38%)
  starting transfers between devices  63.2 us (36%)
  waiting for transfers between devices  38.1 us (22%)
  local copies, waits for them, and re-layouts  4.96 us (3%)
    pallas_call x11, Pallas kernels, call(): pl.pallas_call(body, in_specs=[SM] + [pl.BlockSpec(memory_space=pl.ANY)]...  66.7 us
    all_to_all x2, starting transfers between devices, on_device(): msg = lax.all_to_all(msg, 'prow', 0, 0, tiled=True)  13.1 us
    all_to_all x2, starting transfers between devices, on_device(): small = lax.all_to_all(small, 'prow', 0, 0, tiled=True)  12.6 us
    all_to_all x1, starting transfers between devices, on_device(): end = lax.all_to_all(end, 'pcol', 0, 0, tiled=True)  9.4 us
    all_to_all x2, waiting for transfers between devices, on_device(): small = lax.all_to_all(small, 'prow', 0, 0, tiled=True)  8.7 us
    all_to_all x1, starting transfers between devices, on_device(): f_msg = lax.all_to_all(f_msg, 'prow', 0, 0, tiled=True)  7.61 us
    all_to_all x2, waiting for transfers between devices, on_device(): msg = lax.all_to_all(msg, 'prow', 0, 0, tiled=True)  7.1 us
    ppermute x1, starting transfers between devices, on_device(): y_p = lax.ppermute(y_q, axes, [(b, a) for a, b in enumerate(owner)])  6.98 us
  transfers between devices with their start and end apart: 13, of which 9 were waited for; matrix products, arithmetic and copies ran while one was open for 0% of the time, Pallas kernels for 26%

profile of v4, /device:TPU:1, one launch (start us, length us, event | category | flops | bytes accessed | tf_op | source)
XLA Modules:
  0.0 174.7 jit_solution(1236874021659876)
XLA Ops:
  0.0 1.1 fusion
  2.5 1.3 collective-permute-start
  3.9 3.4 %second.1 = f32[16,160,128]{2,1,0:T(8,128)} custom-call(s32[3]{0:T(128)S(1)} %pad_add_fusion.refs_0_, f32[1280,2560]{1,0:T(8,128)} %refs_1_.5), custom_call_target="tpu_custom_call" | custom-call | flops 128 | bytes 14417920 | tf_op jit(solution)/shard_map/second/pallas_call | solution.py:81
  7.4 3.3 %collective-permute-done = f32[640,128]{1,0:T(8,128)S(1)} collective-permute-done((f32[640,128]{1,0:T(8,128)S(1)}, f32[640,128]{1,0:T(8,128)S(1)}, u32[]{:S(2)}, u32[]{:S(2)}) %collective-permute-start) | collective-permute-done | bytes 327712 | tf_op jit(solution)/shard_map/ppermute | solution.py:328
  11.7 7.6 %all-to-all-start = ((f32[16,160,128]{2,1,0:T(8,128)}), f32[16,160,128]{2,1,0:T(8,128)S(1)}, u32[]{:S(2)}, u32[]{:S(2)}) async-start(f32[16,160,128]{2,1,0:T(8,128)} %second.1), calls=%async_computation | async-start | bytes 2621440 | tf_op jit(solution)/shard_map/all_to_all | solution.py:336
  19.4 1.3 collective-permute-start.3
  20.7 4.0 %collective-permute-done.3 = f32[640,128]{1,0:T(8,128)S(1)} collective-permute-done((f32[640,128]{1,0:T(8,128)S(1)}, f32[640,128]{1,0:T(8,128)S(1)}, u32[]{:S(2)}, u32[]{:S(2)}) %collective-permute-start.3) | collective-permute-done | bytes 327712 | tf_op jit(solution)/shard_map/ppermute | solution.py:337
  24.7 3.4 %collective-permute-start.4 = (f32[640,128]{1,0:T(8,128)S(1)}, f32[640,128]{1,0:T(8,128)S(1)}, u32[]{:S(2)}, u32[]{:S(2)}) collective-permute-start(f32[640,128]{1,0:T(8,128)S(1)} %broadcast_select_fusion.refs_1_.refs_2_.refs_3_), channel_id=1, source_target_pairs={{0,1},{1,0},{2,3},{3,2},{4,5},{5,4},{6,7},{7,6},{8,9},{9,8},{10,11... | collective-permute-start | bytes 983048 | tf_op jit(solution)/shard_map/ppermute | solution.py:339
  28.1 1.3 collective-permute-done.4.refs_2_.refs_3_.refs_4_
  29.4 1.9 %gram.1 = f32[16,16,128]{2,1,0:T(8,128)} custom-call(s32[3]{0:T(128)S(1)} %pad_add_fusion.refs_0_, f32[640,128]{1,0:T(8,128)S(1)} %broadcast_select_fusion.refs_1_.refs_2_.refs_3_, f32[640,128]{1,0:T(8,128)S(1)} %collective-permute-done.4.refs_2_.refs_3_.refs_4_), custom_call_target="tpu_custom_call" | custom-call | flops 125829120 | bytes 786432 | tf_op jit(solution)/shard_map/gram/pallas_call | solution.py:81
  31.3 4.9 %all-to-all-done.refs_3_ = f32[16,160,128]{2,1,0:T(8,128)S(1)} async-done(((f32[16,160,128]{2,1,0:T(8,128)}), f32[16,160,128]{2,1,0:T(8,128)S(1)}, u32[]{:S(2)}, u32[]{:S(2)}) %all-to-all-start) | async-done | bytes 1310752 | tf_op jit(solution)/shard_map/all_to_all | solution.py:336
  36.2 5.3 %all-to-all-start.1 = ((f32[16,16,128]{2,1,0:T(8,128)}), f32[16,16,128]{2,1,0:T(8,128)S(1)}, u32[]{:S(2)}, u32[]{:S(2)}) async-start(f32[16,16,128]{2,1,0:T(8,128)} %gram.1), calls=%async_computation.1 | async-start | bytes 262144 | tf_op jit(solution)/shard_map/all_to_all | solution.py:352
  41.5 6.1 %collective-permute-start.5 = (f32[160,128]{1,0:T(8,128)S(1)}, f32[160,128]{1,0:T(8,128)S(1)}, u32[]{:S(2)}, u32[]{:S(2)}) collective-permute-start(f32[160,128]{1,0:T(8,128)S(1)} %dynamic-slice_select_fusion), channel_id=1, source_target_pairs={{0,0},{1,8},{2,16},{3,24},{4,32},{5,40},{6,48},{7,56},{8,64},{9,72... | collective-permute-start | bytes 245768 | tf_op jit(solution)/shard_map/ppermute | solution.py:348
  47.6 4.0 %collective-permute-done.5.refs_2_ = f32[160,128]{1,0:T(8,128)S(1)} collective-permute-done((f32[160,128]{1,0:T(8,128)S(1)}, f32[160,128]{1,0:T(8,128)S(1)}, u32[]{:S(2)}, u32[]{:S(2)}) %collective-permute-start.5) | collective-permute-done | bytes 81952 | tf_op jit(solution)/shard_map/ppermute | solution.py:348
  51.7 2.2 %mix.1 = f32[16,176,128]{2,1,0:T(8,128)} custom-call(s32[3]{0:T(128)S(1)} %pad_add_fusion.refs_0_, f32[16,16,128]{2,1,0:T(8,128)S(1)} %all-to-all-done.1.refs_1_, f32[160,128]{1,0:T(8,128)S(1)} %collective-permute-done.5.refs_2_), custom_call_target="tpu_custom_call" | custom-call | flops 32768 | bytes 1654784 | tf_op jit(solution)/shard_map/mix/pallas_call | solution.py:81
  53.9 7.3 %all-to-all-start.3 = ((f32[16,176,128]{2,1,0:T(8,128)}), f32[16,176,128]{2,1,0:T(8,128)S(1)}, u32[]{:S(2)}, u32[]{:S(2)}) async-start(f32[16,176,128]{2,1,0:T(8,128)} %mix.1), calls=%async_computation.3 | async-start | bytes 2883584 | tf_op jit(solution)/shard_map/all_to_all | solution.py:363
  61.3 7.7 %first_pass.1 = f32[16,160,128]{2,1,0:T(8,128)} custom-call(s32[3]{0:T(128)S(1)} %pad_add_fusion.refs_0_, f32[1280,2560]{1,0:T(8,128)} %refs_1_.5, f32[640,128]{1,0:T(8,128)S(1)} %broadcast_select_fusion.refs_1_.refs_2_.refs_3_, f32[640,128]{1,0:T(8,128)S(1)} %collective-permute-done.4.refs_2_.refs_3_.refs_4_), custom_call_target="tpu_custom_call" | custom-call | flops 2516582400 | bytes 15073280 | tf_op jit(solution)/shard_map/first_pass/pallas_call | solution.py:81
  68.9 8.7 %all-to-all-done.3.refs_1_ = f32[16,176,128]{2,1,0:T(8,128)S(1)} async-done(((f32[16,176,128]{2,1,0:T(8,128)}), f32[16,176,128]{2,1,0:T(8,128)S(1)}, u32[]{:S(2)}, u32[]{:S(2)}) %all-to-all-start.3) | async-done | bytes 1441824 | tf_op jit(solution)/shard_map/all_to_all | solution.py:363
  77.6 7.2 %all-to-all-start.2 = ((f32[16,160,128]{2,1,0:T(8,128)}), f32[16,160,128]{2,1,0:T(8,128)S(1)}, u32[]{:S(2)}, u32[]{:S(2)}) async-start(f32[16,160,128]{2,1,0:T(8,128)} %first_pass.1), calls=%async_computation.2 | async-start | bytes 2621440 | tf_op jit(solution)/shard_map/all_to_all | solution.py:373
  84.8 10.5 %factor.1.refs_2_ = f32[128,128]{1,0:T(8,128)S(1)} custom-call(s32[3]{0:T(128)S(1)} %pad_add_fusion.refs_0_, f32[16,176,128]{2,1,0:T(8,128)S(1)} %all-to-all-done.3.refs_1_), custom_call_target="tpu_custom_call" | custom-call | flops 8000000000 | bytes 1507328 | tf_op jit(solution)/shard_map/factor/pallas_call | solution.py:81
  96.0 5.7 %all-to-all-done.2.refs_1_ = f32[16,160,128]{2,1,0:T(8,128)S(1)} async-done(((f32[16,160,128]{2,1,0:T(8,128)}), f32[16,160,128]{2,1,0:T(8,128)S(1)}, u32[]{:S(2)}, u32[]{:S(2)}) %all-to-all-start.2) | async-done | bytes 1310752 | tf_op jit(solution)/shard_map/all_to_all | solution.py:373
  102.8 3.5 %piece_image.1 = (f32[16,160,128]{2,1,0:T(8,128)}, f32[160,128]{1,0:T(8,128)}) custom-call(s32[3]{0:T(128)} %copy-done.4, f32[16,160,128]{2,1,0:T(8,128)} %copy-done.7, f32[128,128]{1,0:T(8,128)} %copy-done.3, f32[16,160,128]{2,1,0:T(8,128)} %copy-done.6), custom_call_target="tpu_custom_call" | custom-call | flops 327680 | bytes 4079616 | tf_op jit(solution)/shard_map/piece_image/pallas_call | solution.py:81
  106.3 6.0 %all-to-all-start.4 = ((f32[16,160,128]{2,1,0:T(8,128)}), f32[16,160,128]{2,1,0:T(8,128)S(1)}, u32[]{:S(2)}, u32[]{:S(2)}) async-start(f32[16,160,128]{2,1,0:T(8,128)} %get-tuple-element.28), calls=%async_computation.4 | async-start | bytes 2621440 | tf_op jit(solution)/shard_map/all_to_all | solution.py:386
  112.2 7.0 %collective-permute-start.6 = (f32[160,128]{1,0:T(8,128)S(1)}, f32[160,128]{1,0:T(8,128)S(1)}, u32[]{:S(2)}, u32[]{:S(2)}) collective-permute-start(f32[160,128]{1,0:T(8,128)S(1)} %copy-done.10), channel_id=1, source_target_pairs={{0,0},{8,1},{16,2},{24,3},{32,4},{40,5},{48,6},{56,7},{64,8},{72,9... | collective-permute-start | bytes 245768 | tf_op jit(solution)/shard_map/ppermute | solution.py:385
  119.2 4.3 %vectors.1 = (bf16[2,128,2560]{2,1,0:T(8,128)(2,1)}, bf16[2,1280,128]{2,1,0:T(8,128)(2,1)}) custom-call(s32[3]{0:T(128)} %copy-done.4, f32[16,176,128]{2,1,0:T(8,128)} %copy-done.1, f32[128,128]{1,0:T(8,128)} %copy-done.3, f32[640,128]{1,0:T(8,128)} %copy-done, f32[640,128]{1,0:T(8,128)} %copy-done.2), custom_call_target="tpu_custom_call" | custom-call | flops 377487360 | bytes 6094848 | tf_op jit(solution)/shard_map/vectors/pallas_call | solution.py:81
  123.5 4.8 %collective-permute-done.6.refs_3_ = f32[160,128]{1,0:T(8,128)S(1)} collective-permute-done((f32[160,128]{1,0:T(8,128)S(1)}, f32[160,128]{1,0:T(8,128)S(1)}, u32[]{:S(2)}, u32[]{:S(2)}) %collective-permute-start.6) | collective-permute-done | bytes 81952 | tf_op jit(solution)/shard_map/ppermute | solution.py:385
  128.4 1.4 all-to-all-done.4.refs_2_.refs_1_
  130.9 4.0 %inner.1 = f32[8,288,128]{2,1,0:T(8,128)} custom-call(s32[3]{0:T(128)} %copy-done.4, bf16[2,128,2560]{2,1,0:T(8,128)(2,1)} %get-tuple-element.27.refs_1_.refs_6_, f32[16,160,128]{2,1,0:T(8,128)} %copy-done.5, f32[160,128]{1,0:T(8,128)} %copy-done.9), custom_call_target="tpu_custom_call" | custom-call | flops 251658240 | bytes 5193728 | tf_op jit(solution)/shard_map/inner/pallas_call | solution.py:81
  134.9 9.4 %all-to-all-start.5 = ((f32[8,288,128]{2,1,0:T(8,128)}), f32[8,288,128]{2,1,0:T(8,128)S(1)}, u32[]{:S(2)}, u32[]{:S(2)}) async-start(f32[8,288,128]{2,1,0:T(8,128)} %inner.1), calls=%async_computation.5 | async-start | bytes 2359296 | tf_op jit(solution)/shard_map/all_to_all | solution.py:414
  144.3 13.2 %coupling.1.refs_2_.refs_3_ = f32[128,128]{1,0:T(8,128)} custom-call(s32[3]{0:T(128)} %copy-done.4, f32[16,176,128]{2,1,0:T(8,128)} %copy-done.1, f32[128,128]{1,0:T(8,128)} %copy-done.3), custom_call_target="tpu_custom_call" | custom-call | flops 8000000000 | bytes 1572864 | tf_op jit(solution)/shard_map/coupling/pallas_call | solution.py:81
  157.5 3.8 %sides.1.refs_5_ = f32[128,2560]{1,0:T(8,128)} custom-call(s32[3]{0:T(128)} %copy-done.4, f32[16,160,128]{2,1,0:T(8,128)} %copy-done.5, f32[128,128]{1,0:T(8,128)} %coupling.1.refs_2_.refs_3_), custom_call_target="tpu_custom_call" | custom-call | flops 251658240 | bytes 2686976 | tf_op jit(solution)/shard_map/sides/pallas_call | solution.py:81
  162.3 12.2 %last_pass.1 = f32[1280,2560]{1,0:T(8,128)} custom-call(s32[3]{0:T(128)} %copy-done.4, f32[1280,2560]{1,0:T(8,128)} %refs_1_.5, f32[8,288,128]{2,1,0:T(8,128)} %copy-done.8, f32[128,128]{1,0:T(8,128)} %coupling.1.refs_2_.refs_3_, bf16[2,1280,128]{2,1,0:T(8,128)(2,1)} %get-tuple-element.30.refs_4_, f32[128,2560]{1,0:T(8,128)} %sides.1.refs_5_, ...), custom_call_target="tpu_custom_call" | custom-call | flops 5033164800 | bytes 32702464 | tf_op jit(solution)/shard_map/last_pass/pallas_call | solution.py:81
  (32 shorter events, 6.4 us)
Async XLA Ops:
  1.1 6.2 %collective-permute-start.1 = (f32[640,128]{1,0:T(8,128)S(1)}, f32[640,128]{1,0:T(8,128)S(1)}, u32[]{:S(2)}, u32[]{:S(2)}) collective-permute-start(f32[640,128]{1,0:T(8,128)S(1)} %get-tuple-element.31), channel_id=1, source_target_pairs={{0,2},{8,10},{16,18},{24,26},{32,34},{40,42},{48,50},{56,58},{64,6... | collective-permute-start | bytes 983048 | tf_op jit(solution)/shard_map/ppermute | solution.py:329
  1.8 5.6 %collective-permute-start.2 = (f32[640,128]{1,0:T(8,128)S(1)}, f32[640,128]{1,0:T(8,128)S(1)}, u32[]{:S(2)}, u32[]{:S(2)}) collective-permute-start(f32[640,128]{1,0:T(8,128)S(1)} %get-tuple-element.32), channel_id=1, source_target_pairs={{0,6},{8,14},{16,22},{24,30},{32,38},{40,46},{48,54},{56,62},{64,7... | collective-permute-start | bytes 983048 | tf_op jit(solution)/shard_map/ppermute | solution.py:330
  2.5 8.2 %collective-permute-start = (f32[640,128]{1,0:T(8,128)S(1)}, f32[640,128]{1,0:T(8,128)S(1)}, u32[]{:S(2)}, u32[]{:S(2)}) collective-permute-start(f32[640,128]{1,0:T(8,128)S(1)} %get-tuple-element.32), channel_id=1, source_target_pairs={{0,1},{8,9},{16,17},{24,25},{32,33},{40,41},{48,49},{56,57},{64,65... | collective-permute-start | bytes 983048 | tf_op jit(solution)/shard_map/ppermute | solution.py:328
  3.9 80.9 %copy-start.4 = (s32[3]{0:T(128)}, s32[3]{0:T(128)S(1)}, u32[]{:S(2)}) copy-start(s32[3]{0:T(128)S(1)} %pad_add_fusion.refs_0_) | copy-start | bytes 40
  11.7 24.5 %all-to-all-start = ((f32[16,160,128]{2,1,0:T(8,128)}), f32[16,160,128]{2,1,0:T(8,128)S(1)}, u32[]{:S(2)}, u32[]{:S(2)}) async-start(f32[16,160,128]{2,1,0:T(8,128)} %second.1), calls=%async_computation | async-start | bytes 2621440 | tf_op jit(solution)/shard_map/all_to_all | solution.py:336
  19.4 5.3 %collective-permute-start.3 = (f32[640,128]{1,0:T(8,128)S(1)}, f32[640,128]{1,0:T(8,128)S(1)}, u32[]{:S(2)}, u32[]{:S(2)}) collective-permute-start(f32[640,128]{1,0:T(8,128)S(1)} %select_select_fusion), channel_id=1, source_target_pairs={{0,7},{1,3},{2,4},{6,5},{8,15},{9,11},{10,12},{14,13},{16,23},{17,... | collective-permute-start | bytes 983048 | tf_op jit(solution)/shard_map/ppermute | solution.py:337
  24.7 36.6 %copy-start = (f32[640,128]{1,0:T(8,128)}, f32[640,128]{1,0:T(8,128)S(1)}, u32[]{:S(2)}) copy-start(f32[640,128]{1,0:T(8,128)S(1)} %broadcast_select_fusion.refs_1_.refs_2_.refs_3_) | copy-start | bytes 983044
  24.7 4.7 %collective-permute-start.4 = (f32[640,128]{1,0:T(8,128)S(1)}, f32[640,128]{1,0:T(8,128)S(1)}, u32[]{:S(2)}, u32[]{:S(2)}) collective-permute-start(f32[640,128]{1,0:T(8,128)S(1)} %broadcast_select_fusion.refs_1_.refs_2_.refs_3_), channel_id=1, source_target_pairs={{0,1},{1,0},{2,3},{3,2},{4,5},{5,4},{6,7},{7,6},{8,9},{9,8},{10,11... | collective-permute-start | bytes 983048 | tf_op jit(solution)/shard_map/ppermute | solution.py:339
  29.4 31.8 %copy-start.2 = (f32[640,128]{1,0:T(8,128)}, f32[640,128]{1,0:T(8,128)S(1)}, u32[]{:S(2)}) copy-start(f32[640,128]{1,0:T(8,128)S(1)} %collective-permute-done.4.refs_2_.refs_3_.refs_4_) | copy-start | bytes 983044
  36.2 17.7 %copy-start.6 = (f32[16,160,128]{2,1,0:T(8,128)}, f32[16,160,128]{2,1,0:T(8,128)S(1)}, u32[]{:S(2)}) copy-start(f32[16,160,128]{2,1,0:T(8,128)S(1)} %all-to-all-done.refs_3_) | copy-start | bytes 3932164
  36.2 15.5 %all-to-all-start.1 = ((f32[16,16,128]{2,1,0:T(8,128)}), f32[16,16,128]{2,1,0:T(8,128)S(1)}, u32[]{:S(2)}, u32[]{:S(2)}) async-start(f32[16,16,128]{2,1,0:T(8,128)} %gram.1), calls=%async_computation.1 | async-start | bytes 262144 | tf_op jit(solution)/shard_map/all_to_all | solution.py:352
  41.5 10.2 %collective-permute-start.5 = (f32[160,128]{1,0:T(8,128)S(1)}, f32[160,128]{1,0:T(8,128)S(1)}, u32[]{:S(2)}, u32[]{:S(2)}) collective-permute-start(f32[160,128]{1,0:T(8,128)S(1)} %dynamic-slice_select_fusion), channel_id=1, source_target_pairs={{0,0},{1,8},{2,16},{3,24},{4,32},{5,40},{6,48},{7,56},{8,64},{9,72... | collective-permute-start | bytes 245768 | tf_op jit(solution)/shard_map/ppermute | solution.py:348
  53.9 23.7 %all-to-all-start.3 = ((f32[16,176,128]{2,1,0:T(8,128)}), f32[16,176,128]{2,1,0:T(8,128)S(1)}, u32[]{:S(2)}, u32[]{:S(2)}) async-start(f32[16,176,128]{2,1,0:T(8,128)} %mix.1), calls=%async_computation.3 | async-start | bytes 2883584 | tf_op jit(solution)/shard_map/all_to_all | solution.py:363
  77.6 7.2 %copy-start.1 = (f32[16,176,128]{2,1,0:T(8,128)}, f32[16,176,128]{2,1,0:T(8,128)S(1)}, u32[]{:S(2)}) copy-start(f32[16,176,128]{2,1,0:T(8,128)S(1)} %all-to-all-done.3.refs_1_) | copy-start | bytes 4325380
  77.6 24.0 %all-to-all-start.2 = ((f32[16,160,128]{2,1,0:T(8,128)}), f32[16,160,128]{2,1,0:T(8,128)S(1)}, u32[]{:S(2)}, u32[]{:S(2)}) async-start(f32[16,160,128]{2,1,0:T(8,128)} %first_pass.1), calls=%async_computation.2 | async-start | bytes 2621440 | tf_op jit(solution)/shard_map/all_to_all | solution.py:373
  95.3 0.6 copy-start.3
  101.7 1.1 copy-start.7
  106.2 6.0 %copy-start.10 = (f32[160,128]{1,0:T(8,128)S(1)}, f32[160,128]{1,0:T(8,128)}, u32[]{:S(2)}) copy-start(f32[160,128]{1,0:T(8,128)} %get-tuple-element.29) | copy-start | bytes 245764
  106.3 23.5 %all-to-all-start.4 = ((f32[16,160,128]{2,1,0:T(8,128)}), f32[16,160,128]{2,1,0:T(8,128)S(1)}, u32[]{:S(2)}, u32[]{:S(2)}) async-start(f32[16,160,128]{2,1,0:T(8,128)} %get-tuple-element.28), calls=%async_computation.4 | async-start | bytes 2621440 | tf_op jit(solution)/shard_map/all_to_all | solution.py:386
  112.2 16.2 %collective-permute-start.6 = (f32[160,128]{1,0:T(8,128)S(1)}, f32[160,128]{1,0:T(8,128)S(1)}, u32[]{:S(2)}, u32[]{:S(2)}) collective-permute-start(f32[160,128]{1,0:T(8,128)S(1)} %copy-done.10), channel_id=1, source_target_pairs={{0,0},{8,1},{16,2},{24,3},{32,4},{40,5},{48,6},{56,7},{64,8},{72,9... | collective-permute-start | bytes 245768 | tf_op jit(solution)/shard_map/ppermute | solution.py:385
  128.4 1.4 copy-start.9
  129.8 1.1 copy-start.5
  134.9 26.3 %all-to-all-start.5 = ((f32[8,288,128]{2,1,0:T(8,128)}), f32[8,288,128]{2,1,0:T(8,128)S(1)}, u32[]{:S(2)}, u32[]{:S(2)}) async-start(f32[8,288,128]{2,1,0:T(8,128)} %inner.1), calls=%async_computation.5 | async-start | bytes 2359296 | tf_op jit(solution)/shard_map/all_to_all | solution.py:414
  161.3 1.0 copy-start.8

commit v5 on v4

--- a/solution.py
+++ b/solution.py
@@ -10,7 +10,7 @@
 NC = 8
 STEP = 256
 WIDE = 512
-LIMITS = {"gram": 20, "mix": 20, "factor": 20, "second": 52, "first_pass": 52}
+LIMITS = {"gram": 20, "mix": 20, "factor": 20, "coupling": 20, "piece_image": 20, "vectors": 20, "second": 52, "first_pass": 52}
 F32 = jnp.float32
 BF16 = jnp.bfloat16
 SM = pl.BlockSpec(memory_space=pltpu.SMEM)
@@ -115,14 +115,10 @@
 
 
 def mix_kernel(rc, ins, outs, bufs, copy):
-    msg, p, small = bufs
-    piece, n = p.shape[0], small.shape[0]
-    first = run([copy(ins[0], msg)])
-    wait(run([copy(ins[1], p)]))
-    more = run([copy(p, outs[0].at[k, pl.ds(0, piece)]) for k in range(NR)])
-    wait(first)
+    msg, small = bufs
+    wait(run([copy(ins[0], msg)]))
     small[...] = jnp.sum(msg[...], 0)
-    wait(more + run([copy(small, outs[0].at[k, pl.ds(piece, n)]) for k in range(NR)]))
+    wait(run([copy(small, outs[0].at[k]) for k in range(NR)]))
 
 
 def second_kernel(rc, ins, outs, bufs, copy):
@@ -137,13 +133,16 @@
 
 
 def first_kernel(rc, ins, outs, bufs, copy):
-    a_ref, held, other = ins
-    buf, panel, acc, rows_out = bufs
+    a_ref, held, other, mine_ref = ins
+    buf, panel, acc, rows_out, mine = bufs
+    piece = mine.shape[0]
     rows, cols = buf.shape
     n = rows // STEP
     first = load_panel(rc, held, other, panel, copy)
     copies = run([copy(a_ref.at[pl.ds(k * STEP, STEP)], buf.at[pl.ds(k * STEP, STEP)]) for k in range(n)])
-    wait(first)
+    early = run([copy(mine_ref, mine)])
+    wait(first + early)
+    more = run([copy(mine, outs[0].at[k, pl.ds(piece, piece)]) for k in range(NR)])
     clear_top(rc, panel)
     ph, plow = split(panel[...])
     both = jnp.concatenate([ph, plow], 1)
@@ -161,8 +160,7 @@
                 acc[:, sl] += x
             else:
                 rows_out[sl] = (acc[:, sl] + x).T
-    piece = outs[0].shape[1]
-    wait(run([copy(rows_out.at[pl.ds(k * piece, piece)], outs[0].at[k]) for k in range(NR)]))
+    wait(more + run([copy(rows_out.at[pl.ds(k * piece, piece)], outs[0].at[k, pl.ds(0, piece)]) for k in range(NR)]))
 
 
 def lane(x, k):
@@ -227,7 +225,7 @@
 
 def piece_kernel(rc, ins, outs, bufs, copy):
     msg, linv, f, out = bufs
-    wait(run([copy(ins[0], msg), copy(ins[1], linv), copy(ins[2].at[0], f)]))
+    wait(run([copy(ins[0].at[:, pl.ds(0, msg.shape[1])], msg), copy(ins[1], linv), copy(ins[2], f)]))
     out[...] = dot3(jnp.sum(msg[...], 0), linv[...], 1, 1) - f[...]
     wait(run([copy(out, outs[0].at[k]) for k in range(NR)] + [copy(out, outs[1])]))
 
@@ -237,7 +235,7 @@
     cols, rows = v.shape[2], panel.shape[0]
     more = load_panel(rc, ins[2], ins[3], panel, copy)
     p = msg.reshape(cols, W)
-    wait(run([copy(ins[0].at[:, pl.ds(0, msg.shape[1])], msg), copy(ins[1], linv)]))
+    wait(run([copy(ins[0].at[:, pl.ds(msg.shape[1], msg.shape[1])], msg), copy(ins[1], linv)]))
     ls = split(linv[...])
     for b in range(cols // WIDE):
         sl = slice(b * WIDE, (b + 1) * WIDE)
@@ -348,16 +346,16 @@
     panel_q = lax.ppermute(mine, axes, list(enumerate(owner)))
     half_bufs = [shape(rows, W)]
     small = call(gram_kernel, "gram", 6 * rows * W * W, (rc, held, other), shape(NR, 16, W), half_bufs + [shape(NR, 16, W)], 3)
-    small, f_msg = lax.optimization_barrier((small, f_msg))
+    small, f_q = lax.optimization_barrier((small, f_msg[0]))
     small = lax.all_to_all(small, "prow", 0, 0, tiled=True)
     small = call(
         mix_kernel,
         "mix",
         NR * 16 * W,
-        (rc, small, panel_q),
-        shape(NR, piece + 16, W),
-        [shape(NR, 16, W), shape(piece, W), shape(16, W)],
-        2 + 2 * NR,
+        (rc, small),
+        shape(NR, 16, W),
+        [shape(NR, 16, W), shape(16, W)],
+        1 + NR,
     )
     small, held, other = lax.optimization_barrier((small, held, other))
     small = lax.all_to_all(small, "prow", 0, 0, tiled=True)
@@ -365,33 +363,33 @@
         first_kernel,
         "first_pass",
         big,
-        (rc, matrix, held, other),
-        shape(NR, piece, W),
-        [shape(rows, cols), shape(rows, W), shape(W, cols), shape(cols, W)],
-        2 + rows // STEP + NR,
+        (rc, matrix, held, other, panel_q),
+        shape(NR, 2 * piece, W),
+        [shape(rows, cols), shape(rows, W), shape(W, cols), shape(cols, W), shape(piece, W)],
+        3 + rows // STEP + 2 * NR,
     )
     msg = lax.all_to_all(msg, "prow", 0, 0, tiled=True)
     linv = call(factor_kernel, "factor", 8e9, (rc, small), shape(W, W), [shape(NR, 8, W), shape(W, W)], 2)
+    coup = call(
+        coupling_kernel, "coupling", 8e9, (rc, small, linv), shape(W, W), [shape(NR, 8, W), shape(W, W), shape(W, W)], 3
+    )
+    sums, linv, coup = lax.optimization_barrier((msg, linv, coup))
     msg, y_q = call(
         piece_kernel,
         "piece_image",
         msg.size,
-        (rc, msg, linv, f_msg),
+        (rc, sums, linv, f_q),
         [shape(NR, piece, W), shape(piece, W)],
         [shape(NR, piece, W), shape(W, W), shape(piece, W), shape(piece, W)],
         3 + NR + 1,
     )
-    y_q, small = lax.optimization_barrier((y_q, small))
     y_p = lax.ppermute(y_q, axes, [(b, a) for a, b in enumerate(owner)])
     msg = lax.all_to_all(msg, "prow", 0, 0, tiled=True)
-    coup = call(
-        coupling_kernel, "coupling", 8e9, (rc, small, linv), shape(W, W), [shape(NR, 8, W), shape(W, W), shape(W, W)], 3
-    )
     vt, left = call(
         vectors_kernel,
         "vectors",
         6 * (rows + cols) * W * W,
-        (rc, small, linv, held, other),
+        (rc, sums, linv, held, other),
         [shape(2, W, cols, dtype=BF16), shape(2, rows, W, dtype=BF16)],
         [
             shape(NR, piece, W),

time: 176 us -> 176 us (level)
  Pallas kernels: 66.7 us -> 62.9 us
  starting transfers between devices: 63.2 us -> 66.8 us
  local copies, waits for them, and re-layouts: 4.96 us -> 7.02 us
    all_to_all x1, waiting for transfers between devices: 0.01 us -> 12.7 us  [on_device(): end = lax.all_to_all(end, 'pcol', 0, 0, tiled=True)]
    all_to_all x2, waiting for transfers between devices: 8.7 us -> 0.56 us  [on_device(): small = lax.all_to_all(small, 'prow', 0, 0, tiled=True)]
    ppermute x1, waiting for transfers between devices: 4.05 us -> 0.01 us  [on_device(): panel_q = lax.ppermute(mine, axes, list(enumerate(owner)))]
    pallas_call x11, Pallas kernels: 66.7 us -> 62.9 us  [call(): pl.pallas_call(body, in_specs=[SM] + [pl.BlockSpec(memory_space=pl.ANY)]...]
    all_to_all x2, starting transfers between devices: 12.6 us -> 9.54 us  [on_device(): small = lax.all_to_all(small, 'prow', 0, 0, tiled=True)]
    all_to_all x1, starting transfers between devices: 9.4 us -> 12.1 us  [on_device(): end = lax.all_to_all(end, 'pcol', 0, 0, tiled=True)]
    ppermute x1, starting transfers between devices: 6.98 us -> 9.28 us  [on_device(): y_p = lax.ppermute(y_q, axes, [(b, a) for a, b in enumerate(owner)])]
    unnamed x22 -> x18, local copies, waits for them, and re-layouts: 3.84 us -> 5.9 us
  transfers between devices with their start and end apart: 13 -> 13, of which waited for: 9 -> 8; matrix products, arithmetic and copies ran while one was open for 0% -> 0% of each run, Pallas kernels for 26% -> 25%
where the time goes in v5:
time: 176 us; the launch traced here: 175 us
  starting transfers between devices  66.8 us (38%)
  Pallas kernels  62.9 us (36%)
  waiting for transfers between devices  36.4 us (21%)
  local copies, waits for them, and re-layouts  7.02 us (4%)
    pallas_call x11, Pallas kernels, call(): pl.pallas_call(body, in_specs=[SM] + [pl.BlockSpec(memory_space=pl.ANY)]...  62.9 us
    all_to_all x2, starting transfers between devices, on_device(): msg = lax.all_to_all(msg, 'prow', 0, 0, tiled=True)  14.7 us
    all_to_all x1, waiting for transfers between devices, on_device(): end = lax.all_to_all(end, 'pcol', 0, 0, tiled=True)  12.7 us
    all_to_all x1, starting transfers between devices, on_device(): end = lax.all_to_all(end, 'pcol', 0, 0, tiled=True)  12.1 us
    all_to_all x2, starting transfers between devices, on_device(): small = lax.all_to_all(small, 'prow', 0, 0, tiled=True)  9.54 us
    ppermute x1, starting transfers between devices, on_device(): y_p = lax.ppermute(y_q, axes, [(b, a) for a, b in enumerate(owner)])  9.28 us
    all_to_all x1, starting transfers between devices, on_device(): f_msg = lax.all_to_all(f_msg, 'prow', 0, 0, tiled=True)  7.61 us
    all_to_all x2, waiting for transfers between devices, on_device(): msg = lax.all_to_all(msg, 'prow', 0, 0, tiled=True)  6.64 us
  transfers between devices with their start and end apart: 13, of which 8 were waited for; matrix products, arithmetic and copies ran while one was open for 0% of the time, Pallas kernels for 25%

profile of v5, /device:TPU:1, one launch (start us, length us, event | category | flops | bytes accessed | tf_op | source)
XLA Modules:
  0.0 174.7 jit_solution(5283869467112791492)
XLA Ops:
  0.0 1.1 fusion
  2.5 1.3 collective-permute-start
  3.9 3.4 %second.1 = f32[16,160,128]{2,1,0:T(8,128)} custom-call(s32[3]{0:T(128)S(1)} %pad_add_fusion.refs_0_, f32[1280,2560]{1,0:T(8,128)} %refs_1_.5), custom_call_target="tpu_custom_call" | custom-call | flops 128 | bytes 14417920 | tf_op jit(solution)/shard_map/second/pallas_call | solution.py:81
  7.4 3.3 %collective-permute-done = f32[640,128]{1,0:T(8,128)S(1)} collective-permute-done((f32[640,128]{1,0:T(8,128)S(1)}, f32[640,128]{1,0:T(8,128)S(1)}, u32[]{:S(2)}, u32[]{:S(2)}) %collective-permute-start) | collective-permute-done | bytes 327712 | tf_op jit(solution)/shard_map/ppermute | solution.py:326
  11.7 7.6 %all-to-all-start = ((f32[16,160,128]{2,1,0:T(8,128)}), f32[16,160,128]{2,1,0:T(8,128)S(1)}, u32[]{:S(2)}, u32[]{:S(2)}) async-start(f32[16,160,128]{2,1,0:T(8,128)} %second.1), calls=%async_computation | async-start | bytes 2621440 | tf_op jit(solution)/shard_map/all_to_all | solution.py:334
  19.3 1.3 collective-permute-start.3
  20.7 4.0 %collective-permute-done.3 = f32[640,128]{1,0:T(8,128)S(1)} collective-permute-done((f32[640,128]{1,0:T(8,128)S(1)}, f32[640,128]{1,0:T(8,128)S(1)}, u32[]{:S(2)}, u32[]{:S(2)}) %collective-permute-start.3) | collective-permute-done | bytes 327712 | tf_op jit(solution)/shard_map/ppermute | solution.py:335
  24.7 3.4 %collective-permute-start.4 = (f32[640,128]{1,0:T(8,128)S(1)}, f32[640,128]{1,0:T(8,128)S(1)}, u32[]{:S(2)}, u32[]{:S(2)}) collective-permute-start(f32[640,128]{1,0:T(8,128)S(1)} %broadcast_select_fusion.refs_1_.refs_2_.refs_3_), channel_id=1, source_target_pairs={{0,1},{1,0},{2,3},{3,2},{4,5},{5,4},{6,7},{7,6},{8,9},{9,8},{10,11... | collective-permute-start | bytes 983048 | tf_op jit(solution)/shard_map/ppermute | solution.py:337
  28.1 1.3 collective-permute-done.4.refs_2_.refs_3_.refs_4_
  29.4 1.9 %gram.1 = f32[16,16,128]{2,1,0:T(8,128)} custom-call(s32[3]{0:T(128)S(1)} %pad_add_fusion.refs_0_, f32[640,128]{1,0:T(8,128)S(1)} %broadcast_select_fusion.refs_1_.refs_2_.refs_3_, f32[640,128]{1,0:T(8,128)S(1)} %collective-permute-done.4.refs_2_.refs_3_.refs_4_), custom_call_target="tpu_custom_call" | custom-call | flops 125829120 | bytes 786432 | tf_op jit(solution)/shard_map/gram/pallas_call | solution.py:81
  31.3 4.9 %all-to-all-done = f32[16,160,128]{2,1,0:T(8,128)S(1)} async-done(((f32[16,160,128]{2,1,0:T(8,128)}), f32[16,160,128]{2,1,0:T(8,128)S(1)}, u32[]{:S(2)}, u32[]{:S(2)}) %all-to-all-start) | async-done | bytes 1310752 | tf_op jit(solution)/shard_map/all_to_all | solution.py:334
  36.2 5.3 %all-to-all-start.1 = ((f32[16,16,128]{2,1,0:T(8,128)}), f32[16,16,128]{2,1,0:T(8,128)S(1)}, u32[]{:S(2)}, u32[]{:S(2)}) async-start(f32[16,16,128]{2,1,0:T(8,128)} %gram.1), calls=%async_computation.1 | async-start | bytes 262144 | tf_op jit(solution)/shard_map/all_to_all | solution.py:350
  41.5 6.1 %collective-permute-start.5 = (f32[160,128]{1,0:T(8,128)S(1)}, f32[160,128]{1,0:T(8,128)S(1)}, u32[]{:S(2)}, u32[]{:S(2)}) collective-permute-start(f32[160,128]{1,0:T(8,128)S(1)} %dynamic-slice_select_fusion), channel_id=1, source_target_pairs={{0,0},{1,8},{2,16},{3,24},{4,32},{5,40},{6,48},{7,56},{8,64},{9,72... | collective-permute-start | bytes 245768 | tf_op jit(solution)/shard_map/ppermute | solution.py:346
  48.1 1.5 mix.1
  49.7 4.3 %all-to-all-start.3 = ((f32[16,16,128]{2,1,0:T(8,128)}), f32[16,16,128]{2,1,0:T(8,128)S(1)}, u32[]{:S(2)}, u32[]{:S(2)}) async-start(f32[16,16,128]{2,1,0:T(8,128)} %mix.1), calls=%async_computation.3 | async-start | bytes 262144 | tf_op jit(solution)/shard_map/all_to_all | solution.py:361
  54.0 8.3 %first_pass.1 = f32[16,320,128]{2,1,0:T(8,128)} custom-call(s32[3]{0:T(128)S(1)} %pad_add_fusion.refs_0_, f32[1280,2560]{1,0:T(8,128)} %refs_1_.5, f32[640,128]{1,0:T(8,128)S(1)} %broadcast_select_fusion.refs_1_.refs_2_.refs_3_, f32[640,128]{1,0:T(8,128)S(1)} %collective-permute-done.4.refs_2_.refs_3_.refs_4_, f32[160,128]{1,0:T(8,128)S(1)} %collective-permute-done.5.refs_4_), custom_call_target="tpu_custom_call" | custom-call | flops 2516582400 | bytes 16465920 | tf_op jit(solution)/shard_map/first_pass/pallas_call | solution.py:81
  62.3 6.7 %all-to-all-start.2 = ((f32[16,320,128]{2,1,0:T(8,128)}), f32[16,320,128]{2,1,0:T(8,128)S(1)}, u32[]{:S(2)}, u32[]{:S(2)}) async-start(f32[16,320,128]{2,1,0:T(8,128)} %first_pass.1), calls=%async_computation.2 | async-start | bytes 5242880 | tf_op jit(solution)/shard_map/all_to_all | solution.py:371
  69.6 10.5 %factor.1.refs_2_ = f32[128,128]{1,0:T(8,128)S(1)} custom-call(s32[3]{0:T(128)S(1)} %copy-done.5, f32[16,16,128]{2,1,0:T(8,128)S(1)} %all-to-all-done.3.refs_1_), custom_call_target="tpu_custom_call" | custom-call | flops 8000000000 | bytes 196608 | tf_op jit(solution)/shard_map/factor/pallas_call | solution.py:81
  80.1 11.7 %coupling.1.refs_2_.refs_3_ = f32[128,128]{1,0:T(8,128)S(1)} custom-call(s32[3]{0:T(128)S(1)} %copy-done.5, f32[16,16,128]{2,1,0:T(8,128)S(1)} %all-to-all-done.3.refs_1_, f32[128,128]{1,0:T(8,128)S(1)} %factor.1.refs_2_), custom_call_target="tpu_custom_call" | custom-call | flops 8000000000 | bytes 262144 | tf_op jit(solution)/shard_map/coupling/pallas_call | solution.py:81
  92.5 6.6 %all-to-all-done.2.refs_1_ = f32[16,320,128]{2,1,0:T(8,128)S(1)} async-done(((f32[16,320,128]{2,1,0:T(8,128)}), f32[16,320,128]{2,1,0:T(8,128)S(1)}, u32[]{:S(2)}, u32[]{:S(2)}) %all-to-all-start.2) | async-done | bytes 2621472 | tf_op jit(solution)/shard_map/all_to_all | solution.py:371
  99.7 3.0 %piece_image.1 = (f32[16,160,128]{2,1,0:T(8,128)S(1)}, f32[160,128]{1,0:T(8,128)S(1)}) custom-call(s32[3]{0:T(128)S(1)} %copy-done.6, f32[16,320,128]{2,1,0:T(8,128)S(1)} %all-to-all-done.2.refs_1_, f32[128,128]{1,0:T(8,128)S(1)} %factor.1.refs_2_, f32[160,128]{1,0:T(8,128)S(1)} %slice_bitcast_fusion.refs_3_), custom_call_target="tpu_custom_call" | custom-call | flops 655360 | bytes 4161536 | tf_op jit(solution)/shard_map/piece_image/pallas_call | solution.py:81
  102.8 1.0 copy-done.1
  103.8 8.0 %all-to-all-start.4 = ((f32[16,160,128]{2,1,0:T(8,128)}), f32[16,160,128]{2,1,0:T(8,128)}, u32[]{:S(2)}, u32[]{:S(2)}) async-start(f32[16,160,128]{2,1,0:T(8,128)} %copy-done.1), calls=%async_computation.4 | async-start | bytes 2621440 | tf_op jit(solution)/shard_map/all_to_all | solution.py:387
  111.9 9.3 %collective-permute-start.6 = (f32[160,128]{1,0:T(8,128)S(1)}, f32[160,128]{1,0:T(8,128)}, u32[]{:S(2)}, u32[]{:S(2)}) collective-permute-start(f32[160,128]{1,0:T(8,128)S(1)} %get-tuple-element.30), channel_id=1, source_target_pairs={{0,0},{8,1},{16,2},{24,3},{32,4},{40,5},{48,6},{56,7},{64,8},{72,9... | collective-permute-start | bytes 245768 | tf_op jit(solution)/shard_map/ppermute | solution.py:386
  121.2 2.5 %vectors.1 = (bf16[2,128,2560]{2,1,0:T(8,128)(2,1)S(1)}, bf16[2,1280,128]{2,1,0:T(8,128)(2,1)S(1)}) custom-call(s32[3]{0:T(128)S(1)} %copy-done.7, f32[16,320,128]{2,1,0:T(8,128)S(1)} %all-to-all-done.2.refs_1_, f32[128,128]{1,0:T(8,128)S(1)} %factor.1.refs_2_, f32[640,128]{1,0:T(8,128)S(1)} %broadcast_select_fusion.refs_1_.refs_2_.refs_3_, ...), custom_call_target="tpu_custom_call" | custom-call | flops 377487360 | bytes 7274496 | tf_op jit(solution)/shard_map/vectors/pallas_call | solution.py:81
  123.7 1.1 copy-done
  125.6 3.0 %collective-permute-done.6.refs_3_ = f32[160,128]{1,0:T(8,128)} collective-permute-done((f32[160,128]{1,0:T(8,128)S(1)}, f32[160,128]{1,0:T(8,128)}, u32[]{:S(2)}, u32[]{:S(2)}) %collective-permute-start.6) | collective-permute-done | bytes 81952 | tf_op jit(solution)/shard_map/ppermute | solution.py:386
  128.6 4.0 %inner.1 = f32[8,288,128]{2,1,0:T(8,128)} custom-call(s32[3]{0:T(128)} %copy-done.4, bf16[2,128,2560]{2,1,0:T(8,128)(2,1)} %copy-done, f32[16,160,128]{2,1,0:T(8,128)} %all-to-all-done.4.refs_2_.refs_1_, f32[160,128]{1,0:T(8,128)} %collective-permute-done.6.refs_3_), custom_call_target="tpu_custom_call" | custom-call | flops 251658240 | bytes 5193728 | tf_op jit(solution)/shard_map/inner/pallas_call | solution.py:81
  132.6 12.1 %all-to-all-start.5 = ((f32[8,288,128]{2,1,0:T(8,128)}), f32[8,288,128]{2,1,0:T(8,128)S(1)}, u32[]{:S(2)}, u32[]{:S(2)}) async-start(f32[8,288,128]{2,1,0:T(8,128)} %inner.1), calls=%async_computation.5 | async-start | bytes 2359296 | tf_op jit(solution)/shard_map/all_to_all | solution.py:412
  144.8 3.8 %sides.1.refs_5_ = f32[128,2560]{1,0:T(8,128)} custom-call(s32[3]{0:T(128)} %copy-done.4, f32[16,160,128]{2,1,0:T(8,128)} %all-to-all-done.4.refs_2_.refs_1_, f32[128,128]{1,0:T(8,128)} %copy-done.3), custom_call_target="tpu_custom_call" | custom-call | flops 251658240 | bytes 2686976 | tf_op jit(solution)/shard_map/sides/pallas_call | solution.py:81
  148.5 12.7 %all-to-all-done.5.refs_2_ = f32[8,288,128]{2,1,0:T(8,128)S(1)} async-done(((f32[8,288,128]{2,1,0:T(8,128)}), f32[8,288,128]{2,1,0:T(8,128)S(1)}, u32[]{:S(2)}, u32[]{:S(2)}) %all-to-all-start.5) | async-done | bytes 1179680 | tf_op jit(solution)/shard_map/all_to_all | solution.py:412
  162.3 12.2 %last_pass.1 = f32[1280,2560]{1,0:T(8,128)} custom-call(s32[3]{0:T(128)} %copy-done.4, f32[1280,2560]{1,0:T(8,128)} %refs_1_.5, f32[8,288,128]{2,1,0:T(8,128)} %copy-done.8, f32[128,128]{1,0:T(8,128)} %copy-done.3, bf16[2,1280,128]{2,1,0:T(8,128)(2,1)} %copy-done.2, f32[128,2560]{1,0:T(8,128)} %sides.1.refs_5_, bf16[2,128,2560]{2,1,0:T(8,128)(2,1)} %copy-done), custom_call_target="tpu_custom_call" | custom-call | flops 5033164800 | bytes 32702464 | tf_op jit(solution)/shard_map/last_pass/pallas_call | solution.py:81
  (29 shorter events, 6.9 us)
Async XLA Ops:
  1.1 6.2 %collective-permute-start.1 = (f32[640,128]{1,0:T(8,128)S(1)}, f32[640,128]{1,0:T(8,128)S(1)}, u32[]{:S(2)}, u32[]{:S(2)}) collective-permute-start(f32[640,128]{1,0:T(8,128)S(1)} %get-tuple-element.33), channel_id=1, source_target_pairs={{0,2},{8,10},{16,18},{24,26},{32,34},{40,42},{48,50},{56,58},{64,6... | collective-permute-start | bytes 983048 | tf_op jit(solution)/shard_map/ppermute | solution.py:327
  1.8 5.6 %collective-permute-start.2 = (f32[640,128]{1,0:T(8,128)S(1)}, f32[640,128]{1,0:T(8,128)S(1)}, u32[]{:S(2)}, u32[]{:S(2)}) collective-permute-start(f32[640,128]{1,0:T(8,128)S(1)} %get-tuple-element.34), channel_id=1, source_target_pairs={{0,6},{8,14},{16,22},{24,30},{32,38},{40,46},{48,54},{56,62},{64,7... | collective-permute-start | bytes 983048 | tf_op jit(solution)/shard_map/ppermute | solution.py:328
  2.5 8.2 %collective-permute-start = (f32[640,128]{1,0:T(8,128)S(1)}, f32[640,128]{1,0:T(8,128)S(1)}, u32[]{:S(2)}, u32[]{:S(2)}) collective-permute-start(f32[640,128]{1,0:T(8,128)S(1)} %get-tuple-element.34), channel_id=1, source_target_pairs={{0,1},{8,9},{16,17},{24,25},{32,33},{40,41},{48,49},{56,57},{64,65... | collective-permute-start | bytes 983048 | tf_op jit(solution)/shard_map/ppermute | solution.py:326
  3.9 50.1 %copy-start.4 = (s32[3]{0:T(128)}, s32[3]{0:T(128)S(1)}, u32[]{:S(2)}) copy-start(s32[3]{0:T(128)S(1)} %pad_add_fusion.refs_0_) | copy-start | bytes 40
  11.7 24.5 %all-to-all-start = ((f32[16,160,128]{2,1,0:T(8,128)}), f32[16,160,128]{2,1,0:T(8,128)S(1)}, u32[]{:S(2)}, u32[]{:S(2)}) async-start(f32[16,160,128]{2,1,0:T(8,128)} %second.1), calls=%async_computation | async-start | bytes 2621440 | tf_op jit(solution)/shard_map/all_to_all | solution.py:334
  19.3 5.3 %collective-permute-start.3 = (f32[640,128]{1,0:T(8,128)S(1)}, f32[640,128]{1,0:T(8,128)S(1)}, u32[]{:S(2)}, u32[]{:S(2)}) collective-permute-start(f32[640,128]{1,0:T(8,128)S(1)} %select_select_fusion), channel_id=1, source_target_pairs={{0,7},{1,3},{2,4},{6,5},{8,15},{9,11},{10,12},{14,13},{16,23},{17,... | collective-permute-start | bytes 983048 | tf_op jit(solution)/shard_map/ppermute | solution.py:335
  24.7 4.7 %collective-permute-start.4 = (f32[640,128]{1,0:T(8,128)S(1)}, f32[640,128]{1,0:T(8,128)S(1)}, u32[]{:S(2)}, u32[]{:S(2)}) collective-permute-start(f32[640,128]{1,0:T(8,128)S(1)} %broadcast_select_fusion.refs_1_.refs_2_.refs_3_), channel_id=1, source_target_pairs={{0,1},{1,0},{2,3},{3,2},{4,5},{5,4},{6,7},{7,6},{8,9},{9,8},{10,11... | collective-permute-start | bytes 983048 | tf_op jit(solution)/shard_map/ppermute | solution.py:337
  36.2 12.0 %all-to-all-start.1 = ((f32[16,16,128]{2,1,0:T(8,128)}), f32[16,16,128]{2,1,0:T(8,128)S(1)}, u32[]{:S(2)}, u32[]{:S(2)}) async-start(f32[16,16,128]{2,1,0:T(8,128)} %gram.1), calls=%async_computation.1 | async-start | bytes 262144 | tf_op jit(solution)/shard_map/all_to_all | solution.py:350
  41.5 12.5 %collective-permute-start.5 = (f32[160,128]{1,0:T(8,128)S(1)}, f32[160,128]{1,0:T(8,128)S(1)}, u32[]{:S(2)}, u32[]{:S(2)}) collective-permute-start(f32[160,128]{1,0:T(8,128)S(1)} %dynamic-slice_select_fusion), channel_id=1, source_target_pairs={{0,0},{1,8},{2,16},{3,24},{4,32},{5,40},{6,48},{7,56},{8,64},{9,72... | collective-permute-start | bytes 245768 | tf_op jit(solution)/shard_map/ppermute | solution.py:346
  49.7 12.6 %all-to-all-start.3 = ((f32[16,16,128]{2,1,0:T(8,128)}), f32[16,16,128]{2,1,0:T(8,128)S(1)}, u32[]{:S(2)}, u32[]{:S(2)}) async-start(f32[16,16,128]{2,1,0:T(8,128)} %mix.1), calls=%async_computation.3 | async-start | bytes 262144 | tf_op jit(solution)/shard_map/all_to_all | solution.py:361
  62.3 36.8 %all-to-all-start.2 = ((f32[16,320,128]{2,1,0:T(8,128)}), f32[16,320,128]{2,1,0:T(8,128)S(1)}, u32[]{:S(2)}, u32[]{:S(2)}) async-start(f32[16,320,128]{2,1,0:T(8,128)} %first_pass.1), calls=%async_computation.2 | async-start | bytes 5242880 | tf_op jit(solution)/shard_map/all_to_all | solution.py:371
  68.9 0.6 copy-start.5
  91.8 0.6 copy-start.3
  99.1 0.6 copy-start.6
  102.8 1.1 copy-start.1
  103.8 17.3 %copy-start.7 = (s32[3]{0:T(128)S(1)}, s32[3]{0:T(128)}, u32[]{:S(2)}) copy-start(s32[3]{0:T(128)} %copy-done.4) | copy-start | bytes 40
  103.8 24.8 %all-to-all-start.4 = ((f32[16,160,128]{2,1,0:T(8,128)}), f32[16,160,128]{2,1,0:T(8,128)}, u32[]{:S(2)}, u32[]{:S(2)}) async-start(f32[16,160,128]{2,1,0:T(8,128)} %copy-done.1), calls=%async_computation.4 | async-start | bytes 2621440 | tf_op jit(solution)/shard_map/all_to_all | solution.py:387
  111.9 16.8 %collective-permute-start.6 = (f32[160,128]{1,0:T(8,128)S(1)}, f32[160,128]{1,0:T(8,128)}, u32[]{:S(2)}, u32[]{:S(2)}) collective-permute-start(f32[160,128]{1,0:T(8,128)S(1)} %get-tuple-element.30), channel_id=1, source_target_pairs={{0,0},{8,1},{16,2},{24,3},{32,4},{40,5},{48,6},{56,7},{64,8},{72,9... | collective-permute-start | bytes 245768 | tf_op jit(solution)/shard_map/ppermute | solution.py:386
  123.7 1.1 copy-start
  124.8 0.8 copy-start.2
  132.6 28.6 %all-to-all-start.5 = ((f32[8,288,128]{2,1,0:T(8,128)}), f32[8,288,128]{2,1,0:T(8,128)S(1)}, u32[]{:S(2)}, u32[]{:S(2)}) async-start(f32[8,288,128]{2,1,0:T(8,128)} %inner.1), calls=%async_computation.5 | async-start | bytes 2359296 | tf_op jit(solution)/shard_map/all_to_all | solution.py:412
  161.3 1.0 copy-start.8

commit v6 on v5

--- a/solution.py
+++ b/solution.py
@@ -384,6 +384,7 @@
         3 + NR + 1,
     )
     y_p = lax.ppermute(y_q, axes, [(b, a) for a, b in enumerate(owner)])
+    msg, y_p = lax.optimization_barrier((msg, y_p))
     msg = lax.all_to_all(msg, "prow", 0, 0, tiled=True)
     vt, left = call(
         vectors_kernel,

time: 176 us -> 185 us (1.051)
  waiting for transfers between devices: 36.4 us -> 46.6 us
    all_to_all x2, waiting for transfers between devices: 6.64 us -> 18.4 us  [on_device(): msg = lax.all_to_all(msg, 'prow', 0, 0, tiled=True)]
    all_to_all x1, starting transfers between devices: 12.1 us -> 9.12 us  [on_device(): end = lax.all_to_all(end, 'pcol', 0, 0, tiled=True)]
    unnamed x18 -> x20, local copies, waits for them, and re-layouts: 5.9 us -> 6.48 us
  transfers between devices with their start and end apart: 13 -> 13, of which waited for: 8 -> 9; matrix products, arithmetic and copies ran while one was open for 0% -> 0% of each run, Pallas kernels for 25% -> 24%
where the time goes in v6:
time: 185 us; the launch traced here: 184 us
  starting transfers between devices  65.3 us (35%)
  Pallas kernels  62.9 us (34%)
  waiting for transfers between devices  46.6 us (25%)
  local copies, waits for them, and re-layouts  7.61 us (4%)
    pallas_call x11, Pallas kernels, call(): pl.pallas_call(body, in_specs=[SM] + [pl.BlockSpec(memory_space=pl.ANY)]...  62.9 us
    all_to_all x2, waiting for transfers between devices, on_device(): msg = lax.all_to_all(msg, 'prow', 0, 0, tiled=True)  18.4 us
    all_to_all x2, starting transfers between devices, on_device(): msg = lax.all_to_all(msg, 'prow', 0, 0, tiled=True)  14.8 us
    all_to_all x1, waiting for transfers between devices, on_device(): end = lax.all_to_all(end, 'pcol', 0, 0, tiled=True)  12.8 us
    ppermute x1, starting transfers between devices, on_device(): y_p = lax.ppermute(y_q, axes, [(b, a) for a, b in enumerate(owner)])  10.7 us
    all_to_all x2, starting transfers between devices, on_device(): small = lax.all_to_all(small, 'prow', 0, 0, tiled=True)  9.54 us
    all_to_all x1, starting transfers between devices, on_device(): end = lax.all_to_all(end, 'pcol', 0, 0, tiled=True)  9.12 us
    all_to_all x1, starting transfers between devices, on_device(): f_msg = lax.all_to_all(f_msg, 'prow', 0, 0, tiled=True)  7.61 us
  transfers between devices with their start and end apart: 13, of which 9 were waited for; matrix products, arithmetic and copies ran while one was open for 0% of the time, Pallas kernels for 24%

profile of v6, /device:TPU:1, one launch (start us, length us, event | category | flops | bytes accessed | tf_op | source)
XLA Modules:
  0.0 184.0 jit_solution(6637797025920031621)
XLA Ops:
  0.0 1.1 fusion
  2.5 1.3 collective-permute-start
  3.9 3.4 %second.1 = f32[16,160,128]{2,1,0:T(8,128)} custom-call(s32[3]{0:T(128)S(1)} %pad_add_fusion.refs_0_, f32[1280,2560]{1,0:T(8,128)} %refs_1_.5), custom_call_target="tpu_custom_call" | custom-call | flops 128 | bytes 14417920 | tf_op jit(solution)/shard_map/second/pallas_call | solution.py:81
  7.4 3.3 %collective-permute-done = f32[640,128]{1,0:T(8,128)S(1)} collective-permute-done((f32[640,128]{1,0:T(8,128)S(1)}, f32[640,128]{1,0:T(8,128)S(1)}, u32[]{:S(2)}, u32[]{:S(2)}) %collective-permute-start) | collective-permute-done | bytes 327712 | tf_op jit(solution)/shard_map/ppermute | solution.py:326
  11.7 7.6 %all-to-all-start = ((f32[16,160,128]{2,1,0:T(8,128)}), f32[16,160,128]{2,1,0:T(8,128)S(1)}, u32[]{:S(2)}, u32[]{:S(2)}) async-start(f32[16,160,128]{2,1,0:T(8,128)} %second.1), calls=%async_computation | async-start | bytes 2621440 | tf_op jit(solution)/shard_map/all_to_all | solution.py:334
  19.3 1.3 collective-permute-start.3
  20.7 4.0 %collective-permute-done.3 = f32[640,128]{1,0:T(8,128)S(1)} collective-permute-done((f32[640,128]{1,0:T(8,128)S(1)}, f32[640,128]{1,0:T(8,128)S(1)}, u32[]{:S(2)}, u32[]{:S(2)}) %collective-permute-start.3) | collective-permute-done | bytes 327712 | tf_op jit(solution)/shard_map/ppermute | solution.py:335
  24.7 3.4 %collective-permute-start.4 = (f32[640,128]{1,0:T(8,128)S(1)}, f32[640,128]{1,0:T(8,128)S(1)}, u32[]{:S(2)}, u32[]{:S(2)}) collective-permute-start(f32[640,128]{1,0:T(8,128)S(1)} %broadcast_select_fusion.refs_1_.refs_2_.refs_3_), channel_id=1, source_target_pairs={{0,1},{1,0},{2,3},{3,2},{4,5},{5,4},{6,7},{7,6},{8,9},{9,8},{10,11... | collective-permute-start | bytes 983048 | tf_op jit(solution)/shard_map/ppermute | solution.py:337
  28.1 1.3 collective-permute-done.4.refs_2_.refs_3_.refs_4_
  29.4 1.9 %gram.1 = f32[16,16,128]{2,1,0:T(8,128)} custom-call(s32[3]{0:T(128)S(1)} %pad_add_fusion.refs_0_, f32[640,128]{1,0:T(8,128)S(1)} %broadcast_select_fusion.refs_1_.refs_2_.refs_3_, f32[640,128]{1,0:T(8,128)S(1)} %collective-permute-done.4.refs_2_.refs_3_.refs_4_), custom_call_target="tpu_custom_call" | custom-call | flops 125829120 | bytes 786432 | tf_op jit(solution)/shard_map/gram/pallas_call | solution.py:81
  31.3 4.9 %all-to-all-done = f32[16,160,128]{2,1,0:T(8,128)S(1)} async-done(((f32[16,160,128]{2,1,0:T(8,128)}), f32[16,160,128]{2,1,0:T(8,128)S(1)}, u32[]{:S(2)}, u32[]{:S(2)}) %all-to-all-start) | async-done | bytes 1310752 | tf_op jit(solution)/shard_map/all_to_all | solution.py:334
  36.2 5.3 %all-to-all-start.1 = ((f32[16,16,128]{2,1,0:T(8,128)}), f32[16,16,128]{2,1,0:T(8,128)S(1)}, u32[]{:S(2)}, u32[]{:S(2)}) async-start(f32[16,16,128]{2,1,0:T(8,128)} %gram.1), calls=%async_computation.1 | async-start | bytes 262144 | tf_op jit(solution)/shard_map/all_to_all | solution.py:350
  41.5 6.1 %collective-permute-start.5 = (f32[160,128]{1,0:T(8,128)S(1)}, f32[160,128]{1,0:T(8,128)S(1)}, u32[]{:S(2)}, u32[]{:S(2)}) collective-permute-start(f32[160,128]{1,0:T(8,128)S(1)} %dynamic-slice_select_fusion), channel_id=1, source_target_pairs={{0,0},{1,8},{2,16},{3,24},{4,32},{5,40},{6,48},{7,56},{8,64},{9,72... | collective-permute-start | bytes 245768 | tf_op jit(solution)/shard_map/ppermute | solution.py:346
  48.1 1.5 mix.1
  49.7 4.3 %all-to-all-start.3 = ((f32[16,16,128]{2,1,0:T(8,128)}), f32[16,16,128]{2,1,0:T(8,128)S(1)}, u32[]{:S(2)}, u32[]{:S(2)}) async-start(f32[16,16,128]{2,1,0:T(8,128)} %mix.1), calls=%async_computation.3 | async-start | bytes 262144 | tf_op jit(solution)/shard_map/all_to_all | solution.py:361
  54.0 8.2 %first_pass.1 = f32[16,320,128]{2,1,0:T(8,128)} custom-call(s32[3]{0:T(128)S(1)} %pad_add_fusion.refs_0_, f32[1280,2560]{1,0:T(8,128)} %refs_1_.5, f32[640,128]{1,0:T(8,128)S(1)} %broadcast_select_fusion.refs_1_.refs_2_.refs_3_, f32[640,128]{1,0:T(8,128)S(1)} %collective-permute-done.4.refs_2_.refs_3_.refs_4_, f32[160,128]{1,0:T(8,128)S(1)} %collective-permute-done.5.refs_4_), custom_call_target="tpu_custom_call" | custom-call | flops 2516582400 | bytes 16465920 | tf_op jit(solution)/shard_map/first_pass/pallas_call | solution.py:81
  62.3 6.7 %all-to-all-start.2 = ((f32[16,320,128]{2,1,0:T(8,128)}), f32[16,320,128]{2,1,0:T(8,128)S(1)}, u32[]{:S(2)}, u32[]{:S(2)}) async-start(f32[16,320,128]{2,1,0:T(8,128)} %first_pass.1), calls=%async_computation.2 | async-start | bytes 5242880 | tf_op jit(solution)/shard_map/all_to_all | solution.py:371
  69.6 10.5 %factor.1.refs_2_ = f32[128,128]{1,0:T(8,128)S(1)} custom-call(s32[3]{0:T(128)S(1)} %copy-done.5, f32[16,16,128]{2,1,0:T(8,128)S(1)} %all-to-all-done.3.refs_1_), custom_call_target="tpu_custom_call" | custom-call | flops 8000000000 | bytes 196608 | tf_op jit(solution)/shard_map/factor/pallas_call | solution.py:81
  80.1 11.7 %coupling.1.refs_2_.refs_3_ = f32[128,128]{1,0:T(8,128)S(1)} custom-call(s32[3]{0:T(128)S(1)} %copy-done.5, f32[16,16,128]{2,1,0:T(8,128)S(1)} %all-to-all-done.3.refs_1_, f32[128,128]{1,0:T(8,128)S(1)} %factor.1.refs_2_), custom_call_target="tpu_custom_call" | custom-call | flops 8000000000 | bytes 262144 | tf_op jit(solution)/shard_map/coupling/pallas_call | solution.py:81
  92.4 6.7 %all-to-all-done.2.refs_1_ = f32[16,320,128]{2,1,0:T(8,128)S(1)} async-done(((f32[16,320,128]{2,1,0:T(8,128)}), f32[16,320,128]{2,1,0:T(8,128)S(1)}, u32[]{:S(2)}, u32[]{:S(2)}) %all-to-all-start.2) | async-done | bytes 2621472 | tf_op jit(solution)/shard_map/all_to_all | solution.py:371
  99.7 3.0 %piece_image.1 = (f32[16,160,128]{2,1,0:T(8,128)S(1)}, f32[160,128]{1,0:T(8,128)S(1)}) custom-call(s32[3]{0:T(128)S(1)} %copy-done.6, f32[16,320,128]{2,1,0:T(8,128)S(1)} %all-to-all-done.2.refs_1_, f32[128,128]{1,0:T(8,128)S(1)} %factor.1.refs_2_, f32[160,128]{1,0:T(8,128)S(1)} %slice_bitcast_fusion.refs_3_), custom_call_target="tpu_custom_call" | custom-call | flops 655360 | bytes 4161536 | tf_op jit(solution)/shard_map/piece_image/pallas_call | solution.py:81
  103.8 10.7 %collective-permute-start.6 = (f32[160,128]{1,0:T(8,128)S(1)}, f32[160,128]{1,0:T(8,128)S(1)}, u32[]{:S(2)}, u32[]{:S(2)}) collective-permute-start(f32[160,128]{1,0:T(8,128)S(1)} %get-tuple-element.32), channel_id=1, source_target_pairs={{0,0},{8,1},{16,2},{24,3},{32,4},{40,5},{48,6},{56,7},{64,8},{72,9... | collective-permute-start | bytes 245768 | tf_op jit(solution)/shard_map/ppermute | solution.py:386
  114.6 1.5 collective-permute-done.6.refs_3_
  116.6 8.1 %all-to-all-start.4 = ((f32[16,160,128]{2,1,0:T(8,128)}), f32[16,160,128]{2,1,0:T(8,128)}, u32[]{:S(2)}, u32[]{:S(2)}) async-start(f32[16,160,128]{2,1,0:T(8,128)} %copy-done.1), calls=%async_computation.4 | async-start | bytes 2621440 | tf_op jit(solution)/shard_map/all_to_all | solution.py:388
  124.8 2.5 %vectors.1 = (bf16[2,128,2560]{2,1,0:T(8,128)(2,1)S(1)}, bf16[2,1280,128]{2,1,0:T(8,128)(2,1)S(1)}) custom-call(s32[3]{0:T(128)S(1)} %copy-done.7, f32[16,320,128]{2,1,0:T(8,128)S(1)} %all-to-all-done.2.refs_1_, f32[128,128]{1,0:T(8,128)S(1)} %factor.1.refs_2_, f32[640,128]{1,0:T(8,128)S(1)} %broadcast_select_fusion.refs_1_.refs_2_.refs_3_, ...), custom_call_target="tpu_custom_call" | custom-call | flops 377487360 | bytes 7274496 | tf_op jit(solution)/shard_map/vectors/pallas_call | solution.py:81
  127.3 1.1 copy-done
  129.2 11.7 %all-to-all-done.4.refs_2_.refs_1_ = f32[16,160,128]{2,1,0:T(8,128)} async-done(((f32[16,160,128]{2,1,0:T(8,128)}), f32[16,160,128]{2,1,0:T(8,128)}, u32[]{:S(2)}, u32[]{:S(2)}) %all-to-all-start.4) | async-done | bytes 1310752 | tf_op jit(solution)/shard_map/all_to_all | solution.py:388
  140.9 4.0 %inner.1 = f32[8,288,128]{2,1,0:T(8,128)} custom-call(s32[3]{0:T(128)} %copy-done.4, bf16[2,128,2560]{2,1,0:T(8,128)(2,1)} %copy-done, f32[16,160,128]{2,1,0:T(8,128)} %all-to-all-done.4.refs_2_.refs_1_, f32[160,128]{1,0:T(8,128)} %copy-done.9), custom_call_target="tpu_custom_call" | custom-call | flops 251658240 | bytes 5193728 | tf_op jit(solution)/shard_map/inner/pallas_call | solution.py:81
  144.9 9.1 %all-to-all-start.5 = ((f32[8,288,128]{2,1,0:T(8,128)}), f32[8,288,128]{2,1,0:T(8,128)S(1)}, u32[]{:S(2)}, u32[]{:S(2)}) async-start(f32[8,288,128]{2,1,0:T(8,128)} %inner.1), calls=%async_computation.5 | async-start | bytes 2359296 | tf_op jit(solution)/shard_map/all_to_all | solution.py:413
  154.0 3.7 %sides.1.refs_5_ = f32[128,2560]{1,0:T(8,128)} custom-call(s32[3]{0:T(128)} %copy-done.4, f32[16,160,128]{2,1,0:T(8,128)} %all-to-all-done.4.refs_2_.refs_1_, f32[128,128]{1,0:T(8,128)} %copy-done.3), custom_call_target="tpu_custom_call" | custom-call | flops 251658240 | bytes 2686976 | tf_op jit(solution)/shard_map/sides/pallas_call | solution.py:81
  157.8 12.8 %all-to-all-done.5.refs_2_ = f32[8,288,128]{2,1,0:T(8,128)S(1)} async-done(((f32[8,288,128]{2,1,0:T(8,128)}), f32[8,288,128]{2,1,0:T(8,128)S(1)}, u32[]{:S(2)}, u32[]{:S(2)}) %all-to-all-start.5) | async-done | bytes 1179680 | tf_op jit(solution)/shard_map/all_to_all | solution.py:413
  171.6 12.2 %last_pass.1 = f32[1280,2560]{1,0:T(8,128)} custom-call(s32[3]{0:T(128)} %copy-done.4, f32[1280,2560]{1,0:T(8,128)} %refs_1_.5, f32[8,288,128]{2,1,0:T(8,128)} %copy-done.8, f32[128,128]{1,0:T(8,128)} %copy-done.3, bf16[2,1280,128]{2,1,0:T(8,128)(2,1)} %copy-done.2, f32[128,2560]{1,0:T(8,128)} %sides.1.refs_5_, bf16[2,128,2560]{2,1,0:T(8,128)(2,1)} %copy-done), custom_call_target="tpu_custom_call" | custom-call | flops 5033164800 | bytes 32702464 | tf_op jit(solution)/shard_map/last_pass/pallas_call | solution.py:81
  (31 shorter events, 8.5 us)
Async XLA Ops:
  1.1 6.2 %collective-permute-start.1 = (f32[640,128]{1,0:T(8,128)S(1)}, f32[640,128]{1,0:T(8,128)S(1)}, u32[]{:S(2)}, u32[]{:S(2)}) collective-permute-start(f32[640,128]{1,0:T(8,128)S(1)} %get-tuple-element.37), channel_id=1, source_target_pairs={{0,2},{8,10},{16,18},{24,26},{32,34},{40,42},{48,50},{56,58},{64,6... | collective-permute-start | bytes 983048 | tf_op jit(solution)/shard_map/ppermute | solution.py:327
  1.8 5.6 %collective-permute-start.2 = (f32[640,128]{1,0:T(8,128)S(1)}, f32[640,128]{1,0:T(8,128)S(1)}, u32[]{:S(2)}, u32[]{:S(2)}) collective-permute-start(f32[640,128]{1,0:T(8,128)S(1)} %get-tuple-element.38), channel_id=1, source_target_pairs={{0,6},{8,14},{16,22},{24,30},{32,38},{40,46},{48,54},{56,62},{64,7... | collective-permute-start | bytes 983048 | tf_op jit(solution)/shard_map/ppermute | solution.py:328
  2.5 8.2 %collective-permute-start = (f32[640,128]{1,0:T(8,128)S(1)}, f32[640,128]{1,0:T(8,128)S(1)}, u32[]{:S(2)}, u32[]{:S(2)}) collective-permute-start(f32[640,128]{1,0:T(8,128)S(1)} %get-tuple-element.38), channel_id=1, source_target_pairs={{0,1},{8,9},{16,17},{24,25},{32,33},{40,41},{48,49},{56,57},{64,65... | collective-permute-start | bytes 983048 | tf_op jit(solution)/shard_map/ppermute | solution.py:326
  3.9 50.1 %copy-start.4 = (s32[3]{0:T(128)}, s32[3]{0:T(128)S(1)}, u32[]{:S(2)}) copy-start(s32[3]{0:T(128)S(1)} %pad_add_fusion.refs_0_) | copy-start | bytes 40
  11.7 24.5 %all-to-all-start = ((f32[16,160,128]{2,1,0:T(8,128)}), f32[16,160,128]{2,1,0:T(8,128)S(1)}, u32[]{:S(2)}, u32[]{:S(2)}) async-start(f32[16,160,128]{2,1,0:T(8,128)} %second.1), calls=%async_computation | async-start | bytes 2621440 | tf_op jit(solution)/shard_map/all_to_all | solution.py:334
  19.3 5.3 %collective-permute-start.3 = (f32[640,128]{1,0:T(8,128)S(1)}, f32[640,128]{1,0:T(8,128)S(1)}, u32[]{:S(2)}, u32[]{:S(2)}) collective-permute-start(f32[640,128]{1,0:T(8,128)S(1)} %select_select_fusion), channel_id=1, source_target_pairs={{0,7},{1,3},{2,4},{6,5},{8,15},{9,11},{10,12},{14,13},{16,23},{17,... | collective-permute-start | bytes 983048 | tf_op jit(solution)/shard_map/ppermute | solution.py:335
  24.7 4.7 %collective-permute-start.4 = (f32[640,128]{1,0:T(8,128)S(1)}, f32[640,128]{1,0:T(8,128)S(1)}, u32[]{:S(2)}, u32[]{:S(2)}) collective-permute-start(f32[640,128]{1,0:T(8,128)S(1)} %broadcast_select_fusion.refs_1_.refs_2_.refs_3_), channel_id=1, source_target_pairs={{0,1},{1,0},{2,3},{3,2},{4,5},{5,4},{6,7},{7,6},{8,9},{9,8},{10,11... | collective-permute-start | bytes 983048 | tf_op jit(solution)/shard_map/ppermute | solution.py:337
  36.2 12.0 %all-to-all-start.1 = ((f32[16,16,128]{2,1,0:T(8,128)}), f32[16,16,128]{2,1,0:T(8,128)S(1)}, u32[]{:S(2)}, u32[]{:S(2)}) async-start(f32[16,16,128]{2,1,0:T(8,128)} %gram.1), calls=%async_computation.1 | async-start | bytes 262144 | tf_op jit(solution)/shard_map/all_to_all | solution.py:350
  41.5 12.5 %collective-permute-start.5 = (f32[160,128]{1,0:T(8,128)S(1)}, f32[160,128]{1,0:T(8,128)S(1)}, u32[]{:S(2)}, u32[]{:S(2)}) collective-permute-start(f32[160,128]{1,0:T(8,128)S(1)} %dynamic-slice_select_fusion), channel_id=1, source_target_pairs={{0,0},{1,8},{2,16},{3,24},{4,32},{5,40},{6,48},{7,56},{8,64},{9,72... | collective-permute-start | bytes 245768 | tf_op jit(solution)/shard_map/ppermute | solution.py:346
  49.7 12.6 %all-to-all-start.3 = ((f32[16,16,128]{2,1,0:T(8,128)}), f32[16,16,128]{2,1,0:T(8,128)S(1)}, u32[]{:S(2)}, u32[]{:S(2)}) async-start(f32[16,16,128]{2,1,0:T(8,128)} %mix.1), calls=%async_computation.3 | async-start | bytes 262144 | tf_op jit(solution)/shard_map/all_to_all | solution.py:361
  62.3 36.8 %all-to-all-start.2 = ((f32[16,320,128]{2,1,0:T(8,128)}), f32[16,320,128]{2,1,0:T(8,128)S(1)}, u32[]{:S(2)}, u32[]{:S(2)}) async-start(f32[16,320,128]{2,1,0:T(8,128)} %first_pass.1), calls=%async_computation.2 | async-start | bytes 5242880 | tf_op jit(solution)/shard_map/all_to_all | solution.py:371
  68.9 0.6 copy-start.5
  91.8 0.6 copy-start.3
  99.1 0.6 copy-start.6
  102.8 1.1 copy-start.1
  103.8 12.2 %collective-permute-start.6 = (f32[160,128]{1,0:T(8,128)S(1)}, f32[160,128]{1,0:T(8,128)S(1)}, u32[]{:S(2)}, u32[]{:S(2)}) collective-permute-start(f32[160,128]{1,0:T(8,128)S(1)} %get-tuple-element.32), channel_id=1, source_target_pairs={{0,0},{8,1},{16,2},{24,3},{32,4},{40,5},{48,6},{56,7},{64,8},{72,9... | collective-permute-start | bytes 245768 | tf_op jit(solution)/shard_map/ppermute | solution.py:386
  116.0 0.6 copy-start.9
  116.0 8.7 %copy-start.7 = (s32[3]{0:T(128)S(1)}, s32[3]{0:T(128)}, u32[]{:S(2)}) copy-start(s32[3]{0:T(128)} %copy-done.4) | copy-start | bytes 40
  116.6 24.3 %all-to-all-start.4 = ((f32[16,160,128]{2,1,0:T(8,128)}), f32[16,160,128]{2,1,0:T(8,128)}, u32[]{:S(2)}, u32[]{:S(2)}) async-start(f32[16,160,128]{2,1,0:T(8,128)} %copy-done.1), calls=%async_computation.4 | async-start | bytes 2621440 | tf_op jit(solution)/shard_map/all_to_all | solution.py:388
  127.3 1.1 copy-start
  128.4 0.8 copy-start.2
  144.9 25.6 %all-to-all-start.5 = ((f32[8,288,128]{2,1,0:T(8,128)}), f32[8,288,128]{2,1,0:T(8,128)S(1)}, u32[]{:S(2)}, u32[]{:S(2)}) async-start(f32[8,288,128]{2,1,0:T(8,128)} %inner.1), calls=%async_computation.5 | async-start | bytes 2359296 | tf_op jit(solution)/shard_map/all_to_all | solution.py:413
  170.6 1.0 copy-start.8
